TPU v7x, 32 devices: a whole 2x2x4 slice. The times are simulated.
32 devices in a mesh: groups: 2 (over y), dp: 4 (over z), sub: 2 (over x), pair: 2 (over core).
Axes of the slice: x: 2, y: 2, z: 4, core: 2. Of those that a mesh axis runs over, the one named last changes fastest.
Arguments:
- query_inputs: bfloat16 [2048, 4096], P(('groups', 'dp', 'sub', 'pair')), parts along dimension 0, may hold values from -0.31835938 to 0.31835938
- query_gradient: bfloat16 [2048, 4096], P(('groups', 'dp', 'sub', 'pair')), parts along dimension 0, may hold values from -0.31835938 to 0.31835938
- query_sequence_index: int32 [2048], P(('groups', 'dp', 'sub', 'pair')), parts along dimension 0, may hold values from 0 to 15, never falling along the last dimension, each value on 1 to 128 neighbouring positions
- training_inputs: bfloat16 [32, 128, 4096], P(('groups', 'dp', 'pair')), parts along dimension 0, may hold values from -0.31835938 to 0.31835938
- training_gradient: bfloat16 [32, 128, 4096], P(('groups', 'dp', 'pair')), parts along dimension 0, may hold values from -0.31835938 to 0.31835938
- training_length: int32 [32], P(('groups', 'dp', 'pair')), parts along dimension 0, may hold values from 1 to 128, 1536 in all
- adapter_down_map: bfloat16 [4096, 16], replicated, may hold values from -0.796875 to 0.796875
- adapter_up_map: bfloat16 [4096, 16], replicated, may hold values from -0.796875 to 0.796875
Outputs:
- scores: float32 [32, 16], P(('groups', 'sub'), ('dp', 'pair')), parts along dimension 0
There are 2 independent parts, one for each index of `groups`. A program takes and returns all parts, laid end to end along the dimension named above; an argument that names none is the same for every part. Nothing has to cross between parts.
Inputs may be any that keep to these rules, and one draw needn't show every extreme that they name: `query_sequence_index`: ids do not fall along the tokens; every id from 0 to 15 is held by 1 to 128 tokens, one id by exactly 128. `training_length`: they sum to 1536; at least one sequence fills all 128 slots.
All inputs are finite; a program needn't handle non-finite values. No bound on the sum of `training_length` on one device may be relied on, other than what follows from the above.
Results may differ from a plain program's by a relative error of at most 0.004.
Values may be sent and summed in bfloat16 or wider, within the bound.
No kernel may reach another device: no remote copies, remote signals or barrier semaphores. Data moves between devices by JAX's collectives and lax.ppermute only.
A program may use at most 64 MiB of HBM per device.

v0:
```python
import jax
import jax.numpy as jnp
from jax import lax
from jax.sharding import PartitionSpec as P

QMEAN = 64


def from_behind(value, axis, steps):
    count = lax.axis_size(axis)
    pairs = [(source, (source + steps) % count) for source in range(count)]
    return lax.ppermute(value, axis, pairs)


def reduced_rank(values, weights):
    return jnp.dot(values, weights, preferred_element_type=jnp.float32).astype(jnp.bfloat16)


def token_gram(left_rows, right_rows):
    return lax.dot_general(
        left_rows, right_rows, (((1,), (1,)), ((), ())), preferred_element_type=jnp.float32
    )


def per_device(
    query_inputs,
    query_gradient,
    query_sequence_index,
    training_inputs,
    training_gradient,
    training_length,
    adapter_down_map,
    adapter_up_map,
):
    slot_count, slot_total, features = training_inputs.shape
    flattened_inputs = training_inputs.reshape(slot_count * slot_total, features)
    flattened_gradient = training_gradient.reshape(slot_count * slot_total, features)
    training_down_map = reduced_rank(flattened_inputs, adapter_down_map)
    training_up_map = reduced_rank(flattened_gradient, adapter_up_map)
    offsets = jnp.arange(slot_total, dtype=jnp.int32)
    live_mask = (offsets[None, :] < training_length[:, None]).astype(jnp.float32)
    query_block = lax.all_gather(
        jnp.stack([query_inputs, query_gradient]), "pair", axis=1, tiled=True
    )
    column_ids = lax.all_gather(query_sequence_index, ("dp", "pair"), axis=0, tiled=True)
    query_count = (
        query_inputs.shape[0]
        * lax.axis_size("dp")
        * lax.axis_size("sub")
        * lax.axis_size("pair")
        // QMEAN
    )
    sequence_index = jnp.arange(query_count, dtype=jnp.int32)
    block_rows = query_block.shape[1]

    def contribute(scores, shard_piece, first_row):
        piece_rows = shard_piece.shape[1]
        portion_inputs = shard_piece[0]
        portion_gradient = shard_piece[1]
        portion_down_map = reduced_rank(portion_inputs, adapter_down_map)
        portion_up_map = reduced_rank(portion_gradient, adapter_up_map)
        gram_acts = token_gram(portion_inputs, flattened_inputs)
        gram_grads = token_gram(portion_gradient, flattened_gradient)
        gram_down = token_gram(portion_down_map, training_down_map)
        gram_up = token_gram(portion_up_map, training_up_map)
        pair_term = gram_grads * gram_down + gram_up * gram_acts
        per_slot = jnp.sum(
            pair_term.reshape(piece_rows, slot_count, slot_total) * live_mask[None], axis=2
        )
        slice_ids = lax.dynamic_slice_in_dim(column_ids, first_row, piece_rows)
        one_hot = (slice_ids[:, None] == sequence_index[None, :]).astype(jnp.float32)
        return scores + lax.dot_general(
            one_hot,
            per_slot,
            (((0,), (0,)), ((), ())),
            precision=lax.Precision.HIGHEST,
            preferred_element_type=jnp.float32,
        )

    zero_scores = jnp.zeros((query_count, slot_count), jnp.float32)
    cycle_size = lax.axis_size("dp")
    position = lax.axis_index("dp")
    final_turn = cycle_size - 1

    def turn_single(step_index, loop_state):
        scores, travelling = loop_state
        scores = contribute(scores, travelling, (position - step_index) % cycle_size * block_rows)
        travelling = from_behind(travelling, "dp", 1)
        return (scores, travelling)

    scores, travelling = lax.fori_loop(0, final_turn, turn_single, (zero_scores, query_block))
    scores = contribute(scores, travelling, (position - final_turn) % cycle_size * block_rows)
    return lax.psum_scatter(scores, "sub", scatter_dimension=0, tiled=True)


def solution(mesh):
    placed = (
        P(("groups", "dp", "sub", "pair"), None),
        P(("groups", "dp", "sub", "pair"), None),
        P(("groups", "dp", "sub", "pair")),
        P(("groups", "dp", "pair"), None, None),
        P(("groups", "dp", "pair"), None, None),
        P(("groups", "dp", "pair")),
        P(),
        P(),
    )
    return jax.shard_map(
        per_device,
        mesh=mesh,
        in_specs=placed,
        out_specs=P(("groups", "sub"), ("dp", "pair")),
        check_vma=False,
    )
```

profile of v0, /device:TPU:0, one launch (start us, length us, event | category | flops | bytes accessed | tf_op | source)
XLA Modules:
  0.0 194.2 jit_solution(17226882783203474823)
XLA Ops:
  6.6 2.3 %pad_maximum_fusion = bf16[2,64,4096]{2,1,0:T(8,128)(2,1)} fusion(bf16[1,64,4096]{2,1,0:T(8,128)(2,1)} %bitcast.72, bf16[1,64,4096]{2,1,0:T(8,128)(2,1)} %bitcast.73), kind=kLoop, calls=%fused_computation.32 | loop fusion | flops 524288 | bytes 2097152 | tf_op jit(solution)/shard_map/stack | solution.py:43
  9.0 0.6 dynamic-slice
  10.5 10.6 %all-reduce = s32[512]{0:T(512)S(1)} all-reduce(s32[512]{0:T(512)S(1)} %dynamic-update-slice), channel_id=1, replica_groups=mesh['groups'=2,'dp'=4,'sub'=2,'pair'=2] {'dp','pair'}, use_global_device_ids=true, to_apply=%add | all-reduce | flops 512 | bytes 4096
  21.2 0.6 dynamic-slice.1
  22.5 2.2 %fusion.38 = bf16[256,16]{0,1:T(8,128)(2,1)S(1)} fusion(bf16[256,4096]{1,0:T(8,128)(2,1)} %bitcast.4, bf16[4096,16]{0,1:T(8,128)(2,1)S(1)} %copy-done), kind=kOutput, calls=%fused_computation.46 | convolution fusion | flops 33554432 | bytes 2236416 | tf_op jit(solution)/shard_map/dot_general | solution.py:16
  24.7 2.3 %fusion.39 = bf16[256,16]{0,1:T(8,128)(2,1)S(1)} fusion(bf16[256,4096]{1,0:T(8,128)(2,1)} %bitcast.3, bf16[4096,16]{0,1:T(8,128)(2,1)S(1)} %copy-done.1), kind=kOutput, calls=%fused_computation.47 | convolution fusion | flops 33554432 | bytes 2236416 | tf_op jit(solution)/shard_map/dot_general | solution.py:16
  27.0 145.2 %while.18 = (s32[]{:T(128)}, f32[16,2]{0,1:T(2,128)S(1)}, bf16[2,128,4096]{2,1,0:T(8,128)(2,1)}, s32[]{:T(128)}, s32[512]{0:T(512)S(1)}, /*index=5*/bf16[256,409...) while((s32[]{:T(128)}, f32[16,2]{0,1:T(2,128)S(1)}, ...), condition=%wide.region_2.3_spmd.clone, body=%wide.region_0.2_spmd.clone.sunk | while | flops 572741952 | bytes 22567048 | solution.py:91
  27.0 1.6 copy.17
  28.6 0.9 collective-permute-start
  29.5 0.5 fusion.83
  30.0 0.5 fusion.84
  30.6 2.4 %convolution_multiply_fusion.5 = f32[128,256]{1,0:T(8,128)S(1)} fusion(f32[128,256]{1,0:T(8,128)S(1)} %fusion.83, bf16[256,4096]{1,0:T(8,128)(2,1)} %get-tuple-element.499, bf16[2,128,4096]{2,1,0:T(8,128)(2,1)S(1)} %copy.17), kind=kOutput, calls=%fused_computation.4.clone.1 | convolution fusion | flops 268468224 | bytes 3407872 | tf_op jit(solution)/shard_map/while/body/eval_jaxpr/dot_general | solution.py:20
  33.0 2.4 %fusion.85 = f32[128,256]{1,0:T(8,128)S(1)} fusion(f32[128,256]{1,0:T(8,128)S(1)} %convolution_multiply_fusion.5, f32[128,256]{1,0:T(8,128)S(1)} %fusion.84, bf16[256,4096]{1,0:T(8,128)(2,1)} %get-tuple-element.504, bf16[2,128,4096]{2,1,0:T(8,128)(2,1)S(1)} %copy.17), kind=kOutput, calls=%fused_computation.3.clone.1 | convolution fusion | flops 268500992 | bytes 3538944 | tf_op jit(solution)/shard_map/while/body/eval_jaxpr/dot_general | solution.py:20
  36.1 40.2 %collective-permute-done = bf16[2,128,4096]{2,1,0:T(8,128)(2,1)} collective-permute-done((bf16[2,128,4096]{2,1,0:T(8,128)(2,1)S(1)}, bf16[2,128,4096]{2,1,0:T(8,128)(2,1)}, u32[]{:S(2)}, u32[]{:S(2)}) %collective-permute-start) | collective-permute-done | bytes 2097184 | tf_op jit(solution)/shard_map/while/body/eval_jaxpr/ppermute | solution.py:12
  76.3 1.6 copy.17
  77.9 0.5 fusion.83
  78.5 0.5 fusion.84
  79.0 2.4 %convolution_multiply_fusion.5 = f32[128,256]{1,0:T(8,128)S(1)} fusion(f32[128,256]{1,0:T(8,128)S(1)} %fusion.83, bf16[256,4096]{1,0:T(8,128)(2,1)} %get-tuple-element.499, bf16[2,128,4096]{2,1,0:T(8,128)(2,1)S(1)} %copy.17), kind=kOutput, calls=%fused_computation.4.clone.1 | convolution fusion | flops 268468224 | bytes 3407872 | tf_op jit(solution)/shard_map/while/body/eval_jaxpr/dot_general | solution.py:20
  81.5 2.4 %fusion.85 = f32[128,256]{1,0:T(8,128)S(1)} fusion(f32[128,256]{1,0:T(8,128)S(1)} %convolution_multiply_fusion.5, f32[128,256]{1,0:T(8,128)S(1)} %fusion.84, bf16[256,4096]{1,0:T(8,128)(2,1)} %get-tuple-element.504, bf16[2,128,4096]{2,1,0:T(8,128)(2,1)S(1)} %copy.17), kind=kOutput, calls=%fused_computation.3.clone.1 | convolution fusion | flops 268500992 | bytes 3538944 | tf_op jit(solution)/shard_map/while/body/eval_jaxpr/dot_general | solution.py:20
  84.6 40.1 %collective-permute-done = bf16[2,128,4096]{2,1,0:T(8,128)(2,1)} collective-permute-done((bf16[2,128,4096]{2,1,0:T(8,128)(2,1)S(1)}, bf16[2,128,4096]{2,1,0:T(8,128)(2,1)}, u32[]{:S(2)}, u32[]{:S(2)}) %collective-permute-start) | collective-permute-done | bytes 2097184 | tf_op jit(solution)/shard_map/while/body/eval_jaxpr/ppermute | solution.py:12
  124.7 1.6 copy.17
  126.3 0.5 fusion.83
  126.9 0.5 fusion.84
  127.4 2.4 %convolution_multiply_fusion.5 = f32[128,256]{1,0:T(8,128)S(1)} fusion(f32[128,256]{1,0:T(8,128)S(1)} %fusion.83, bf16[256,4096]{1,0:T(8,128)(2,1)} %get-tuple-element.499, bf16[2,128,4096]{2,1,0:T(8,128)(2,1)S(1)} %copy.17), kind=kOutput, calls=%fused_computation.4.clone.1 | convolution fusion | flops 268468224 | bytes 3407872 | tf_op jit(solution)/shard_map/while/body/eval_jaxpr/dot_general | solution.py:20
  129.9 2.4 %fusion.85 = f32[128,256]{1,0:T(8,128)S(1)} fusion(f32[128,256]{1,0:T(8,128)S(1)} %convolution_multiply_fusion.5, f32[128,256]{1,0:T(8,128)S(1)} %fusion.84, bf16[256,4096]{1,0:T(8,128)(2,1)} %get-tuple-element.504, bf16[2,128,4096]{2,1,0:T(8,128)(2,1)S(1)} %copy.17), kind=kOutput, calls=%fused_computation.3.clone.1 | convolution fusion | flops 268500992 | bytes 3538944 | tf_op jit(solution)/shard_map/while/body/eval_jaxpr/dot_general | solution.py:20
  133.0 39.2 %collective-permute-done = bf16[2,128,4096]{2,1,0:T(8,128)(2,1)} collective-permute-done((bf16[2,128,4096]{2,1,0:T(8,128)(2,1)S(1)}, bf16[2,128,4096]{2,1,0:T(8,128)(2,1)}, u32[]{:S(2)}, u32[]{:S(2)}) %collective-permute-start) | collective-permute-done | bytes 2097184 | tf_op jit(solution)/shard_map/while/body/eval_jaxpr/ppermute | solution.py:12
  172.2 1.8 fusion.21
  174.0 1.8 fusion.22
  175.7 2.8 %convolution_multiply_fusion.3 = f32[128,256]{1,0:T(8,128)S(1)} fusion(f32[128,256]{1,0:T(8,128)S(1)} %fusion.21, bf16[256,4096]{1,0:T(8,128)(2,1)} %bitcast.3, bf16[2,128,4096]{2,1,0:T(8,128)(2,1)} %get-tuple-element.316), kind=kOutput, calls=%fused_computation.24 | convolution fusion | flops 268468224 | bytes 3407872 | tf_op jit(solution)/shard_map/dot_general | solution.py:20
  178.5 2.8 %fusion.20 = f32[128,256]{1,0:T(8,128)S(1)} fusion(f32[128,256]{1,0:T(8,128)S(1)} %convolution_multiply_fusion.3, f32[128,256]{1,0:T(8,128)S(1)} %fusion.22, bf16[256,4096]{1,0:T(8,128)(2,1)} %bitcast.4, bf16[2,128,4096]{2,1,0:T(8,128)(2,1)} %get-tuple-element.316), kind=kOutput, calls=%fused_computation.23 | convolution fusion | flops 268500992 | bytes 3538944 | tf_op jit(solution)/shard_map/dot_general | solution.py:20
  181.8 4.9 %all-reduce.1 = f32[16,2]{0,1:T(2,128)S(1)} all-reduce(f32[16,2]{0,1:T(2,128)S(1)} %convolution_add_fusion.1), channel_id=2, replica_groups=mesh['groups'=2,'dp'=4,'sub'=2,'pair'=2] {'sub'}, use_global_device_ids=true, to_apply=%region_4.5.clone | all-reduce | flops 32 | bytes 256
  186.7 0.6 constant_dynamic-slice_fusion
  (40 shorter events, 3.0 us)
Async XLA Ops:
  6.5 2.5 %copy-start.5 = (u32[32]{0:T(128)S(1)}, u32[32]{0:T(128)}, u32[]{:S(2)}) copy-start(u32[32]{0:T(128)} %constant.102) | copy-start | bytes 388
  6.5 14.7 %copy-start.4 = (u32[32]{0:T(128)S(1)}, u32[32]{0:T(128)}, u32[]{:S(2)}) copy-start(u32[32]{0:T(128)} %constant.108) | copy-start | bytes 388
  6.5 3.7 %copy-start.2 = (s32[64]{0:T(128)S(1)}, s32[64]{0:T(128)}, u32[]{:S(2)}) copy-start(s32[64]{0:T(128)} %param.12) | copy-start | bytes 772
  6.5 15.9 %copy-start.3 = (s32[2]{0:T(128)S(1)}, s32[2]{0:T(128)}, u32[]{:S(2)}) copy-start(s32[2]{0:T(128)} %param.15) | copy-start | bytes 28
  6.5 16.0 %copy-start = (bf16[4096,16]{0,1:T(8,128)(2,1)S(1)}, bf16[4096,16]{0,1:T(8,128)(2,1)}, u32[]{:S(2)}) copy-start(bf16[4096,16]{0,1:T(8,128)(2,1)} %param.16) | copy-start | bytes 393220
  6.5 20.4 %all-gather.2.cloned.1.call-start = ((), (), s32[]{:S(2)}) async-start(), calls=%async_computation | async-start | bytes 3145728 | tf_op jit(solution)/shard_map/all_gather | solution.py:42
  8.9 15.8 %copy-start.1 = (bf16[4096,16]{0,1:T(8,128)(2,1)S(1)}, bf16[4096,16]{0,1:T(8,128)(2,1)}, u32[]{:S(2)}) copy-start(bf16[4096,16]{0,1:T(8,128)(2,1)} %param.17) | copy-start | bytes 393220
  28.6 47.7 %collective-permute-start = (bf16[2,128,4096]{2,1,0:T(8,128)(2,1)S(1)}, bf16[2,128,4096]{2,1,0:T(8,128)(2,1)}, u32[]{:S(2)}, u32[]{:S(2)}) collective-permute-start(bf16[2,128,4096]{2,1,0:T(8,128)(2,1)S(1)} %copy.17), channel_id=1, source_target_pairs={{0,4},{4,8},{8,12},{12,0},{1,5},{5,9},{9,13},{13,1},{2,6},{6,10},{... | collective-permute-start | bytes 6291464 | tf_op jit(solution)/shard_map/while/body/eval_jaxpr/ppermute | solution.py:12
  77.9 46.8 %collective-permute-start = (bf16[2,128,4096]{2,1,0:T(8,128)(2,1)S(1)}, bf16[2,128,4096]{2,1,0:T(8,128)(2,1)}, u32[]{:S(2)}, u32[]{:S(2)}) collective-permute-start(bf16[2,128,4096]{2,1,0:T(8,128)(2,1)S(1)} %copy.17), channel_id=1, source_target_pairs={{0,4},{4,8},{8,12},{12,0},{1,5},{5,9},{9,13},{13,1},{2,6},{6,10},{... | collective-permute-start | bytes 6291464 | tf_op jit(solution)/shard_map/while/body/eval_jaxpr/ppermute | solution.py:12
  126.3 45.9 %collective-permute-start = (bf16[2,128,4096]{2,1,0:T(8,128)(2,1)S(1)}, bf16[2,128,4096]{2,1,0:T(8,128)(2,1)}, u32[]{:S(2)}, u32[]{:S(2)}) collective-permute-start(bf16[2,128,4096]{2,1,0:T(8,128)(2,1)S(1)} %copy.17), channel_id=1, source_target_pairs={{0,4},{4,8},{8,12},{12,0},{1,5},{5,9},{9,13},{13,1},{2,6},{6,10},{... | collective-permute-start | bytes 6291464 | tf_op jit(solution)/shard_map/while/body/eval_jaxpr/ppermute | solution.py:12
Sparse Core Ops, SparseCore 0:
  9.1 13.2 all-gather.1
where the time goes:
time: 195 us; the launch traced here: 194 us
  waiting for transfers between devices  120 us (62%)
  matrix products  32.3 us (17%)
  blocking collectives  15.5 us (8%)
  between operations  14.8 us (8%)
  local copies, waits for them, and re-layouts  7.47 us (4%)
  other arithmetic  3.46 us (2%)
    ppermute x3, waiting for transfers between devices, from_behind(): return lax.ppermute(value, axis, pairs)  120 us
    dot_general x16, matrix products, token_gram(): lax.dot_general(left_rows, right_rows, (((1,), (1,)), ((), ())), preferre...  26.9 us
    unnamed x2, blocking collectives  15.5 us
    while x3, local copies, waits for them, and re-layouts  4.79 us
    dot_general x2, matrix products, reduced_rank(): jnp.dot(values, weights, preferred_element_type=jnp.float32)  4.48 us
  transfers between devices with their start and end apart: 4, of which 3 were waited for; matrix products, arithmetic and copies ran while one was open for 13% of the time, Pallas kernels for 0%

commit v1 on v0

v1 whole, which is shorter than its diff:
```python
import functools

import jax
import jax.numpy as jnp
from jax import lax
from jax.experimental import pallas as pl
from jax.experimental.pallas import tpu as pltpu
from jax.sharding import PartitionSpec as P

QMEAN = 64
EXTRA = 16
VMEM = pl.BlockSpec(memory_space=pltpu.VMEM)
SMEM = pl.BlockSpec(memory_space=pltpu.SMEM)
HBM = pl.BlockSpec(memory_space=pl.ANY)
LIMIT = 48 * 1024 * 1024


def rows_by_rows(left, right, **kwargs):
    return lax.dot_general(
        left, right, (((1,), (1,)), ((), ())), preferred_element_type=jnp.float32, **kwargs
    )


def swap(value, axis, distance):
    count = lax.axis_size(axis)
    return lax.ppermute(value, axis, [(source, source ^ distance) for source in range(count)])


def share_start(nlo, nsub, dlo, dsub, width):
    low = (lax.axis_index("dp") % nlo) ^ dlo
    part = low * nsub + (lax.axis_index("sub") ^ dsub)
    return pl.multiple_of(part * width, width)


def query_kernel(nlo, nsub, inputs, gradient, ids, down, up, *shares):
    tokens, features = inputs.shape
    width = features // (nlo * nsub)
    low_down = rows_by_rows(down[...], inputs[...]).astype(jnp.bfloat16)
    low_up = rows_by_rows(up[...], gradient[...]).astype(jnp.bfloat16)
    rank = low_down.shape[0]
    id_rows = jnp.broadcast_to(ids[...].astype(jnp.bfloat16), (EXTRA, tokens))
    for place, share in enumerate(shares):
        columns = pl.ds(share_start(nlo, nsub, place // nsub, place % nsub, width), width)
        share[0:tokens, :] = inputs[:, columns]
        share[tokens : 2 * tokens, :] = gradient[:, columns]
        share[2 * tokens :, :] = jnp.zeros((EXTRA, width), jnp.bfloat16)
        share[2 * tokens : 2 * tokens + rank, 0:tokens] = low_down
        share[2 * tokens : 2 * tokens + rank, 64 : 64 + tokens] = low_up
        share[2 * tokens :, 128 : 128 + tokens] = id_rows


def training_kernel(nlo, nsub, lengths, inputs, gradient, down, up, *rest):
    outs, (held_inputs, held_gradient, sems) = rest[:nlo], rest[nlo:]
    sequences, slots, features = inputs.shape
    rows = sequences * slots
    rank = down.shape[0]
    width = features // (nlo * nsub)
    pieces = 4
    step = features // pieces
    copies = []
    for array, (source, target) in enumerate(((inputs, held_inputs), (gradient, held_gradient))):
        for piece in range(pieces):
            columns = pl.ds(piece * step, step)
            copy = pltpu.make_async_copy(
                source.at[:, :, columns], target.at[:, :, columns], sems.at[array, piece]
            )
            copy.start()
            copies.append(copy)

    live = jnp.concatenate(
        [
            jnp.concatenate(
                [
                    (lax.broadcasted_iota(jnp.int32, (rank, slots), 1) < lengths[row])
                    if row == column
                    else jnp.zeros((rank, slots), jnp.bool_)
                    for column in range(sequences)
                ],
                axis=1,
            ).astype(jnp.float32)
            for row in range(sequences)
        ],
        axis=0,
    )
    low = []
    for array, (target, weights) in enumerate(((held_inputs, down), (held_gradient, up))):
        total = jnp.zeros((rank, rows), jnp.float32)
        for piece in range(pieces):
            copies[array * pieces + piece].wait()
            columns = pl.ds(piece * step, step)
            total += rows_by_rows(weights[:, columns], target[:, :, columns].reshape(rows, step))
        rounded = total.astype(jnp.bfloat16).astype(jnp.float32)
        low.append((jnp.concatenate([rounded] * sequences, axis=0) * live).astype(jnp.bfloat16))

    for place, out in enumerate(outs):
        columns = pl.ds(share_start(nlo, nsub, place, 0, width), width)
        for half, (factor, target) in enumerate(((low[0], held_gradient), (low[1], held_inputs))):
            product = jnp.dot(
                factor,
                target[:, :, columns].reshape(rows, width),
                preferred_element_type=jnp.float32,
            )
            out[half * sequences * rank : (half + 1) * sequences * rank, :] = product.astype(
                jnp.bfloat16
            )


def score_kernel(nblocks, ndp, nsub, rank, count, *refs):
    blocks, grads = refs[:nblocks], refs[nblocks : nblocks + ndp]
    out, tokens_in, tokens_gr, extras, grad_down, grad_up, sems = refs[nblocks + ndp :]
    tokens = (blocks[0].shape[0] - EXTRA) // 2
    per = grads[0].shape[0] // 2
    copies = []
    for place, block in enumerate(blocks):
        for part, (start, size, target) in enumerate(
            ((0, tokens, tokens_in), (tokens, tokens, tokens_gr))
        ):
            copies.append(
                pltpu.make_async_copy(
                    block.at[pl.ds(start, size), :],
                    target.at[pl.ds(place * size, size), :],
                    sems.at[3 * place + part],
                )
            )
        copies.append(
            pltpu.make_async_copy(
                block.at[pl.ds(2 * tokens, EXTRA), pl.ds(0, 256)],
                extras.at[place],
                sems.at[3 * place + 2],
            )
        )
    for place, grad in enumerate(grads):
        for part, target in enumerate((grad_down, grad_up)):
            copies.append(
                pltpu.make_async_copy(
                    grad.at[pl.ds(part * per, per), :],
                    target.at[pl.ds(place * per, per), :],
                    sems.at[3 * nblocks + 2 * place + part],
                )
            )
    for copy in copies:
        copy.start()
    for copy in copies:
        copy.wait()

    gathered = [extras[place] for place in range(nblocks)]

    def along(lane):
        return jnp.concatenate(
            [piece[:, lane : lane + tokens].astype(jnp.float32) for piece in gathered], axis=1
        )

    low_down, low_up, ids = along(0)[:rank], along(64)[:rank], along(128)[0:1]
    sequences = ndp * per // rank
    total = nblocks * tokens
    product = rows_by_rows(grad_down[...], tokens_gr[...]).reshape(
        sequences, rank, total
    ) * low_down[None]
    product += rows_by_rows(grad_up[...], tokens_in[...]).reshape(
        sequences, rank, total
    ) * low_up[None]
    per_token = jnp.sum(product, axis=1)
    owned = count // nsub
    place = lax.broadcasted_iota(jnp.int32, (count, total), 0)
    number = ((place // owned) ^ lax.axis_index("sub")) * owned + place % owned
    one_hot = (ids.astype(jnp.int32) == number).astype(jnp.float32)
    out[...] = rows_by_rows(one_hot, per_token, precision=lax.Precision.HIGHEST)


def per_device(
    query_inputs,
    query_gradient,
    query_sequence_index,
    training_inputs,
    training_gradient,
    training_length,
    adapter_down_map,
    adapter_up_map,
):
    tokens, features = query_inputs.shape
    sequences, slots, _ = training_inputs.shape
    rank = adapter_down_map.shape[1]
    ndp, nsub, npair = (lax.axis_size(name) for name in ("dp", "sub", "pair"))
    nlo = 2
    width = features // (nlo * nsub)
    count = tokens * ndp * nsub * npair // QMEAN
    down, up = adapter_down_map.T, adapter_up_map.T
    params = pltpu.CompilerParams(vmem_limit_bytes=LIMIT)

    shares = pl.pallas_call(
        functools.partial(query_kernel, nlo, nsub),
        out_shape=[jax.ShapeDtypeStruct((2 * tokens + EXTRA, width), jnp.bfloat16)] * (nlo * nsub),
        in_specs=[VMEM] * 5,
        out_specs=[VMEM] * (nlo * nsub),
        compiler_params=params,
        name="query_shares",
    )(query_inputs, query_gradient, query_sequence_index.reshape(1, tokens), down, up)
    blocks = [shares[0]]
    for place in range(1, nlo * nsub):
        dlo, dsub = place // nsub, place % nsub
        pairs = [
            (i * nsub + j, (i ^ dlo) * nsub + (j ^ dsub)) for i in range(ndp) for j in range(nsub)
        ]
        blocks.append(lax.ppermute(shares[place], ("dp", "sub"), pairs))

    grads = pl.pallas_call(
        functools.partial(training_kernel, nlo, nsub),
        out_shape=[jax.ShapeDtypeStruct((2 * sequences * rank, width), jnp.bfloat16)] * nlo,
        in_specs=[SMEM, HBM, HBM, VMEM, VMEM],
        out_specs=[VMEM] * nlo,
        scratch_shapes=[
            pltpu.VMEM((sequences, slots, features), jnp.bfloat16),
            pltpu.VMEM((sequences, slots, features), jnp.bfloat16),
            pltpu.SemaphoreType.DMA((2, 4)),
        ],
        compiler_params=params,
        name="training_gradients",
    )(training_length, training_inputs, training_gradient, down, up)
    every = [grads[0]] + [swap(grads[distance % nlo], "dp", distance) for distance in range(1, ndp)]

    blocks += [swap(block, "pair", 1) for block in blocks]
    nblocks = len(blocks)
    scores = pl.pallas_call(
        functools.partial(score_kernel, nblocks, ndp, nsub, rank, count),
        out_shape=jax.ShapeDtypeStruct((count, ndp * sequences), jnp.float32),
        in_specs=[HBM] * (nblocks + ndp),
        out_specs=VMEM,
        scratch_shapes=[
            pltpu.VMEM((nblocks * tokens, width), jnp.bfloat16),
            pltpu.VMEM((nblocks * tokens, width), jnp.bfloat16),
            pltpu.VMEM((nblocks, EXTRA, 256), jnp.bfloat16),
            pltpu.VMEM((ndp * sequences * rank, width), jnp.bfloat16),
            pltpu.VMEM((ndp * sequences * rank, width), jnp.bfloat16),
            pltpu.SemaphoreType.DMA((3 * nblocks + 2 * ndp,)),
        ],
        compiler_params=params,
        name="scores",
    )(*blocks, *every)

    scores = scores.reshape(nsub, count // nsub, ndp, sequences)
    distance = nsub // 2
    while distance:
        scores = scores[:distance] + swap(scores[distance:], "sub", distance)
        distance //= 2
    scores = scores[0]
    distance = ndp // 2
    while distance:
        scores = scores[:, :distance] + swap(scores[:, distance:], "dp", distance)
        distance //= 2
    return scores[:, 0]


def solution(mesh):
    placed = (
        P(("groups", "dp", "sub", "pair"), None),
        P(("groups", "dp", "sub", "pair"), None),
        P(("groups", "dp", "sub", "pair")),
        P(("groups", "dp", "pair"), None, None),
        P(("groups", "dp", "pair"), None, None),
        P(("groups", "dp", "pair")),
        P(),
        P(),
    )
    return jax.shard_map(
        per_device,
        mesh=mesh,
        in_specs=placed,
        out_specs=P(("groups", "sub"), ("dp", "pair")),
        check_vma=False,
    )
```

time: 195 us -> 57.1 us (0.29)
  waiting for transfers between devices: 120 us -> 16.7 us
  matrix products: 32.3 us -> 0 us
  starting transfers between devices: 0.9 us -> 19.9 us
  blocking collectives: 15.5 us -> 0 us
  between operations: 14.8 us -> 0.06 us
  Pallas kernels: 0 us -> 9.12 us
  other arithmetic: 3.46 us -> 0.57 us
  local copies, waits for them, and re-layouts: 7.47 us -> 10.3 us
    ppermute x3 -> x13, waiting for transfers between devices: 120 us -> 16.7 us  [the longest x10 16.7 us: swap(): lax.ppermute(value, axis, [(source, source ^ distance) for source in rang...]
    dot_general x22 -> x0, matrix products: 32.3 us -> none  [the longest x16 26.9 us: token_gram(): lax.dot_general(left_rows, right_rows, (((1,), (1,)), ((), ())), preferre...]
    ppermute x3 -> x13, starting transfers between devices: 0.87 us -> 19.9 us  [the longest x10 15.4 us: swap(): lax.ppermute(value, axis, [(source, source ^ distance) for source in rang...]
    unnamed x2 -> x0, blocking collectives: 15.5 us -> none
    pallas_call x0 -> x3, Pallas kernels: none -> 9.12 us  [the longest x1 4.77 us: per_device(): pl.pallas_call(functools.partial(score_kernel, nblocks, ndp, nsub, rank,...]
    unnamed x17 -> x20, local copies, waits for them, and re-layouts: 2.09 us -> 10.2 us
    while x3 -> x0, local copies, waits for them, and re-layouts: 4.79 us -> none
    another operation x1 -> x0, other arithmetic: 2.35 us -> none  [per_device(): jnp.stack([query_inputs, query_gradient])]
  transfers between devices with their start and end apart: 4 -> 13, of which waited for: 3 -> 6; matrix products, arithmetic and copies ran while one was open for 13% -> 0% of each run, Pallas kernels for 0% -> 7%
where the time goes in v1:
time: 57.1 us; the launch traced here: 56.7 us
  starting transfers between devices  19.9 us (35%)
  waiting for transfers between devices  16.7 us (29%)
  local copies, waits for them, and re-layouts  10.3 us (18%)
  Pallas kernels  9.12 us (16%)
    ppermute x10, waiting for transfers between devices, swap(): lax.ppermute(value, axis, [(source, source ^ distance) for source in rang...  16.7 us
    ppermute x10, starting transfers between devices, swap(): lax.ppermute(value, axis, [(source, source ^ distance) for source in rang...  15.4 us
    unnamed x20, local copies, waits for them, and re-layouts  10.2 us
    pallas_call x1, Pallas kernels, per_device(): pl.pallas_call(functools.partial(score_kernel, nblocks, ndp, nsub, rank,...  4.77 us
    ppermute x3, starting transfers between devices, per_device(): blocks.append(lax.ppermute(shares[place], ('dp', 'sub'), pairs))  4.52 us
    pallas_call x1, Pallas kernels, per_device(): pl.pallas_call(functools.partial(training_kernel, nlo, nsub), out_shape=[...  3.89 us
  transfers between devices with their start and end apart: 13, of which 6 were waited for; matrix products, arithmetic and copies ran while one was open for 0% of the time, Pallas kernels for 7%

profile of v1, /device:TPU:0, one launch (start us, length us, event | category | flops | bytes accessed | tf_op | source)
XLA Modules:
  0.0 56.7 jit_solution(11923621139752905540)
XLA Ops:
  0.0 1.0 %copy-done.2 = bf16[64,4096]{1,0:T(8,128)(2,1)S(1)} copy-done((bf16[64,4096]{1,0:T(8,128)(2,1)S(1)}, bf16[64,4096]{1,0:T(8,128)(2,1)}, u32[]{:S(2)}) %copy-start.2) | copy-done | bytes 524312
  1.0 1.0 %copy-done.3 = bf16[64,4096]{1,0:T(8,128)(2,1)S(1)} copy-done((bf16[64,4096]{1,0:T(8,128)(2,1)S(1)}, bf16[64,4096]{1,0:T(8,128)(2,1)}, u32[]{:S(2)}) %copy-start.3) | copy-done | bytes 524312
  2.1 0.9 %copy-done.4 = bf16[4096,16]{0,1:T(8,128)(2,1)S(1)} copy-done((bf16[4096,16]{0,1:T(8,128)(2,1)S(1)}, bf16[4096,16]{0,1:T(8,128)(2,1)}, u32[]{:S(2)}) %copy-start.4) | copy-done | bytes 131096
  3.0 0.9 %copy-done.6 = bf16[4096,16]{0,1:T(8,128)(2,1)S(1)} copy-done((bf16[4096,16]{0,1:T(8,128)(2,1)S(1)}, bf16[4096,16]{0,1:T(8,128)(2,1)}, u32[]{:S(2)}) %copy-start.6) | copy-done | bytes 131096
  3.9 0.7 %copy-done.8 = s32[64]{0:T(128)S(1)} copy-done((s32[64]{0:T(128)S(1)}, s32[64]{0:T(128)}, u32[]{:S(2)}) %copy-start.8) | copy-done | bytes 280
  4.5 0.5 query_shares.1
  5.0 2.9 %collective-permute-start = (bf16[144,1024]{1,0:T(8,128)(2,1)S(1)}, bf16[144,1024]{1,0:T(8,128)(2,1)S(1)}, u32[]{:S(2)}, u32[]{:S(2)}) collective-permute-start(bf16[144,1024]{1,0:T(8,128)(2,1)S(1)} %get-tuple-element.12), channel_id=1, source_target_pairs={{0,2},{2,0},{4,6},{6,4},{8,10},{10,8},{12,14},{14,12},{1,3},{3,1},... | collective-permute-start | bytes 884744 | tf_op jit(solution)/shard_map/ppermute | solution.py:204
  8.0 1.6 %collective-permute-start.1 = (bf16[144,1024]{1,0:T(8,128)(2,1)S(1)}, bf16[144,1024]{1,0:T(8,128)(2,1)S(1)}, u32[]{:S(2)}, u32[]{:S(2)}) collective-permute-start(bf16[144,1024]{1,0:T(8,128)(2,1)S(1)} %get-tuple-element.13), channel_id=1, source_target_pairs={{0,4},{2,6},{4,0},{6,2},{8,12},{10,14},{12,8},{14,10},{1,5},{3,7},... | collective-permute-start | bytes 884744 | tf_op jit(solution)/shard_map/ppermute | solution.py:204
  9.5 1.6 %copy-done = bf16[2,128,4096]{2,1,0:T(8,128)(2,1)S(1)} copy-done((bf16[2,128,4096]{2,1,0:T(8,128)(2,1)S(1)}, bf16[2,128,4096]{2,1,0:T(8,128)(2,1)}, u32[]{:S(2)}) %copy-start) | copy-done | bytes 2097176
  11.1 1.6 %copy-done.1 = bf16[2,128,4096]{2,1,0:T(8,128)(2,1)S(1)} copy-done((bf16[2,128,4096]{2,1,0:T(8,128)(2,1)S(1)}, bf16[2,128,4096]{2,1,0:T(8,128)(2,1)}, u32[]{:S(2)}) %copy-start.1) | copy-done | bytes 2097176
  12.7 0.9 %copy-done.5 = bf16[4096,16]{0,1:T(8,128)(2,1)S(1)} copy-done((bf16[4096,16]{0,1:T(8,128)(2,1)S(1)}, bf16[4096,16]{0,1:T(8,128)(2,1)}, u32[]{:S(2)}) %copy-start.5) | copy-done | bytes 131096
  13.6 0.9 %copy-done.7 = bf16[4096,16]{0,1:T(8,128)(2,1)S(1)} copy-done((bf16[4096,16]{0,1:T(8,128)(2,1)S(1)}, bf16[4096,16]{0,1:T(8,128)(2,1)}, u32[]{:S(2)}) %copy-start.7) | copy-done | bytes 131096
  14.5 0.7 %copy-done.9 = s32[2]{0:T(128)S(1)} copy-done((s32[2]{0:T(128)S(1)}, s32[2]{0:T(128)}, u32[]{:S(2)}) %copy-start.9) | copy-done | bytes 32
  15.2 3.9 %training_gradients.1 = (bf16[64,1024]{1,0:T(8,128)(2,1)S(1)}, bf16[64,1024]{1,0:T(8,128)(2,1)S(1)}) custom-call(s32[2]{0:T(128)S(1)} %copy-done.9, bf16[2,128,4096]{2,1,0:T(8,128)(2,1)S(1)} %copy-done, bf16[2,128,4096]{2,1,0:T(8,128)(2,1)S(1)} %copy-done.1, bf16[16,4096]{1,0:T(8,128)(2,1)S(1)} %bitcast.10, bf16[16,4096]{1,0:T(8,128)(2,1)S(1)} %bitcast.12), custom_call_target="tpu_custom_call" | custom-call | tf_op jit(solution)/shard_map/training_gradients/pallas_call | solution.py:206
  19.1 3.1 %collective-permute-start.8 = (bf16[64,1024]{1,0:T(8,128)(2,1)S(1)}, bf16[64,1024]{1,0:T(8,128)(2,1)S(1)}, u32[]{:S(2)}, u32[]{:S(2)}) collective-permute-start(bf16[64,1024]{1,0:T(8,128)(2,1)S(1)} %get-tuple-element.15.refs_8_), channel_id=1, source_target_pairs={{0,8},{4,12},{8,0},{12,4},{1,9},{5,13},{9,1},{13,5},{2,10},{6,14},... | collective-permute-start | bytes 393224 | tf_op jit(solution)/shard_map/ppermute | solution.py:26
  22.2 0.5 collective-permute-start.4
  22.7 0.1 collective-permute-start.5
  22.7 0.4 collective-permute-start.6
  23.2 4.5 %collective-permute-done.8.refs_10_ = bf16[64,1024]{1,0:T(8,128)(2,1)S(1)} collective-permute-done((bf16[64,1024]{1,0:T(8,128)(2,1)S(1)}, bf16[64,1024]{1,0:T(8,128)(2,1)S(1)}, u32[]{:S(2)}, u32[]{:S(2)}) %collective-permute-start.8) | collective-permute-done | bytes 131104 | tf_op jit(solution)/shard_map/ppermute | solution.py:26
  27.7 3.6 %collective-permute-start.9 = (bf16[64,1024]{1,0:T(8,128)(2,1)S(1)}, bf16[64,1024]{1,0:T(8,128)(2,1)S(1)}, u32[]{:S(2)}, u32[]{:S(2)}) collective-permute-start(bf16[64,1024]{1,0:T(8,128)(2,1)S(1)} %get-tuple-element.16), channel_id=1, source_target_pairs={{0,12},{4,8},{8,4},{12,0},{1,13},{5,9},{9,5},{13,1},{2,14},{6,10},... | collective-permute-start | bytes 393224 | tf_op jit(solution)/shard_map/ppermute | solution.py:26
  31.3 3.2 %collective-permute-done.9.refs_11_ = bf16[64,1024]{1,0:T(8,128)(2,1)S(1)} collective-permute-done((bf16[64,1024]{1,0:T(8,128)(2,1)S(1)}, bf16[64,1024]{1,0:T(8,128)(2,1)S(1)}, u32[]{:S(2)}, u32[]{:S(2)}) %collective-permute-start.9) | collective-permute-done | bytes 131104 | tf_op jit(solution)/shard_map/ppermute | solution.py:26
  34.5 1.7 %collective-permute-start.7 = (bf16[64,1024]{1,0:T(8,128)(2,1)S(1)}, bf16[64,1024]{1,0:T(8,128)(2,1)S(1)}, u32[]{:S(2)}, u32[]{:S(2)}) collective-permute-start(bf16[64,1024]{1,0:T(8,128)(2,1)S(1)} %get-tuple-element.16), channel_id=1, source_target_pairs={{0,4},{4,0},{8,12},{12,8},{1,5},{5,1},{9,13},{13,9},{2,6},{6,2},{1... | collective-permute-start | bytes 393224 | tf_op jit(solution)/shard_map/ppermute | solution.py:26
  36.2 3.3 %collective-permute-done.7.refs_9_ = bf16[64,1024]{1,0:T(8,128)(2,1)S(1)} collective-permute-done((bf16[64,1024]{1,0:T(8,128)(2,1)S(1)}, bf16[64,1024]{1,0:T(8,128)(2,1)S(1)}, u32[]{:S(2)}, u32[]{:S(2)}) %collective-permute-start.7) | collective-permute-done | bytes 131104 | tf_op jit(solution)/shard_map/ppermute | solution.py:26
  39.5 4.8 %scores.1 = f32[16,8]{1,0:T(8,128)S(1)} custom-call(bf16[144,1024]{1,0:T(8,128)(2,1)S(1)} %get-tuple-element.11.refs_0_, bf16[144,1024]{1,0:T(8,128)(2,1)S(1)} %collective-permute-done.refs_1_, bf16[144,1024]{1,0:T(8,128)(2,1)S(1)} %collective-permute-done.1.refs_2_, bf16[144,1024]{1,0:T(8,128)(2,1)S(1)} %collective-permute-done.2.refs_3_, ...), custom_call_target="tpu_custom_call" | custom-call | tf_op jit(solution)/shard_map/scores/pallas_call | solution.py:223
  44.3 0.1 copy.10
  44.4 1.6 %collective-permute-start.10 = (f32[1,8,4,2]{1,3,2,0:T(2,128)S(1)}, f32[1,8,4,2]{1,3,2,0:T(2,128)S(1)}, u32[]{:S(2)}, u32[]{:S(2)}) collective-permute-start(f32[1,8,4,2]{1,3,2,0:T(2,128)S(1)} %bitcast.17), channel_id=1, source_target_pairs={{0,2},{2,0},{1,3},{3,1},{4,6},{6,4},{5,7},{7,5},{8,10},{10,8},{9,1... | collective-permute-start | bytes 776 | tf_op jit(solution)/shard_map/ppermute | solution.py:26
  46.0 2.0 %collective-permute-done.10 = f32[1,8,4,2]{1,3,2,0:T(2,128)S(1)} collective-permute-done((f32[1,8,4,2]{1,3,2,0:T(2,128)S(1)}, f32[1,8,4,2]{1,3,2,0:T(2,128)S(1)}, u32[]{:S(2)}, u32[]{:S(2)}) %collective-permute-start.10) | collective-permute-done | bytes 288 | tf_op jit(solution)/shard_map/ppermute | solution.py:26
  48.0 2.7 %collective-permute-start.11 = (f32[8,2,2]{0,1,2:T(2,128)S(1)}, f32[8,2,2]{0,1,2:T(2,128)S(1)}, u32[]{:S(2)}, u32[]{:S(2)}) collective-permute-start(f32[8,2,2]{0,1,2:T(2,128)S(1)} %slice.35), channel_id=1, source_target_pairs={{0,8},{4,12},{8,0},{12,4},{1,9},{5,13},{9,1},{13,5},{2,10},{6,14},... | collective-permute-start | bytes 392 | tf_op jit(solution)/shard_map/ppermute | solution.py:26
  50.7 1.9 %collective-permute-done.11 = f32[8,2,2]{0,1,2:T(2,128)S(1)} collective-permute-done((f32[8,2,2]{0,1,2:T(2,128)S(1)}, f32[8,2,2]{0,1,2:T(2,128)S(1)}, u32[]{:S(2)}, u32[]{:S(2)}) %collective-permute-start.11) | collective-permute-done | bytes 160 | tf_op jit(solution)/shard_map/ppermute | solution.py:26
  52.6 1.7 %collective-permute-start.12 = (f32[8,1,2]{0,1,2:T(1,128)S(1)}, f32[8,1,2]{0,1,2:T(1,128)S(1)}, u32[]{:S(2)}, u32[]{:S(2)}) collective-permute-start(f32[8,1,2]{0,1,2:T(1,128)S(1)} %slice.37), channel_id=1, source_target_pairs={{0,4},{4,0},{8,12},{12,8},{1,5},{5,1},{9,13},{13,9},{2,6},{6,2},{1... | collective-permute-start | bytes 200 | tf_op jit(solution)/shard_map/ppermute | solution.py:26
  54.3 1.8 %collective-permute-done.12 = f32[8,1,2]{0,1,2:T(1,128)S(1)} collective-permute-done((f32[8,1,2]{0,1,2:T(1,128)S(1)}, f32[8,1,2]{0,1,2:T(1,128)S(1)}, u32[]{:S(2)}, u32[]{:S(2)}) %collective-permute-start.12) | collective-permute-done | bytes 96 | tf_op jit(solution)/shard_map/ppermute | solution.py:26
  56.1 0.6 slice_add_fusion.1
  (26 shorter events, 0.1 us)
Async XLA Ops:
  0.0 1.0 %copy-start.2 = (bf16[64,4096]{1,0:T(8,128)(2,1)S(1)}, bf16[64,4096]{1,0:T(8,128)(2,1)}, u32[]{:S(2)}) copy-start(bf16[64,4096]{1,0:T(8,128)(2,1)} %inputs.2) | copy-start | bytes 1572868
  1.0 1.0 %copy-start.3 = (bf16[64,4096]{1,0:T(8,128)(2,1)S(1)}, bf16[64,4096]{1,0:T(8,128)(2,1)}, u32[]{:S(2)}) copy-start(bf16[64,4096]{1,0:T(8,128)(2,1)} %gradient.2) | copy-start | bytes 1572868
  2.1 0.9 %copy-start.4 = (bf16[4096,16]{0,1:T(8,128)(2,1)S(1)}, bf16[4096,16]{0,1:T(8,128)(2,1)}, u32[]{:S(2)}) copy-start(bf16[4096,16]{0,1:T(8,128)(2,1)} %param.14) | copy-start | bytes 393220
  3.0 0.9 %copy-start.6 = (bf16[4096,16]{0,1:T(8,128)(2,1)S(1)}, bf16[4096,16]{0,1:T(8,128)(2,1)}, u32[]{:S(2)}) copy-start(bf16[4096,16]{0,1:T(8,128)(2,1)} %param.15) | copy-start | bytes 393220
  3.9 0.7 %copy-start.8 = (s32[64]{0:T(128)S(1)}, s32[64]{0:T(128)}, u32[]{:S(2)}) copy-start(s32[64]{0:T(128)} %param.10) | copy-start | bytes 772
  5.0 17.2 %collective-permute-start = (bf16[144,1024]{1,0:T(8,128)(2,1)S(1)}, bf16[144,1024]{1,0:T(8,128)(2,1)S(1)}, u32[]{:S(2)}, u32[]{:S(2)}) collective-permute-start(bf16[144,1024]{1,0:T(8,128)(2,1)S(1)} %get-tuple-element.12), channel_id=1, source_target_pairs={{0,2},{2,0},{4,6},{6,4},{8,10},{10,8},{12,14},{14,12},{1,3},{3,1},... | collective-permute-start | bytes 884744 | tf_op jit(solution)/shard_map/ppermute | solution.py:204
  8.0 14.7 %collective-permute-start.1 = (bf16[144,1024]{1,0:T(8,128)(2,1)S(1)}, bf16[144,1024]{1,0:T(8,128)(2,1)S(1)}, u32[]{:S(2)}, u32[]{:S(2)}) collective-permute-start(bf16[144,1024]{1,0:T(8,128)(2,1)S(1)} %get-tuple-element.13), channel_id=1, source_target_pairs={{0,4},{2,6},{4,0},{6,2},{8,12},{10,14},{12,8},{14,10},{1,5},{3,7},... | collective-permute-start | bytes 884744 | tf_op jit(solution)/shard_map/ppermute | solution.py:204
  9.5 13.2 %collective-permute-start.2 = (bf16[144,1024]{1,0:T(8,128)(2,1)S(1)}, bf16[144,1024]{1,0:T(8,128)(2,1)S(1)}, u32[]{:S(2)}, u32[]{:S(2)}) collective-permute-start(bf16[144,1024]{1,0:T(8,128)(2,1)S(1)} %get-tuple-element.14), channel_id=1, source_target_pairs={{0,6},{2,4},{4,2},{6,0},{8,14},{10,12},{12,10},{14,8},{1,7},{3,5},... | collective-permute-start | bytes 884744 | tf_op jit(solution)/shard_map/ppermute | solution.py:204
  9.5 1.6 %copy-start = (bf16[2,128,4096]{2,1,0:T(8,128)(2,1)S(1)}, bf16[2,128,4096]{2,1,0:T(8,128)(2,1)}, u32[]{:S(2)}) copy-start(bf16[2,128,4096]{2,1,0:T(8,128)(2,1)} %inputs.3) | copy-start | bytes 6291460
  11.1 1.6 %copy-start.1 = (bf16[2,128,4096]{2,1,0:T(8,128)(2,1)S(1)}, bf16[2,128,4096]{2,1,0:T(8,128)(2,1)}, u32[]{:S(2)}) copy-start(bf16[2,128,4096]{2,1,0:T(8,128)(2,1)} %gradient.3) | copy-start | bytes 6291460
  12.7 0.9 %copy-start.5 = (bf16[4096,16]{0,1:T(8,128)(2,1)S(1)}, bf16[4096,16]{0,1:T(8,128)(2,1)}, u32[]{:S(2)}) copy-start(bf16[4096,16]{0,1:T(8,128)(2,1)} %param.14) | copy-start | bytes 393220
  13.6 0.9 %copy-start.7 = (bf16[4096,16]{0,1:T(8,128)(2,1)S(1)}, bf16[4096,16]{0,1:T(8,128)(2,1)}, u32[]{:S(2)}) copy-start(bf16[4096,16]{0,1:T(8,128)(2,1)} %param.15) | copy-start | bytes 393220
  14.5 0.7 %copy-start.9 = (s32[2]{0:T(128)S(1)}, s32[2]{0:T(128)}, u32[]{:S(2)}) copy-start(s32[2]{0:T(128)} %lengths.1) | copy-start | bytes 28
  19.1 8.6 %collective-permute-start.8 = (bf16[64,1024]{1,0:T(8,128)(2,1)S(1)}, bf16[64,1024]{1,0:T(8,128)(2,1)S(1)}, u32[]{:S(2)}, u32[]{:S(2)}) collective-permute-start(bf16[64,1024]{1,0:T(8,128)(2,1)S(1)} %get-tuple-element.15.refs_8_), channel_id=1, source_target_pairs={{0,8},{4,12},{8,0},{12,4},{1,9},{5,13},{9,1},{13,5},{2,10},{6,14},... | collective-permute-start | bytes 393224 | tf_op jit(solution)/shard_map/ppermute | solution.py:26
  22.2 17.4 %collective-permute-start.3 = (bf16[144,1024]{1,0:T(8,128)(2,1)S(1)}, bf16[144,1024]{1,0:T(8,128)(2,1)S(1)}, u32[]{:S(2)}, u32[]{:S(2)}) collective-permute-start(bf16[144,1024]{1,0:T(8,128)(2,1)S(1)} %get-tuple-element.11.refs_0_), channel_id=1, source_target_pairs={{0,1},{1,0},{2,3},{3,2},{4,5},{5,4},{6,7},{7,6},{8,9},{9,8},{10,11... | collective-permute-start | bytes 884744 | tf_op jit(solution)/shard_map/ppermute | solution.py:26
  22.2 17.4 %collective-permute-start.4 = (bf16[144,1024]{1,0:T(8,128)(2,1)S(1)}, bf16[144,1024]{1,0:T(8,128)(2,1)S(1)}, u32[]{:S(2)}, u32[]{:S(2)}) collective-permute-start(bf16[144,1024]{1,0:T(8,128)(2,1)S(1)} %collective-permute-done.refs_1_), channel_id=1, source_target_pairs={{0,1},{1,0},{2,3},{3,2},{4,5},{5,4},{6,7},{7,6},{8,9},{9,8},{10,11... | collective-permute-start | bytes 884744 | tf_op jit(solution)/shard_map/ppermute | solution.py:26
  22.7 16.8 %collective-permute-start.5 = (bf16[144,1024]{1,0:T(8,128)(2,1)S(1)}, bf16[144,1024]{1,0:T(8,128)(2,1)S(1)}, u32[]{:S(2)}, u32[]{:S(2)}) collective-permute-start(bf16[144,1024]{1,0:T(8,128)(2,1)S(1)} %collective-permute-done.1.refs_2_), channel_id=1, source_target_pairs={{0,1},{1,0},{2,3},{3,2},{4,5},{5,4},{6,7},{7,6},{8,9},{9,8},{10,11... | collective-permute-start | bytes 884744 | tf_op jit(solution)/shard_map/ppermute | solution.py:26
  22.7 16.8 %collective-permute-start.6 = (bf16[144,1024]{1,0:T(8,128)(2,1)S(1)}, bf16[144,1024]{1,0:T(8,128)(2,1)S(1)}, u32[]{:S(2)}, u32[]{:S(2)}) collective-permute-start(bf16[144,1024]{1,0:T(8,128)(2,1)S(1)} %collective-permute-done.2.refs_3_), channel_id=1, source_target_pairs={{0,1},{1,0},{2,3},{3,2},{4,5},{5,4},{6,7},{7,6},{8,9},{9,8},{10,11... | collective-permute-start | bytes 884744 | tf_op jit(solution)/shard_map/ppermute | solution.py:26
  27.7 6.8 %collective-permute-start.9 = (bf16[64,1024]{1,0:T(8,128)(2,1)S(1)}, bf16[64,1024]{1,0:T(8,128)(2,1)S(1)}, u32[]{:S(2)}, u32[]{:S(2)}) collective-permute-start(bf16[64,1024]{1,0:T(8,128)(2,1)S(1)} %get-tuple-element.16), channel_id=1, source_target_pairs={{0,12},{4,8},{8,4},{12,0},{1,13},{5,9},{9,5},{13,1},{2,14},{6,10},... | collective-permute-start | bytes 393224 | tf_op jit(solution)/shard_map/ppermute | solution.py:26
  34.5 5.0 %collective-permute-start.7 = (bf16[64,1024]{1,0:T(8,128)(2,1)S(1)}, bf16[64,1024]{1,0:T(8,128)(2,1)S(1)}, u32[]{:S(2)}, u32[]{:S(2)}) collective-permute-start(bf16[64,1024]{1,0:T(8,128)(2,1)S(1)} %get-tuple-element.16), channel_id=1, source_target_pairs={{0,4},{4,0},{8,12},{12,8},{1,5},{5,1},{9,13},{13,9},{2,6},{6,2},{1... | collective-permute-start | bytes 393224 | tf_op jit(solution)/shard_map/ppermute | solution.py:26
  44.4 3.6 %collective-permute-start.10 = (f32[1,8,4,2]{1,3,2,0:T(2,128)S(1)}, f32[1,8,4,2]{1,3,2,0:T(2,128)S(1)}, u32[]{:S(2)}, u32[]{:S(2)}) collective-permute-start(f32[1,8,4,2]{1,3,2,0:T(2,128)S(1)} %bitcast.17), channel_id=1, source_target_pairs={{0,2},{2,0},{1,3},{3,1},{4,6},{6,4},{5,7},{7,5},{8,10},{10,8},{9,1... | collective-permute-start | bytes 776 | tf_op jit(solution)/shard_map/ppermute | solution.py:26
  48.0 4.5 %collective-permute-start.11 = (f32[8,2,2]{0,1,2:T(2,128)S(1)}, f32[8,2,2]{0,1,2:T(2,128)S(1)}, u32[]{:S(2)}, u32[]{:S(2)}) collective-permute-start(f32[8,2,2]{0,1,2:T(2,128)S(1)} %slice.35), channel_id=1, source_target_pairs={{0,8},{4,12},{8,0},{12,4},{1,9},{5,13},{9,1},{13,5},{2,10},{6,14},... | collective-permute-start | bytes 392 | tf_op jit(solution)/shard_map/ppermute | solution.py:26
  52.6 3.6 %collective-permute-start.12 = (f32[8,1,2]{0,1,2:T(1,128)S(1)}, f32[8,1,2]{0,1,2:T(1,128)S(1)}, u32[]{:S(2)}, u32[]{:S(2)}) collective-permute-start(f32[8,1,2]{0,1,2:T(1,128)S(1)} %slice.37), channel_id=1, source_target_pairs={{0,4},{4,0},{8,12},{12,8},{1,5},{5,1},{9,13},{13,9},{2,6},{6,2},{1... | collective-permute-start | bytes 200 | tf_op jit(solution)/shard_map/ppermute | solution.py:26

commit v2 on v1

v2 whole, which is shorter than its diff:
```python
import functools

import jax
import jax.numpy as jnp
from jax import lax
from jax.experimental import pallas as pl
from jax.experimental.pallas import tpu as pltpu
from jax.sharding import PartitionSpec as P

QMEAN = 64
EXTRA = 16
FAR_COST = 40000
VMEM = pl.BlockSpec(memory_space=pltpu.VMEM)
SMEM = pl.BlockSpec(memory_space=pltpu.SMEM)
HBM = pl.BlockSpec(memory_space=pltpu.HBM)
LIMIT = 48 * 1024 * 1024


def rows_by_rows(left, right, **kwargs):
    return lax.dot_general(
        left, right, (((1,), (1,)), ((), ())), preferred_element_type=jnp.float32, **kwargs
    )


def in_hbm(*arrays):
    return [pltpu.with_memory_space_constraint(array, pltpu.HBM) for array in arrays]


def swap(value, axis, distance):
    count = lax.axis_size(axis)
    return lax.ppermute(value, axis, [(source, source ^ distance) for source in range(count)])


def share_start(nlo, nsub, dlo, dsub, width):
    low = (lax.axis_index("dp") % nlo) ^ dlo
    part = low * nsub + (lax.axis_index("sub") ^ dsub)
    return pl.multiple_of(part * width, width)


def query_kernel(nlo, nsub, inputs, gradient, ids, down, up, *rest):
    shares, (held_inputs, held_gradient, held_ids, held_down, held_up, sems) = rest[:-6], rest[-6:]
    tokens, features = inputs.shape
    width = features // (nlo * nsub)
    copies = [
        pltpu.make_async_copy(source, target, sems.at[place])
        for place, (source, target) in enumerate(
            (
                (inputs, held_inputs),
                (down, held_down),
                (gradient, held_gradient),
                (up, held_up),
                (ids, held_ids),
            )
        )
    ]
    for copy in copies:
        copy.start()
    copies[0].wait()
    copies[1].wait()
    low_down = rows_by_rows(held_down[...], held_inputs[...]).astype(jnp.bfloat16)
    for copy in copies[2:]:
        copy.wait()
    low_up = rows_by_rows(held_up[...], held_gradient[...]).astype(jnp.bfloat16)
    rank = low_down.shape[0]
    id_rows = jnp.broadcast_to(held_ids[...].astype(jnp.bfloat16), (EXTRA, tokens))
    for place, share in enumerate(shares):
        columns = pl.ds(share_start(nlo, nsub, place // nsub, place % nsub, width), width)
        share[0:tokens, :] = held_inputs[:, columns]
        share[tokens : 2 * tokens, :] = held_gradient[:, columns]
        share[2 * tokens :, :] = jnp.zeros((EXTRA, width), jnp.bfloat16)
        share[2 * tokens : 2 * tokens + rank, 0:tokens] = low_down
        share[2 * tokens : 2 * tokens + rank, 64 : 64 + tokens] = low_up
        share[2 * tokens :, 128 : 128 + tokens] = id_rows


def training_kernel(nlo, nsub, length_source, inputs, gradient, down, up, *rest):
    outs, scratch = rest[:nlo], rest[nlo:]
    held_inputs, held_gradient, held_down, held_up, lengths, sems, map_sems = scratch
    sequences, slots, features = inputs.shape
    rows = sequences * slots
    rank = down.shape[0]
    width = features // (nlo * nsub)
    pieces = sems.shape[1]
    step = features // pieces
    maps = [
        pltpu.make_async_copy(down, held_down, map_sems.at[0]),
        pltpu.make_async_copy(up, held_up, map_sems.at[1]),
        pltpu.make_async_copy(length_source, lengths, map_sems.at[2]),
    ]
    maps[2].start()
    copies = []
    for array, (source, target) in enumerate(((inputs, held_inputs), (gradient, held_gradient))):
        maps[array].start()
        for piece in range(pieces):
            columns = pl.ds(piece * step, step)
            copy = pltpu.make_async_copy(
                source.at[:, :, columns], target.at[:, :, columns], sems.at[array, piece]
            )
            copy.start()
            copies.append(copy)

    maps[2].wait()
    live = jnp.concatenate(
        [
            jnp.concatenate(
                [
                    (lax.broadcasted_iota(jnp.int32, (rank, slots), 1) < lengths[row])
                    if row == column
                    else jnp.zeros((rank, slots), jnp.bool_)
                    for column in range(sequences)
                ],
                axis=1,
            ).astype(jnp.float32)
            for row in range(sequences)
        ],
        axis=0,
    )
    low = []
    for array, (target, weights) in enumerate(((held_inputs, held_down), (held_gradient, held_up))):
        total = jnp.zeros((rank, rows), jnp.float32)
        maps[array].wait()
        for piece in range(pieces):
            copies[array * pieces + piece].wait()
            columns = pl.ds(piece * step, step)
            total += rows_by_rows(weights[:, columns], target[:, :, columns].reshape(rows, step))
        rounded = total.astype(jnp.bfloat16).astype(jnp.float32)
        low.append((jnp.concatenate([rounded] * sequences, axis=0) * live).astype(jnp.bfloat16))

    for place, out in enumerate(outs):
        columns = pl.ds(share_start(nlo, nsub, place, 0, width), width)
        for half, (factor, target) in enumerate(((low[0], held_gradient), (low[1], held_inputs))):
            product = jnp.dot(
                factor,
                target[:, :, columns].reshape(rows, width),
                preferred_element_type=jnp.float32,
            )
            out[half * sequences * rank : (half + 1) * sequences * rank, :] = product.astype(
                jnp.bfloat16
            )


def stack_kernel(*refs):
    blocks, (grad, out, near) = refs[:-3], refs[-3:]
    nblocks = len(blocks)
    tokens = (blocks[0].shape[0] - EXTRA) // 2
    near[...] = grad[...]
    for place, block in enumerate(blocks):
        out[place * tokens : (place + 1) * tokens, :] = block[0:tokens, :]
        start = (nblocks + place) * tokens
        out[start : start + tokens, :] = block[tokens : 2 * tokens, :]
        start = 2 * nblocks * tokens + place * EXTRA
        out[start : start + EXTRA, :] = block[2 * tokens :, :]


def score_kernel(nblocks, nsub, rank, owned, stacks, grads, *refs):
    token_refs, grad_refs, base, out = (
        refs[:stacks],
        refs[stacks : stacks + grads],
        refs[stacks + grads : -1],
        refs[-1],
    )
    total = (token_refs[0].shape[0] - nblocks * EXTRA) // 2
    tokens = total // nblocks
    per = grad_refs[0].shape[0] // 2
    sequences = grads * per // rank
    grad_down = jnp.concatenate([grad[:per] for grad in grad_refs], axis=0)
    grad_up = jnp.concatenate([grad[per:] for grad in grad_refs], axis=0)
    number = lax.broadcasted_iota(jnp.int32, (owned, total), 0)
    scores = [ref[...] for ref in base] or [jnp.zeros(out.shape, jnp.float32)]
    scores = [scores[0][place] for place in range(nsub)]
    for stack in token_refs:
        pieces = [
            stack[2 * total + place * EXTRA : 2 * total + (place + 1) * EXTRA, 0:256].astype(
                jnp.float32
            )
            for place in range(nblocks)
        ]

        def along(lane, pieces=pieces):
            return jnp.concatenate([piece[:, lane : lane + tokens] for piece in pieces], axis=1)

        low_down, low_up = along(0)[:rank], along(64)[:rank]
        ids = along(128)[0:1].astype(jnp.int32)
        product = rows_by_rows(grad_down, stack[total : 2 * total, :]).reshape(
            sequences, rank, total
        ) * low_down[None]
        product += rows_by_rows(grad_up, stack[0:total, :]).reshape(
            sequences, rank, total
        ) * low_up[None]
        per_token = jnp.sum(product, axis=1)
        for place in range(nsub):
            first = (place ^ lax.axis_index("sub")) * owned
            one_hot = (ids == number + first).astype(jnp.float32)
            scores[place] += rows_by_rows(per_token, one_hot, precision=lax.Precision.HIGHEST)
    for place in range(nsub):
        out[place] = scores[place]


def per_device(
    query_inputs,
    query_gradient,
    query_sequence_index,
    training_inputs,
    training_gradient,
    training_length,
    adapter_down_map,
    adapter_up_map,
):
    tokens, features = query_inputs.shape
    sequences, slots, _ = training_inputs.shape
    rank = adapter_down_map.shape[1]
    ndp, nsub, npair = (lax.axis_size(name) for name in ("dp", "sub", "pair"))
    nlo = 2
    width = features // (nlo * nsub)
    count = tokens * ndp * nsub * npair // QMEAN
    down, up = adapter_down_map.T, adapter_up_map.T
    params = pltpu.CompilerParams(vmem_limit_bytes=LIMIT)

    shares = pl.pallas_call(
        functools.partial(query_kernel, nlo, nsub),
        out_shape=[jax.ShapeDtypeStruct((2 * tokens + EXTRA, width), jnp.bfloat16)] * (nlo * nsub),
        in_specs=[HBM] * 5,
        out_specs=[VMEM] * (nlo * nsub),
        scratch_shapes=[
            pltpu.VMEM((tokens, features), jnp.bfloat16),
            pltpu.VMEM((tokens, features), jnp.bfloat16),
            pltpu.VMEM((1, tokens), jnp.int32),
            pltpu.VMEM((rank, features), jnp.bfloat16),
            pltpu.VMEM((rank, features), jnp.bfloat16),
            pltpu.SemaphoreType.DMA((5,)),
        ],
        compiler_params=params,
        name="query_shares",
    )(*in_hbm(query_inputs, query_gradient, query_sequence_index.reshape(1, tokens), down, up))
    blocks = [shares[0]]
    for place in sorted(range(1, nlo * nsub), key=lambda place: place < nsub):
        dlo, dsub = place // nsub, place % nsub
        pairs = [
            (i * nsub + j, (i ^ dlo) * nsub + (j ^ dsub)) for i in range(ndp) for j in range(nsub)
        ]
        blocks.append(lax.ppermute(shares[place], ("dp", "sub"), pairs))

    grads = pl.pallas_call(
        functools.partial(training_kernel, nlo, nsub),
        out_shape=[jax.ShapeDtypeStruct((2 * sequences * rank, width), jnp.bfloat16)] * nlo,
        in_specs=[HBM] * 5,
        out_specs=[VMEM] * nlo,
        scratch_shapes=[
            pltpu.VMEM((sequences, slots, features), jnp.bfloat16),
            pltpu.VMEM((sequences, slots, features), jnp.bfloat16),
            pltpu.VMEM((rank, features), jnp.bfloat16),
            pltpu.VMEM((rank, features), jnp.bfloat16),
            pltpu.SMEM((sequences,), jnp.int32),
            pltpu.SemaphoreType.DMA((2, 4)),
            pltpu.SemaphoreType.DMA((3,)),
        ],
        cost_estimate=pl.CostEstimate(
            flops=12 * sequences * slots * features * rank,
            bytes_accessed=12 * sequences * slots * features,
            transcendentals=0,
        ),
        compiler_params=params,
        name="training_gradients",
    )(*in_hbm(training_length, training_inputs, training_gradient, down, up))
    nblocks = len(blocks)
    rows = nblocks * (2 * tokens + EXTRA)
    stack, near = pl.pallas_call(
        stack_kernel,
        out_shape=[
            jax.ShapeDtypeStruct((rows, width), jnp.bfloat16),
            jax.ShapeDtypeStruct(grads[-1].shape, jnp.bfloat16),
        ],
        in_specs=[VMEM] * (nblocks + 1),
        out_specs=[VMEM] * 2,
        compiler_params=params,
        name="token_stack",
    )(*blocks, grads[-1])
    far = [swap(grads[distance % nlo], "dp", distance) for distance in range(2, ndp)]
    owned = count // nsub

    def partial(stacks, some, base, flops, name):
        return pl.pallas_call(
            functools.partial(score_kernel, nblocks, nsub, rank, owned, len(stacks), len(some)),
            out_shape=jax.ShapeDtypeStruct((nsub, len(some) * sequences, owned), jnp.float32),
            in_specs=[VMEM] * (len(stacks) + len(some) + len(base)),
            out_specs=VMEM,
            compiler_params=params,
            cost_estimate=pl.CostEstimate(
                flops=flops, bytes_accessed=3 * stack.size, transcendentals=0
            ),
            name=name,
        )(*stacks, *some, *base)

    far_scores = partial([stack], far, [], FAR_COST * stack.size, "far_scores_part")
    other = swap(stack, "pair", 1)
    far_scores = partial([other], far, [far_scores], stack.size, "far_scores")
    near_scores = partial(
        [stack, other], [grads[0], swap(near, "dp", 1)], [], stack.size, "near_scores"
    )
    distance = ndp // 2
    while distance > 1:
        kept = (distance - 2) * sequences
        received = swap(far_scores[:, kept:], "dp", distance)
        near_scores += received[:, : 2 * sequences]
        far_scores = far_scores[:, :kept] + received[:, 2 * sequences :]
        distance //= 2
    distance = nsub // 2
    while distance:
        near_scores = near_scores[:distance] + swap(near_scores[distance:], "sub", distance)
        distance //= 2
    scores = near_scores[0]
    return (scores[:sequences] + swap(scores[sequences:], "dp", 1)).T


def solution(mesh):
    placed = (
        P(("groups", "dp", "sub", "pair"), None),
        P(("groups", "dp", "sub", "pair"), None),
        P(("groups", "dp", "sub", "pair")),
        P(("groups", "dp", "pair"), None, None),
        P(("groups", "dp", "pair"), None, None),
        P(("groups", "dp", "pair")),
        P(),
        P(),
    )
    return jax.shard_map(
        per_device,
        mesh=mesh,
        in_specs=placed,
        out_specs=P(("groups", "sub"), ("dp", "pair")),
        check_vma=False,
    )
```

time: 57.1 us -> 40 us (0.70)
  local copies, waits for them, and re-layouts: 10.3 us -> 0.01 us
  starting transfers between devices: 19.9 us -> 13.6 us
    unnamed x20 -> x0, local copies, waits for them, and re-layouts: 10.2 us -> none
    ppermute x10 -> x7, waiting for transfers between devices: 16.7 us -> 10.1 us  [swap(): lax.ppermute(value, axis, [(source, source ^ distance) for source in rang...]
    ppermute x3, waiting for transfers between devices: 0.01 us -> 6.52 us  [per_device(): blocks.append(lax.ppermute(shares[place], ('dp', 'sub'), pairs))]
    ppermute x10 -> x7, starting transfers between devices: 15.4 us -> 8.95 us  [swap(): lax.ppermute(value, axis, [(source, source ^ distance) for source in rang...]
    pallas_call x1 -> x4, Pallas kernels: 4.77 us -> 2.2 us  [the longest x3 2.11 us: partial(): pl.pallas_call(functools.partial(score_kernel, nblocks, nsub, rank, owned...]
    pallas_call x1, Pallas kernels: 0.46 us -> 1.97 us  [per_device(): pl.pallas_call(functools.partial(query_kernel, nlo, nsub), out_shape=[jax...]
    pallas_call x1, Pallas kernels: 3.89 us -> 4.79 us  [per_device(): pl.pallas_call(functools.partial(training_kernel, nlo, nsub), out_shape=[...]
  transfers between devices with their start and end apart: 13 -> 10, of which waited for: 6 -> 5; matrix products, arithmetic and copies ran while one was open for 0% -> 0% of each run, Pallas kernels for 7% -> 18%
where the time goes in v2:
time: 40 us; the launch traced here: 39.8 us
  waiting for transfers between devices  16.7 us (42%)
  starting transfers between devices  13.6 us (34%)
  Pallas kernels  8.96 us (22%)
  other arithmetic  0.57 us (1%)
    ppermute x7, waiting for transfers between devices, swap(): lax.ppermute(value, axis, [(source, source ^ distance) for source in rang...  10.1 us
    ppermute x7, starting transfers between devices, swap(): lax.ppermute(value, axis, [(source, source ^ distance) for source in rang...  8.95 us
    ppermute x3, waiting for transfers between devices, per_device(): blocks.append(lax.ppermute(shares[place], ('dp', 'sub'), pairs))  6.52 us
    pallas_call x1, Pallas kernels, per_device(): pl.pallas_call(functools.partial(training_kernel, nlo, nsub), out_shape=[...  4.79 us
    ppermute x3, starting transfers between devices, per_device(): blocks.append(lax.ppermute(shares[place], ('dp', 'sub'), pairs))  4.63 us
    pallas_call x3, Pallas kernels, partial(): pl.pallas_call(functools.partial(score_kernel, nblocks, nsub, rank, owned...  2.11 us
    pallas_call x1, Pallas kernels, per_device(): pl.pallas_call(functools.partial(query_kernel, nlo, nsub), out_shape=[jax...  1.97 us
  transfers between devices with their start and end apart: 10, of which 5 were waited for; matrix products, arithmetic and copies ran while one was open for 0% of the time, Pallas kernels for 18%

profile of v2, /device:TPU:0, one launch (start us, length us, event | category | flops | bytes accessed | tf_op | source)
XLA Modules:
  0.0 39.8 jit_solution(12522661827330919308)
XLA Ops:
  0.0 2.0 %query_shares.1 = (bf16[144,1024]{1,0:T(8,128)(2,1)S(1)}, bf16[144,1024]{1,0:T(8,128)(2,1)S(1)}, bf16[144,1024]{1,0:T(8,128)(2,1)S(1)}, bf16[144,1024]{1,0:T(8,128)(2,1)S(1)}) custom-call(bf16[64,4096]{1,0:T(8,128)(2,1)} %inputs.2, bf16[64,4096]{1,0:T(8,128)(2,1)} %gradient.2, s32[1,64]{1,0:T(1,128)} %bitcast.15, bf16[16,4096]{1,0:T(8,128)(2,1)} %bitcast.11, ...), custom_call_target="tpu_custom_call" | custom-call | tf_op jit(solution)/shard_map/query_shares/pallas_call | solution.py:219
  2.0 3.1 %collective-permute-start = (bf16[144,1024]{1,0:T(8,128)(2,1)S(1)}, bf16[144,1024]{1,0:T(8,128)(2,1)S(1)}, u32[]{:S(2)}, u32[]{:S(2)}) collective-permute-start(bf16[144,1024]{1,0:T(8,128)(2,1)S(1)} %get-tuple-element.14), channel_id=1, source_target_pairs={{0,4},{2,6},{4,0},{6,2},{8,12},{10,14},{12,8},{14,10},{1,5},{3,7},... | collective-permute-start | bytes 884744 | tf_op jit(solution)/shard_map/ppermute | solution.py:241
  5.1 1.4 %collective-permute-start.1 = (bf16[144,1024]{1,0:T(8,128)(2,1)S(1)}, bf16[144,1024]{1,0:T(8,128)(2,1)S(1)}, u32[]{:S(2)}, u32[]{:S(2)}) collective-permute-start(bf16[144,1024]{1,0:T(8,128)(2,1)S(1)} %get-tuple-element.15), channel_id=1, source_target_pairs={{0,6},{2,4},{4,2},{6,0},{8,14},{10,12},{12,10},{14,8},{1,7},{3,5},... | collective-permute-start | bytes 884744 | tf_op jit(solution)/shard_map/ppermute | solution.py:241
  6.4 0.2 collective-permute-start.2
  6.6 4.8 %training_gradients.1 = (bf16[64,1024]{1,0:T(8,128)(2,1)S(1)}, bf16[64,1024]{1,0:T(8,128)(2,1)S(1)}) custom-call(s32[2]{0:T(128)} %length_source.1, bf16[2,128,4096]{2,1,0:T(8,128)(2,1)} %inputs.3, bf16[2,128,4096]{2,1,0:T(8,128)(2,1)} %gradient.3, bf16[16,4096]{1,0:T(8,128)(2,1)} %bitcast.12, bf16[16,4096]{1,0:T(8,128)(2,1)} %bitcast.14), custom_call_target="tpu_custom_call" | custom-call | flops 201326592 | bytes 12582912 | tf_op jit(solution)/shard_map/training_gradients/pallas_call | solution.py:243
  11.4 3.0 %collective-permute-start.5 = (bf16[64,1024]{1,0:T(8,128)(2,1)S(1)}, bf16[64,1024]{1,0:T(8,128)(2,1)S(1)}, u32[]{:S(2)}, u32[]{:S(2)}) collective-permute-start(bf16[64,1024]{1,0:T(8,128)(2,1)S(1)} %get-tuple-element.19.refs_2_), channel_id=1, source_target_pairs={{0,8},{4,12},{8,0},{12,4},{1,9},{5,13},{9,1},{13,5},{2,10},{6,14},... | collective-permute-start | bytes 393224 | tf_op jit(solution)/shard_map/ppermute | solution.py:31
  14.4 1.3 %collective-permute-start.6 = (bf16[64,1024]{1,0:T(8,128)(2,1)S(1)}, bf16[64,1024]{1,0:T(8,128)(2,1)S(1)}, u32[]{:S(2)}, u32[]{:S(2)}) collective-permute-start(bf16[64,1024]{1,0:T(8,128)(2,1)S(1)} %get-tuple-element.17.refs_4_), channel_id=1, source_target_pairs={{0,12},{4,8},{8,4},{12,0},{1,13},{5,9},{9,5},{13,1},{2,14},{6,10},... | collective-permute-start | bytes 393224 | tf_op jit(solution)/shard_map/ppermute | solution.py:31
  15.8 0.0 collective-permute-done.refs_1_
  15.8 6.5 %collective-permute-done.1.refs_2_ = bf16[144,1024]{1,0:T(8,128)(2,1)S(1)} collective-permute-done((bf16[144,1024]{1,0:T(8,128)(2,1)S(1)}, bf16[144,1024]{1,0:T(8,128)(2,1)S(1)}, u32[]{:S(2)}, u32[]{:S(2)}) %collective-permute-start.1) | collective-permute-done | bytes 294944 | tf_op jit(solution)/shard_map/ppermute | solution.py:241
  22.3 0.0 collective-permute-done.2.refs_3_
  22.3 0.1 token_stack.1
  22.4 0.1 collective-permute-start.3
  22.5 0.3 collective-permute-start.4
  22.8 0.0 collective-permute-done.5.refs_1_
  22.8 3.6 %collective-permute-done.6.refs_2_ = bf16[64,1024]{1,0:T(8,128)(2,1)S(1)} collective-permute-done((bf16[64,1024]{1,0:T(8,128)(2,1)S(1)}, bf16[64,1024]{1,0:T(8,128)(2,1)S(1)}, u32[]{:S(2)}, u32[]{:S(2)}) %collective-permute-start.6) | collective-permute-done | bytes 131104 | tf_op jit(solution)/shard_map/ppermute | solution.py:31
  26.3 0.6 %far_scores_part.1.refs_3_ = f32[2,4,8]{2,1,0:T(4,128)S(1)} custom-call(bf16[576,1024]{1,0:T(8,128)(2,1)S(1)} %get-tuple-element.18.refs_0_, bf16[64,1024]{1,0:T(8,128)(2,1)S(1)} %collective-permute-done.5.refs_1_, bf16[64,1024]{1,0:T(8,128)(2,1)S(1)} %collective-permute-done.6.refs_2_), custom_call_target="tpu_custom_call" | custom-call | flops 23592960000 | bytes 1769472 | tf_op jit(solution)/shard_map/far_scores_part/pallas_call | solution.py:282
  26.9 0.0 collective-permute-done.3.refs_1_.refs_0_
  26.9 0.6 %far_scores.1 = f32[2,4,8]{2,1,0:T(4,128)S(1)} custom-call(bf16[576,1024]{1,0:T(8,128)(2,1)S(1)} %collective-permute-done.3.refs_1_.refs_0_, bf16[64,1024]{1,0:T(8,128)(2,1)S(1)} %collective-permute-done.5.refs_1_, bf16[64,1024]{1,0:T(8,128)(2,1)S(1)} %collective-permute-done.6.refs_2_, f32[2,4,8]{2,1,0:T(4,128)S(1)} %far_scores_part.1.refs_3_), custom_call_target="tpu_custom_call" | custom-call | flops 589824 | bytes 1769472 | tf_op jit(solution)/shard_map/far_scores/pallas_call | solution.py:282
  27.5 2.1 %collective-permute-start.7 = (f32[2,4,8]{2,1,0:T(4,128)S(1)}, f32[2,4,8]{2,1,0:T(4,128)S(1)}, u32[]{:S(2)}, u32[]{:S(2)}) collective-permute-start(f32[2,4,8]{2,1,0:T(4,128)S(1)} %far_scores.1), channel_id=1, source_target_pairs={{0,8},{4,12},{8,0},{12,4},{1,9},{5,13},{9,1},{13,5},{2,10},{6,14},... | collective-permute-start | bytes 776 | tf_op jit(solution)/shard_map/ppermute | solution.py:31
  29.6 0.0 collective-permute-done.4.refs_3_
  29.6 0.9 %near_scores.1 = f32[2,4,8]{2,1,0:T(4,128)S(1)} custom-call(bf16[576,1024]{1,0:T(8,128)(2,1)S(1)} %get-tuple-element.18.refs_0_, bf16[576,1024]{1,0:T(8,128)(2,1)S(1)} %collective-permute-done.3.refs_1_.refs_0_, bf16[64,1024]{1,0:T(8,128)(2,1)S(1)} %get-tuple-element.19.refs_2_, bf16[64,1024]{1,0:T(8,128)(2,1)S(1)} %collective-permute-done.4.refs_3_), custom_call_target="tpu_custom_call" | custom-call | flops 589824 | bytes 1769472 | tf_op jit(solution)/shard_map/near_scores/pallas_call | solution.py:282
  30.5 1.6 %collective-permute-done.7 = f32[2,4,8]{2,1,0:T(4,128)S(1)} collective-permute-done((f32[2,4,8]{2,1,0:T(4,128)S(1)}, f32[2,4,8]{2,1,0:T(4,128)S(1)}, u32[]{:S(2)}, u32[]{:S(2)}) %collective-permute-start.7) | collective-permute-done | bytes 288 | tf_op jit(solution)/shard_map/ppermute | solution.py:31
  32.1 1.5 %collective-permute-start.8 = (f32[1,4,8]{2,1,0:T(4,128)S(1)}, f32[1,4,8]{2,1,0:T(4,128)S(1)}, u32[]{:S(2)}, u32[]{:S(2)}) collective-permute-start(f32[1,4,8]{2,1,0:T(4,128)S(1)} %slice.25), channel_id=1, source_target_pairs={{0,2},{2,0},{1,3},{3,1},{4,6},{6,4},{5,7},{7,5},{8,10},{10,8},{9,1... | collective-permute-start | bytes 392 | tf_op jit(solution)/shard_map/ppermute | solution.py:31
  33.6 2.1 %collective-permute-done.8 = f32[1,4,8]{2,1,0:T(4,128)S(1)} collective-permute-done((f32[1,4,8]{2,1,0:T(4,128)S(1)}, f32[1,4,8]{2,1,0:T(4,128)S(1)}, u32[]{:S(2)}, u32[]{:S(2)}) %collective-permute-start.8) | collective-permute-done | bytes 160 | tf_op jit(solution)/shard_map/ppermute | solution.py:31
  35.7 0.6 %collective-permute-start.9 = (f32[2,8]{1,0:T(2,128)S(1)}, f32[2,8]{1,0:T(2,128)S(1)}, u32[]{:S(2)}, u32[]{:S(2)}) collective-permute-start(f32[2,8]{1,0:T(2,128)S(1)} %slice_bitcast_fusion), channel_id=1, source_target_pairs={{0,4},{4,0},{8,12},{12,8},{1,5},{5,1},{9,13},{13,9},{2,6},{6,2},{1... | collective-permute-start | bytes 200 | tf_op jit(solution)/shard_map/ppermute | solution.py:31
  36.3 2.9 %collective-permute-done.9 = f32[2,8]{1,0:T(2,128)S(1)} collective-permute-done((f32[2,8]{1,0:T(2,128)S(1)}, f32[2,8]{1,0:T(2,128)S(1)}, u32[]{:S(2)}, u32[]{:S(2)}) %collective-permute-start.9) | collective-permute-done | bytes 96 | tf_op jit(solution)/shard_map/ppermute | solution.py:31
  39.3 0.6 %fusion = f32[8,2]{0,1:T(2,128)} fusion(f32[2,8]{1,0:T(2,128)S(1)} %collective-permute-done.9, f32[1,4,8]{2,1,0:T(4,128)S(1)} %slice_add_fusion), kind=kLoop, calls=%fused_computation.2 | loop fusion | flops 16 | bytes 192 | tf_op jit(solution)/shard_map/transpose | solution.py:312
  (4 shorter events, 0.0 us)
Async XLA Ops:
  2.0 13.8 %collective-permute-start = (bf16[144,1024]{1,0:T(8,128)(2,1)S(1)}, bf16[144,1024]{1,0:T(8,128)(2,1)S(1)}, u32[]{:S(2)}, u32[]{:S(2)}) collective-permute-start(bf16[144,1024]{1,0:T(8,128)(2,1)S(1)} %get-tuple-element.14), channel_id=1, source_target_pairs={{0,4},{2,6},{4,0},{6,2},{8,12},{10,14},{12,8},{14,10},{1,5},{3,7},... | collective-permute-start | bytes 884744 | tf_op jit(solution)/shard_map/ppermute | solution.py:241
  5.1 17.2 %collective-permute-start.1 = (bf16[144,1024]{1,0:T(8,128)(2,1)S(1)}, bf16[144,1024]{1,0:T(8,128)(2,1)S(1)}, u32[]{:S(2)}, u32[]{:S(2)}) collective-permute-start(bf16[144,1024]{1,0:T(8,128)(2,1)S(1)} %get-tuple-element.15), channel_id=1, source_target_pairs={{0,6},{2,4},{4,2},{6,0},{8,14},{10,12},{12,10},{14,8},{1,7},{3,5},... | collective-permute-start | bytes 884744 | tf_op jit(solution)/shard_map/ppermute | solution.py:241
  6.4 15.9 %collective-permute-start.2 = (bf16[144,1024]{1,0:T(8,128)(2,1)S(1)}, bf16[144,1024]{1,0:T(8,128)(2,1)S(1)}, u32[]{:S(2)}, u32[]{:S(2)}) collective-permute-start(bf16[144,1024]{1,0:T(8,128)(2,1)S(1)} %get-tuple-element.16), channel_id=1, source_target_pairs={{0,2},{2,0},{4,6},{6,4},{8,10},{10,8},{12,14},{14,12},{1,3},{3,1},... | collective-permute-start | bytes 884744 | tf_op jit(solution)/shard_map/ppermute | solution.py:241
  11.4 11.4 %collective-permute-start.5 = (bf16[64,1024]{1,0:T(8,128)(2,1)S(1)}, bf16[64,1024]{1,0:T(8,128)(2,1)S(1)}, u32[]{:S(2)}, u32[]{:S(2)}) collective-permute-start(bf16[64,1024]{1,0:T(8,128)(2,1)S(1)} %get-tuple-element.19.refs_2_), channel_id=1, source_target_pairs={{0,8},{4,12},{8,0},{12,4},{1,9},{5,13},{9,1},{13,5},{2,10},{6,14},... | collective-permute-start | bytes 393224 | tf_op jit(solution)/shard_map/ppermute | solution.py:31
  14.4 11.9 %collective-permute-start.6 = (bf16[64,1024]{1,0:T(8,128)(2,1)S(1)}, bf16[64,1024]{1,0:T(8,128)(2,1)S(1)}, u32[]{:S(2)}, u32[]{:S(2)}) collective-permute-start(bf16[64,1024]{1,0:T(8,128)(2,1)S(1)} %get-tuple-element.17.refs_4_), channel_id=1, source_target_pairs={{0,12},{4,8},{8,4},{12,0},{1,13},{5,9},{9,5},{13,1},{2,14},{6,10},... | collective-permute-start | bytes 393224 | tf_op jit(solution)/shard_map/ppermute | solution.py:31
  22.4 4.5 %collective-permute-start.3 = (bf16[576,1024]{1,0:T(8,128)(2,1)S(1)}, bf16[576,1024]{1,0:T(8,128)(2,1)S(1)}, u32[]{:S(2)}, u32[]{:S(2)}) collective-permute-start(bf16[576,1024]{1,0:T(8,128)(2,1)S(1)} %get-tuple-element.18.refs_0_), channel_id=1, source_target_pairs={{0,1},{1,0},{2,3},{3,2},{4,5},{5,4},{6,7},{7,6},{8,9},{9,8},{10,11... | collective-permute-start | bytes 3538952 | tf_op jit(solution)/shard_map/ppermute | solution.py:31
  22.5 7.1 %collective-permute-start.4 = (bf16[64,1024]{1,0:T(8,128)(2,1)S(1)}, bf16[64,1024]{1,0:T(8,128)(2,1)S(1)}, u32[]{:S(2)}, u32[]{:S(2)}) collective-permute-start(bf16[64,1024]{1,0:T(8,128)(2,1)S(1)} %get-tuple-element.20), channel_id=1, source_target_pairs={{0,4},{4,0},{8,12},{12,8},{1,5},{5,1},{9,13},{13,9},{2,6},{6,2},{1... | collective-permute-start | bytes 393224 | tf_op jit(solution)/shard_map/ppermute | solution.py:31
  27.5 4.6 %collective-permute-start.7 = (f32[2,4,8]{2,1,0:T(4,128)S(1)}, f32[2,4,8]{2,1,0:T(4,128)S(1)}, u32[]{:S(2)}, u32[]{:S(2)}) collective-permute-start(f32[2,4,8]{2,1,0:T(4,128)S(1)} %far_scores.1), channel_id=1, source_target_pairs={{0,8},{4,12},{8,0},{12,4},{1,9},{5,13},{9,1},{13,5},{2,10},{6,14},... | collective-permute-start | bytes 776 | tf_op jit(solution)/shard_map/ppermute | solution.py:31
  32.1 3.6 %collective-permute-start.8 = (f32[1,4,8]{2,1,0:T(4,128)S(1)}, f32[1,4,8]{2,1,0:T(4,128)S(1)}, u32[]{:S(2)}, u32[]{:S(2)}) collective-permute-start(f32[1,4,8]{2,1,0:T(4,128)S(1)} %slice.25), channel_id=1, source_target_pairs={{0,2},{2,0},{1,3},{3,1},{4,6},{6,4},{5,7},{7,5},{8,10},{10,8},{9,1... | collective-permute-start | bytes 392 | tf_op jit(solution)/shard_map/ppermute | solution.py:31
  35.7 3.6 %collective-permute-start.9 = (f32[2,8]{1,0:T(2,128)S(1)}, f32[2,8]{1,0:T(2,128)S(1)}, u32[]{:S(2)}, u32[]{:S(2)}) collective-permute-start(f32[2,8]{1,0:T(2,128)S(1)} %slice_bitcast_fusion), channel_id=1, source_target_pairs={{0,4},{4,0},{8,12},{12,8},{1,5},{5,1},{9,13},{13,9},{2,6},{6,2},{1... | collective-permute-start | bytes 200 | tf_op jit(solution)/shard_map/ppermute | solution.py:31

commit v3 on v2

--- a/solution.py
+++ b/solution.py
@@ -8,7 +8,8 @@
 from jax.sharding import PartitionSpec as P
 
 QMEAN = 64
-EXTRA = 16
+EXTRA = 128
+KEPT = 48
 FAR_COST = 40000
 VMEM = pl.BlockSpec(memory_space=pltpu.VMEM)
 SMEM = pl.BlockSpec(memory_space=pltpu.SMEM)
@@ -55,22 +56,25 @@
     ]
     for copy in copies:
         copy.start()
+    starts = [
+        share_start(nlo, nsub, place // nsub, place % nsub, width) for place in range(len(shares))
+    ]
     copies[0].wait()
+    for start, share in zip(starts, shares):
+        share[:, 0:width] = held_inputs[:, pl.ds(start, width)]
     copies[1].wait()
-    low_down = rows_by_rows(held_down[...], held_inputs[...]).astype(jnp.bfloat16)
-    for copy in copies[2:]:
-        copy.wait()
-    low_up = rows_by_rows(held_up[...], held_gradient[...]).astype(jnp.bfloat16)
+    low_down = rows_by_rows(held_down[...], held_inputs[...])
+    copies[2].wait()
+    for start, share in zip(starts, shares):
+        share[:, width : 2 * width] = held_gradient[:, pl.ds(start, width)]
+    copies[3].wait()
+    copies[4].wait()
+    low_up = rows_by_rows(held_up[...], held_gradient[...])
     rank = low_down.shape[0]
-    id_rows = jnp.broadcast_to(held_ids[...].astype(jnp.bfloat16), (EXTRA, tokens))
-    for place, share in enumerate(shares):
-        columns = pl.ds(share_start(nlo, nsub, place // nsub, place % nsub, width), width)
-        share[0:tokens, :] = held_inputs[:, columns]
-        share[tokens : 2 * tokens, :] = held_gradient[:, columns]
-        share[2 * tokens :, :] = jnp.zeros((EXTRA, width), jnp.bfloat16)
-        share[2 * tokens : 2 * tokens + rank, 0:tokens] = low_down
-        share[2 * tokens : 2 * tokens + rank, 64 : 64 + tokens] = low_up
-        share[2 * tokens :, 128 : 128 + tokens] = id_rows
+    id_rows = jnp.broadcast_to(held_ids[...].astype(jnp.float32), (EXTRA - 2 * rank, tokens))
+    extras = jnp.concatenate([low_down, low_up, id_rows], axis=0).T.astype(jnp.bfloat16)
+    for share in shares:
+        share[:, 2 * width :] = extras
 
 
 def training_kernel(nlo, nsub, length_source, inputs, gradient, down, up, *rest):
@@ -88,13 +92,15 @@
         pltpu.make_async_copy(length_source, lengths, map_sems.at[2]),
     ]
     maps[2].start()
+    maps[0].start()
+    maps[1].start()
+    held = (held_inputs, held_gradient)
     copies = []
-    for array, (source, target) in enumerate(((inputs, held_inputs), (gradient, held_gradient))):
-        maps[array].start()
-        for piece in range(pieces):
-            columns = pl.ds(piece * step, step)
+    for piece in range(pieces):
+        columns = pl.ds(piece * step, step)
+        for array, source in enumerate((inputs, gradient)):
             copy = pltpu.make_async_copy(
-                source.at[:, :, columns], target.at[:, :, columns], sems.at[array, piece]
+                source.at[:, :, columns], held[array].at[:, :, columns], sems.at[array, piece]
             )
             copy.start()
             copies.append(copy)
@@ -115,15 +121,19 @@
         ],
         axis=0,
     )
+    maps[0].wait()
+    maps[1].wait()
+    totals = [[0.0] * sequences, [0.0] * sequences]
+    for piece in range(pieces):
+        columns = pl.ds(piece * step, step)
+        for copy in copies[2 * piece : 2 * piece + 2]:
+            copy.wait()
+        for array, weights in enumerate((held_down, held_up)):
+            for row in range(sequences):
+                totals[array][row] += rows_by_rows(weights[:, columns], held[array][row, :, columns])
     low = []
-    for array, (target, weights) in enumerate(((held_inputs, held_down), (held_gradient, held_up))):
-        total = jnp.zeros((rank, rows), jnp.float32)
-        maps[array].wait()
-        for piece in range(pieces):
-            copies[array * pieces + piece].wait()
-            columns = pl.ds(piece * step, step)
-            total += rows_by_rows(weights[:, columns], target[:, :, columns].reshape(rows, step))
-        rounded = total.astype(jnp.bfloat16).astype(jnp.float32)
+    for parts in totals:
+        rounded = jnp.concatenate(parts, axis=1).astype(jnp.bfloat16).astype(jnp.float32)
         low.append((jnp.concatenate([rounded] * sequences, axis=0) * live).astype(jnp.bfloat16))
 
     for place, out in enumerate(outs):
@@ -140,47 +150,54 @@
 
 
 def stack_kernel(*refs):
-    blocks, (grad, out, near) = refs[:-3], refs[-3:]
-    nblocks = len(blocks)
-    tokens = (blocks[0].shape[0] - EXTRA) // 2
-    near[...] = grad[...]
+    blocks, out = refs[:-1], refs[-1]
+    tokens = blocks[0].shape[0]
+    width = out.shape[1]
+    total = len(blocks) * tokens
+    extras = []
     for place, block in enumerate(blocks):
-        out[place * tokens : (place + 1) * tokens, :] = block[0:tokens, :]
-        start = (nblocks + place) * tokens
-        out[start : start + tokens, :] = block[tokens : 2 * tokens, :]
-        start = 2 * nblocks * tokens + place * EXTRA
-        out[start : start + EXTRA, :] = block[2 * tokens :, :]
-
-
-def score_kernel(nblocks, nsub, rank, owned, stacks, grads, *refs):
-    token_refs, grad_refs, base, out = (
-        refs[:stacks],
-        refs[stacks : stacks + grads],
-        refs[stacks + grads : -1],
-        refs[-1],
-    )
-    total = (token_refs[0].shape[0] - nblocks * EXTRA) // 2
-    tokens = total // nblocks
-    per = grad_refs[0].shape[0] // 2
-    sequences = grads * per // rank
-    grad_down = jnp.concatenate([grad[:per] for grad in grad_refs], axis=0)
-    grad_up = jnp.concatenate([grad[per:] for grad in grad_refs], axis=0)
+        out[place * tokens : (place + 1) * tokens, :] = block[:, 0:width]
+        start = total + place * tokens
+        out[start : start + tokens, :] = block[:, width : 2 * width]
+        extras.append(block[:, 2 * width :].astype(jnp.float32).T[:KEPT].astype(jnp.bfloat16))
+    chunk = min(width, total)
+    for place in range(total // chunk):
+        some = extras[place * chunk // tokens : (place + 1) * chunk // tokens]
+        start = 2 * total + place * KEPT
+        out[start : start + KEPT, 0:chunk] = jnp.concatenate(some, axis=1)
+
+
+def gather_kernel(*refs):
+    blocks, out = refs[:-1], refs[-1]
+    for place, block in enumerate(blocks):
+        half = block.shape[0] // 2
+        out[place * half : (place + 1) * half, :] = block[:half, :]
+        start = (len(blocks) + place) * half
+        out[start : start + half, :] = block[half:, :]
+
+
+def copy_kernel(source, _, target):
+    target[...] = source[...]
+
+
+def score_kernel(total, nsub, rank, owned, stacks, *refs):
+    token_refs, grads, out = refs[:stacks], refs[stacks], refs[-1]
+    chunk = min(total, token_refs[0].shape[1])
+    per = grads.shape[0] // 2
+    sequences = per // rank
+    grad_down, grad_up = grads[:per], grads[per:]
     number = lax.broadcasted_iota(jnp.int32, (owned, total), 0)
-    scores = [ref[...] for ref in base] or [jnp.zeros(out.shape, jnp.float32)]
-    scores = [scores[0][place] for place in range(nsub)]
+    scores = [jnp.zeros((sequences, owned), jnp.float32)] * nsub
     for stack in token_refs:
-        pieces = [
-            stack[2 * total + place * EXTRA : 2 * total + (place + 1) * EXTRA, 0:256].astype(
-                jnp.float32
-            )
-            for place in range(nblocks)
-        ]
-
-        def along(lane, pieces=pieces):
-            return jnp.concatenate([piece[:, lane : lane + tokens] for piece in pieces], axis=1)
-
-        low_down, low_up = along(0)[:rank], along(64)[:rank]
-        ids = along(128)[0:1].astype(jnp.int32)
+        extras = jnp.concatenate(
+            [
+                stack[2 * total + place * KEPT : 2 * total + (place + 1) * KEPT, 0:chunk]
+                for place in range(total // chunk)
+            ],
+            axis=1,
+        ).astype(jnp.float32)
+        low_down, low_up = extras[:rank], extras[rank : 2 * rank]
+        ids = extras[2 * rank : 2 * rank + 1].astype(jnp.int32)
         product = rows_by_rows(grad_down, stack[total : 2 * total, :]).reshape(
             sequences, rank, total
         ) * low_down[None]
@@ -218,7 +235,7 @@
 
     shares = pl.pallas_call(
         functools.partial(query_kernel, nlo, nsub),
-        out_shape=[jax.ShapeDtypeStruct((2 * tokens + EXTRA, width), jnp.bfloat16)] * (nlo * nsub),
+        out_shape=[jax.ShapeDtypeStruct((tokens, 2 * width + EXTRA), jnp.bfloat16)] * (nlo * nsub),
         in_specs=[HBM] * 5,
         out_specs=[VMEM] * (nlo * nsub),
         scratch_shapes=[
@@ -251,7 +268,7 @@
             pltpu.VMEM((rank, features), jnp.bfloat16),
             pltpu.VMEM((rank, features), jnp.bfloat16),
             pltpu.SMEM((sequences,), jnp.int32),
-            pltpu.SemaphoreType.DMA((2, 4)),
+            pltpu.SemaphoreType.DMA((2, 2)),
             pltpu.SemaphoreType.DMA((3,)),
         ],
         cost_estimate=pl.CostEstimate(
@@ -263,40 +280,55 @@
         name="training_gradients",
     )(*in_hbm(training_length, training_inputs, training_gradient, down, up))
     nblocks = len(blocks)
-    rows = nblocks * (2 * tokens + EXTRA)
-    stack, near = pl.pallas_call(
-        stack_kernel,
-        out_shape=[
-            jax.ShapeDtypeStruct((rows, width), jnp.bfloat16),
-            jax.ShapeDtypeStruct(grads[-1].shape, jnp.bfloat16),
-        ],
-        in_specs=[VMEM] * (nblocks + 1),
-        out_specs=[VMEM] * 2,
-        compiler_params=params,
-        name="token_stack",
-    )(*blocks, grads[-1])
-    far = [swap(grads[distance % nlo], "dp", distance) for distance in range(2, ndp)]
-    owned = count // nsub
-
-    def partial(stacks, some, base, flops, name):
+    total = nblocks * tokens
+    rows = 2 * total + KEPT * max(1, total // width)
+    def call(kernel, shape, *operands, name, flops=0):
         return pl.pallas_call(
-            functools.partial(score_kernel, nblocks, nsub, rank, owned, len(stacks), len(some)),
-            out_shape=jax.ShapeDtypeStruct((nsub, len(some) * sequences, owned), jnp.float32),
-            in_specs=[VMEM] * (len(stacks) + len(some) + len(base)),
+            kernel,
+            out_shape=jax.ShapeDtypeStruct(*shape),
+            in_specs=[VMEM] * len(operands),
             out_specs=VMEM,
             compiler_params=params,
             cost_estimate=pl.CostEstimate(
-                flops=flops, bytes_accessed=3 * stack.size, transcendentals=0
+                flops=flops, bytes_accessed=rows * width, transcendentals=0
             ),
             name=name,
-        )(*stacks, *some, *base)
-
-    far_scores = partial([stack], far, [], FAR_COST * stack.size, "far_scores_part")
+        )(*operands)
+
+    stack = call(stack_kernel, ((rows, width), jnp.bfloat16), *blocks, name="token_stack")
+    far = [swap(grads[distance % nlo], "dp", distance) for distance in range(2, ndp)]
+    owned = count // nsub
+    per = grads[0].shape[0]
+
+    far = call(
+        gather_kernel,
+        ((per * (ndp - 2), width), jnp.bfloat16),
+        *far,
+        name="far_gradients",
+        flops=FAR_COST * stack.size,
+    )
     other = swap(stack, "pair", 1)
-    far_scores = partial([other], far, [far_scores], stack.size, "far_scores")
-    near_scores = partial(
-        [stack, other], [grads[0], swap(near, "dp", 1)], [], stack.size, "near_scores"
-    )
+    near = call(copy_kernel, ((per, width), jnp.bfloat16), grads[-1], stack, name="near_gradient")
+    near = call(
+        gather_kernel,
+        ((2 * per, width), jnp.bfloat16),
+        grads[0],
+        swap(near, "dp", 1),
+        name="near_gradients",
+    )
+
+    def partial(some, name):
+        return call(
+            functools.partial(score_kernel, total, nsub, rank, owned, 2),
+            ((nsub, some.shape[0] // (2 * rank), owned), jnp.float32),
+            stack,
+            other,
+            some,
+            name=name,
+        )
+
+    far_scores = partial(far, "far_scores")
+    near_scores = partial(near, "near_scores")
     distance = ndp // 2
     while distance > 1:
         kept = (distance - 2) * sequences

time: 40 us -> 39 us (0.975)
  Pallas kernels: 8.96 us -> 7.99 us
  waiting for transfers between devices: 16.7 us -> 16 us
  starting transfers between devices: 13.6 us -> 14.2 us
    pallas_call x1, Pallas kernels: 4.79 us -> 3.87 us  [per_device(): pl.pallas_call(functools.partial(training_kernel, nlo, nsub), out_shape=[...]
    ppermute x7, waiting for transfers between devices: 10.1 us -> 9.3 us  [swap(): lax.ppermute(value, axis, [(source, source ^ distance) for source in rang...]
    ppermute x7, starting transfers between devices: 8.95 us -> 9.56 us  [swap(): lax.ppermute(value, axis, [(source, source ^ distance) for source in rang...]
    pallas_call x4 -> x6, Pallas kernels: 2.2 us -> 2.11 us  [call(): pl.pallas_call(kernel, out_shape=jax.ShapeDtypeStruct(*shape), in_specs=[...]
  transfers between devices with their start and end apart: 10 -> 10, of which waited for: 5 -> 5; matrix products, arithmetic and copies ran while one was open for 0% -> 0% of each run, Pallas kernels for 18% -> 15%
where the time goes in v3:
time: 39 us; the launch traced here: 38.9 us
  waiting for transfers between devices  16 us (41%)
  starting transfers between devices  14.2 us (36%)
  Pallas kernels  7.99 us (20%)
  other arithmetic  0.57 us (1%)
    ppermute x7, starting transfers between devices, swap(): lax.ppermute(value, axis, [(source, source ^ distance) for source in rang...  9.56 us
    ppermute x7, waiting for transfers between devices, swap(): lax.ppermute(value, axis, [(source, source ^ distance) for source in rang...  9.3 us
    ppermute x3, waiting for transfers between devices, per_device(): blocks.append(lax.ppermute(shares[place], ('dp', 'sub'), pairs))  6.73 us
    ppermute x3, starting transfers between devices, per_device(): blocks.append(lax.ppermute(shares[place], ('dp', 'sub'), pairs))  4.63 us
    pallas_call x1, Pallas kernels, per_device(): pl.pallas_call(functools.partial(training_kernel, nlo, nsub), out_shape=[...  3.87 us
    pallas_call x6, Pallas kernels, call(): pl.pallas_call(kernel, out_shape=jax.ShapeDtypeStruct(*shape), in_specs=[...  2.11 us
    pallas_call x1, Pallas kernels, per_device(): pl.pallas_call(functools.partial(query_kernel, nlo, nsub), out_shape=[jax...  2.01 us
  transfers between devices with their start and end apart: 10, of which 5 were waited for; matrix products, arithmetic and copies ran while one was open for 0% of the time, Pallas kernels for 15%

profile of v3, /device:TPU:0, one launch (start us, length us, event | category | flops | bytes accessed | tf_op | source)
XLA Modules:
  0.0 38.9 jit_solution(6717392851121531343)
XLA Ops:
  0.0 2.0 %query_shares.1 = (bf16[64,2176]{1,0:T(8,128)(2,1)S(1)}, bf16[64,2176]{1,0:T(8,128)(2,1)S(1)}, bf16[64,2176]{1,0:T(8,128)(2,1)S(1)}, bf16[64,2176]{1,0:T(8,128)(2,1)S(1)}) custom-call(bf16[64,4096]{1,0:T(8,128)(2,1)} %inputs.2, bf16[64,4096]{1,0:T(8,128)(2,1)} %gradient.2, s32[1,64]{1,0:T(1,128)} %bitcast.15, bf16[16,4096]{1,0:T(8,128)(2,1)} %bitcast.11, ...), custom_call_target="tpu_custom_call" | custom-call | tf_op jit(solution)/shard_map/query_shares/pallas_call | solution.py:236
  2.0 3.1 %collective-permute-start = (bf16[64,2176]{1,0:T(8,128)(2,1)S(1)}, bf16[64,2176]{1,0:T(8,128)(2,1)S(1)}, u32[]{:S(2)}, u32[]{:S(2)}) collective-permute-start(bf16[64,2176]{1,0:T(8,128)(2,1)S(1)} %get-tuple-element.12), channel_id=1, source_target_pairs={{0,4},{2,6},{4,0},{6,2},{8,12},{10,14},{12,8},{14,10},{1,5},{3,7},... | collective-permute-start | bytes 835592 | tf_op jit(solution)/shard_map/ppermute | solution.py:258
  5.1 1.4 %collective-permute-start.1 = (bf16[64,2176]{1,0:T(8,128)(2,1)S(1)}, bf16[64,2176]{1,0:T(8,128)(2,1)S(1)}, u32[]{:S(2)}, u32[]{:S(2)}) collective-permute-start(bf16[64,2176]{1,0:T(8,128)(2,1)S(1)} %get-tuple-element.13), channel_id=1, source_target_pairs={{0,6},{2,4},{4,2},{6,0},{8,14},{10,12},{12,10},{14,8},{1,7},{3,5},... | collective-permute-start | bytes 835592 | tf_op jit(solution)/shard_map/ppermute | solution.py:258
  6.5 0.2 collective-permute-start.2
  6.6 3.9 %training_gradients.1 = (bf16[64,1024]{1,0:T(8,128)(2,1)S(1)}, bf16[64,1024]{1,0:T(8,128)(2,1)S(1)}) custom-call(s32[2]{0:T(128)} %length_source.1, bf16[2,128,4096]{2,1,0:T(8,128)(2,1)} %inputs.3, bf16[2,128,4096]{2,1,0:T(8,128)(2,1)} %gradient.3, bf16[16,4096]{1,0:T(8,128)(2,1)} %bitcast.12, bf16[16,4096]{1,0:T(8,128)(2,1)} %bitcast.14), custom_call_target="tpu_custom_call" | custom-call | flops 201326592 | bytes 12582912 | tf_op jit(solution)/shard_map/training_gradients/pallas_call | solution.py:260
  10.5 3.0 %collective-permute-start.5 = (bf16[64,1024]{1,0:T(8,128)(2,1)S(1)}, bf16[64,1024]{1,0:T(8,128)(2,1)S(1)}, u32[]{:S(2)}, u32[]{:S(2)}) collective-permute-start(bf16[64,1024]{1,0:T(8,128)(2,1)S(1)} %get-tuple-element.15.refs_0_), channel_id=1, source_target_pairs={{0,8},{4,12},{8,0},{12,4},{1,9},{5,13},{9,1},{13,5},{2,10},{6,14},... | collective-permute-start | bytes 393224 | tf_op jit(solution)/shard_map/ppermute | solution.py:32
  13.6 1.3 %collective-permute-start.6 = (bf16[64,1024]{1,0:T(8,128)(2,1)S(1)}, bf16[64,1024]{1,0:T(8,128)(2,1)S(1)}, u32[]{:S(2)}, u32[]{:S(2)}) collective-permute-start(bf16[64,1024]{1,0:T(8,128)(2,1)S(1)} %get-tuple-element.16.source), channel_id=1, source_target_pairs={{0,12},{4,8},{8,4},{12,0},{1,13},{5,9},{9,5},{13,1},{2,14},{6,10},... | collective-permute-start | bytes 393224 | tf_op jit(solution)/shard_map/ppermute | solution.py:32
  14.9 0.0 collective-permute-done.refs_1_
  14.9 6.7 %collective-permute-done.1.refs_2_ = bf16[64,2176]{1,0:T(8,128)(2,1)S(1)} collective-permute-done((bf16[64,2176]{1,0:T(8,128)(2,1)S(1)}, bf16[64,2176]{1,0:T(8,128)(2,1)S(1)}, u32[]{:S(2)}, u32[]{:S(2)}) %collective-permute-start.1) | collective-permute-done | bytes 278560 | tf_op jit(solution)/shard_map/ppermute | solution.py:258
  21.6 0.0 collective-permute-done.2.refs_3_
  21.6 0.2 token_stack.1._.refs_0_
  21.9 0.1 collective-permute-start.3
  22.0 0.3 collective-permute-start.4
  22.2 0.0 collective-permute-done.5.refs_0_
  22.3 3.4 %collective-permute-done.6.refs_1_ = bf16[64,1024]{1,0:T(8,128)(2,1)S(1)} collective-permute-done((bf16[64,1024]{1,0:T(8,128)(2,1)S(1)}, bf16[64,1024]{1,0:T(8,128)(2,1)S(1)}, u32[]{:S(2)}, u32[]{:S(2)}) %collective-permute-start.6) | collective-permute-done | bytes 131104 | tf_op jit(solution)/shard_map/ppermute | solution.py:32
  25.7 0.0 collective-permute-done.3.refs_1_
  25.7 0.9 %far_scores.1 = f32[2,4,8]{2,1,0:T(4,128)S(1)} custom-call(bf16[560,1024]{1,0:T(8,128)(2,1)S(1)} %token_stack.1._.refs_0_, bf16[560,1024]{1,0:T(8,128)(2,1)S(1)} %collective-permute-done.3.refs_1_, bf16[128,1024]{1,0:T(8,128)(2,1)S(1)} %far_gradients.1.refs_2_), custom_call_target="tpu_custom_call" | custom-call | bytes 573440 | tf_op jit(solution)/shard_map/far_scores/pallas_call | solution.py:286
  26.6 1.8 %collective-permute-start.7 = (f32[2,4,8]{2,1,0:T(4,128)S(1)}, f32[2,4,8]{2,1,0:T(4,128)S(1)}, u32[]{:S(2)}, u32[]{:S(2)}) collective-permute-start(f32[2,4,8]{2,1,0:T(4,128)S(1)} %far_scores.1), channel_id=1, source_target_pairs={{0,8},{4,12},{8,0},{12,4},{1,9},{5,13},{9,1},{13,5},{2,10},{6,14},... | collective-permute-start | bytes 776 | tf_op jit(solution)/shard_map/ppermute | solution.py:32
  28.4 0.0 collective-permute-done.4.refs_1_
  28.4 0.9 %near_scores.1 = f32[2,4,8]{2,1,0:T(4,128)S(1)} custom-call(bf16[560,1024]{1,0:T(8,128)(2,1)S(1)} %token_stack.1._.refs_0_, bf16[560,1024]{1,0:T(8,128)(2,1)S(1)} %collective-permute-done.3.refs_1_, bf16[128,1024]{1,0:T(8,128)(2,1)S(1)} %near_gradients.1.refs_2_), custom_call_target="tpu_custom_call" | custom-call | bytes 573440 | tf_op jit(solution)/shard_map/near_scores/pallas_call | solution.py:286
  29.4 1.8 %collective-permute-done.7 = f32[2,4,8]{2,1,0:T(4,128)S(1)} collective-permute-done((f32[2,4,8]{2,1,0:T(4,128)S(1)}, f32[2,4,8]{2,1,0:T(4,128)S(1)}, u32[]{:S(2)}, u32[]{:S(2)}) %collective-permute-start.7) | collective-permute-done | bytes 288 | tf_op jit(solution)/shard_map/ppermute | solution.py:32
  31.1 1.5 %collective-permute-start.8 = (f32[1,4,8]{2,1,0:T(4,128)S(1)}, f32[1,4,8]{2,1,0:T(4,128)S(1)}, u32[]{:S(2)}, u32[]{:S(2)}) collective-permute-start(f32[1,4,8]{2,1,0:T(4,128)S(1)} %slice.25), channel_id=1, source_target_pairs={{0,2},{2,0},{1,3},{3,1},{4,6},{6,4},{5,7},{7,5},{8,10},{10,8},{9,1... | collective-permute-start | bytes 392 | tf_op jit(solution)/shard_map/ppermute | solution.py:32
  32.7 2.0 %collective-permute-done.8 = f32[1,4,8]{2,1,0:T(4,128)S(1)} collective-permute-done((f32[1,4,8]{2,1,0:T(4,128)S(1)}, f32[1,4,8]{2,1,0:T(4,128)S(1)}, u32[]{:S(2)}, u32[]{:S(2)}) %collective-permute-start.8) | collective-permute-done | bytes 160 | tf_op jit(solution)/shard_map/ppermute | solution.py:32
  34.7 1.5 %collective-permute-start.9 = (f32[2,8]{1,0:T(2,128)S(1)}, f32[2,8]{1,0:T(2,128)S(1)}, u32[]{:S(2)}, u32[]{:S(2)}) collective-permute-start(f32[2,8]{1,0:T(2,128)S(1)} %slice_bitcast_fusion), channel_id=1, source_target_pairs={{0,4},{4,0},{8,12},{12,8},{1,5},{5,1},{9,13},{13,9},{2,6},{6,2},{1... | collective-permute-start | bytes 200 | tf_op jit(solution)/shard_map/ppermute | solution.py:32
  36.2 2.1 %collective-permute-done.9 = f32[2,8]{1,0:T(2,128)S(1)} collective-permute-done((f32[2,8]{1,0:T(2,128)S(1)}, f32[2,8]{1,0:T(2,128)S(1)}, u32[]{:S(2)}, u32[]{:S(2)}) %collective-permute-start.9) | collective-permute-done | bytes 96 | tf_op jit(solution)/shard_map/ppermute | solution.py:32
  38.3 0.6 %fusion = f32[8,2]{0,1:T(2,128)} fusion(f32[2,8]{1,0:T(2,128)S(1)} %collective-permute-done.9, f32[1,4,8]{2,1,0:T(4,128)S(1)} %slice_add_fusion), kind=kLoop, calls=%fused_computation.2 | loop fusion | flops 16 | bytes 192 | tf_op jit(solution)/shard_map/transpose | solution.py:344
  (7 shorter events, 0.1 us)
Async XLA Ops:
  2.0 12.9 %collective-permute-start = (bf16[64,2176]{1,0:T(8,128)(2,1)S(1)}, bf16[64,2176]{1,0:T(8,128)(2,1)S(1)}, u32[]{:S(2)}, u32[]{:S(2)}) collective-permute-start(bf16[64,2176]{1,0:T(8,128)(2,1)S(1)} %get-tuple-element.12), channel_id=1, source_target_pairs={{0,4},{2,6},{4,0},{6,2},{8,12},{10,14},{12,8},{14,10},{1,5},{3,7},... | collective-permute-start | bytes 835592 | tf_op jit(solution)/shard_map/ppermute | solution.py:258
  5.1 16.5 %collective-permute-start.1 = (bf16[64,2176]{1,0:T(8,128)(2,1)S(1)}, bf16[64,2176]{1,0:T(8,128)(2,1)S(1)}, u32[]{:S(2)}, u32[]{:S(2)}) collective-permute-start(bf16[64,2176]{1,0:T(8,128)(2,1)S(1)} %get-tuple-element.13), channel_id=1, source_target_pairs={{0,6},{2,4},{4,2},{6,0},{8,14},{10,12},{12,10},{14,8},{1,7},{3,5},... | collective-permute-start | bytes 835592 | tf_op jit(solution)/shard_map/ppermute | solution.py:258
  6.5 15.2 %collective-permute-start.2 = (bf16[64,2176]{1,0:T(8,128)(2,1)S(1)}, bf16[64,2176]{1,0:T(8,128)(2,1)S(1)}, u32[]{:S(2)}, u32[]{:S(2)}) collective-permute-start(bf16[64,2176]{1,0:T(8,128)(2,1)S(1)} %get-tuple-element.14), channel_id=1, source_target_pairs={{0,2},{2,0},{4,6},{6,4},{8,10},{10,8},{12,14},{14,12},{1,3},{3,1},... | collective-permute-start | bytes 835592 | tf_op jit(solution)/shard_map/ppermute | solution.py:258
  10.5 11.7 %collective-permute-start.5 = (bf16[64,1024]{1,0:T(8,128)(2,1)S(1)}, bf16[64,1024]{1,0:T(8,128)(2,1)S(1)}, u32[]{:S(2)}, u32[]{:S(2)}) collective-permute-start(bf16[64,1024]{1,0:T(8,128)(2,1)S(1)} %get-tuple-element.15.refs_0_), channel_id=1, source_target_pairs={{0,8},{4,12},{8,0},{12,4},{1,9},{5,13},{9,1},{13,5},{2,10},{6,14},... | collective-permute-start | bytes 393224 | tf_op jit(solution)/shard_map/ppermute | solution.py:32
  13.6 12.1 %collective-permute-start.6 = (bf16[64,1024]{1,0:T(8,128)(2,1)S(1)}, bf16[64,1024]{1,0:T(8,128)(2,1)S(1)}, u32[]{:S(2)}, u32[]{:S(2)}) collective-permute-start(bf16[64,1024]{1,0:T(8,128)(2,1)S(1)} %get-tuple-element.16.source), channel_id=1, source_target_pairs={{0,12},{4,8},{8,4},{12,0},{1,13},{5,9},{9,5},{13,1},{2,14},{6,10},... | collective-permute-start | bytes 393224 | tf_op jit(solution)/shard_map/ppermute | solution.py:32
  21.9 3.8 %collective-permute-start.3 = (bf16[560,1024]{1,0:T(8,128)(2,1)S(1)}, bf16[560,1024]{1,0:T(8,128)(2,1)S(1)}, u32[]{:S(2)}, u32[]{:S(2)}) collective-permute-start(bf16[560,1024]{1,0:T(8,128)(2,1)S(1)} %token_stack.1._.refs_0_), channel_id=1, source_target_pairs={{0,1},{1,0},{2,3},{3,2},{4,5},{5,4},{6,7},{7,6},{8,9},{9,8},{10,11... | collective-permute-start | bytes 3440648 | tf_op jit(solution)/shard_map/ppermute | solution.py:32
  22.0 6.5 %collective-permute-start.4 = (bf16[64,1024]{1,0:T(8,128)(2,1)S(1)}, bf16[64,1024]{1,0:T(8,128)(2,1)S(1)}, u32[]{:S(2)}, u32[]{:S(2)}) collective-permute-start(bf16[64,1024]{1,0:T(8,128)(2,1)S(1)} %near_gradient.1), channel_id=1, source_target_pairs={{0,4},{4,0},{8,12},{12,8},{1,5},{5,1},{9,13},{13,9},{2,6},{6,2},{1... | collective-permute-start | bytes 393224 | tf_op jit(solution)/shard_map/ppermute | solution.py:32
  26.6 4.5 %collective-permute-start.7 = (f32[2,4,8]{2,1,0:T(4,128)S(1)}, f32[2,4,8]{2,1,0:T(4,128)S(1)}, u32[]{:S(2)}, u32[]{:S(2)}) collective-permute-start(f32[2,4,8]{2,1,0:T(4,128)S(1)} %far_scores.1), channel_id=1, source_target_pairs={{0,8},{4,12},{8,0},{12,4},{1,9},{5,13},{9,1},{13,5},{2,10},{6,14},... | collective-permute-start | bytes 776 | tf_op jit(solution)/shard_map/ppermute | solution.py:32
  31.1 3.6 %collective-permute-start.8 = (f32[1,4,8]{2,1,0:T(4,128)S(1)}, f32[1,4,8]{2,1,0:T(4,128)S(1)}, u32[]{:S(2)}, u32[]{:S(2)}) collective-permute-start(f32[1,4,8]{2,1,0:T(4,128)S(1)} %slice.25), channel_id=1, source_target_pairs={{0,2},{2,0},{1,3},{3,1},{4,6},{6,4},{5,7},{7,5},{8,10},{10,8},{9,1... | collective-permute-start | bytes 392 | tf_op jit(solution)/shard_map/ppermute | solution.py:32
  34.7 3.6 %collective-permute-start.9 = (f32[2,8]{1,0:T(2,128)S(1)}, f32[2,8]{1,0:T(2,128)S(1)}, u32[]{:S(2)}, u32[]{:S(2)}) collective-permute-start(f32[2,8]{1,0:T(2,128)S(1)} %slice_bitcast_fusion), channel_id=1, source_target_pairs={{0,4},{4,0},{8,12},{12,8},{1,5},{5,1},{9,13},{13,9},{2,6},{6,2},{1... | collective-permute-start | bytes 200 | tf_op jit(solution)/shard_map/ppermute | solution.py:32

commit v4 on v3

--- a/solution.py
+++ b/solution.py
@@ -62,14 +62,15 @@
     copies[0].wait()
     for start, share in zip(starts, shares):
         share[:, 0:width] = held_inputs[:, pl.ds(start, width)]
-    copies[1].wait()
-    low_down = rows_by_rows(held_down[...], held_inputs[...])
-    copies[2].wait()
+    for copy in copies[1:]:
+        copy.wait()
+    low_down, low_up = 0.0, 0.0
+    for half in range(2):
+        columns = pl.ds(half * features // 2, features // 2)
+        low_down += rows_by_rows(held_down[:, columns], held_inputs[:, columns])
+        low_up += rows_by_rows(held_up[:, columns], held_gradient[:, columns])
     for start, share in zip(starts, shares):
         share[:, width : 2 * width] = held_gradient[:, pl.ds(start, width)]
-    copies[3].wait()
-    copies[4].wait()
-    low_up = rows_by_rows(held_up[...], held_gradient[...])
     rank = low_down.shape[0]
     id_rows = jnp.broadcast_to(held_ids[...].astype(jnp.float32), (EXTRA - 2 * rank, tokens))
     extras = jnp.concatenate([low_down, low_up, id_rows], axis=0).T.astype(jnp.bfloat16)
@@ -279,7 +280,7 @@
         compiler_params=params,
         name="training_gradients",
     )(*in_hbm(training_length, training_inputs, training_gradient, down, up))
-    nblocks = len(blocks)
+    nblocks = nlo * nsub
     total = nblocks * tokens
     rows = 2 * total + KEPT * max(1, total // width)
     def call(kernel, shape, *operands, name, flops=0):

time: 39 us -> 38.8 us (level)
  no operation moved by 1% of the time
where the time goes in v4:
time: 38.8 us; the launch traced here: 38.7 us
  waiting for transfers between devices  16 us (41%)
  starting transfers between devices  14.2 us (37%)
  Pallas kernels  7.78 us (20%)
  other arithmetic  0.57 us (1%)
    ppermute x7, starting transfers between devices, swap(): lax.ppermute(value, axis, [(source, source ^ distance) for source in rang...  9.56 us
    ppermute x7, waiting for transfers between devices, swap(): lax.ppermute(value, axis, [(source, source ^ distance) for source in rang...  9.3 us
    ppermute x3, waiting for transfers between devices, per_device(): blocks.append(lax.ppermute(shares[place], ('dp', 'sub'), pairs))  6.74 us
    ppermute x3, starting transfers between devices, per_device(): blocks.append(lax.ppermute(shares[place], ('dp', 'sub'), pairs))  4.63 us
    pallas_call x1, Pallas kernels, per_device(): pl.pallas_call(functools.partial(training_kernel, nlo, nsub), out_shape=[...  3.87 us
    pallas_call x6, Pallas kernels, call(): pl.pallas_call(kernel, out_shape=jax.ShapeDtypeStruct(*shape), in_specs=[...  2.11 us
    pallas_call x1, Pallas kernels, per_device(): pl.pallas_call(functools.partial(query_kernel, nlo, nsub), out_shape=[jax...  1.8 us
  transfers between devices with their start and end apart: 10, of which 5 were waited for; matrix products, arithmetic and copies ran while one was open for 0% of the time, Pallas kernels for 15%

profile of v4, /device:TPU:0, one launch (start us, length us, event | category | flops | bytes accessed | tf_op | source)
XLA Modules:
  0.0 38.7 jit_solution(2120252147387760557)
XLA Ops:
  0.0 1.8 %query_shares.1 = (bf16[64,2176]{1,0:T(8,128)(2,1)S(1)}, bf16[64,2176]{1,0:T(8,128)(2,1)S(1)}, bf16[64,2176]{1,0:T(8,128)(2,1)S(1)}, bf16[64,2176]{1,0:T(8,128)(2,1)S(1)}) custom-call(bf16[64,4096]{1,0:T(8,128)(2,1)} %inputs.2, bf16[64,4096]{1,0:T(8,128)(2,1)} %gradient.2, s32[1,64]{1,0:T(1,128)} %bitcast.15, bf16[16,4096]{1,0:T(8,128)(2,1)} %bitcast.11, ...), custom_call_target="tpu_custom_call" | custom-call | tf_op jit(solution)/shard_map/query_shares/pallas_call | solution.py:237
  1.8 3.1 %collective-permute-start = (bf16[64,2176]{1,0:T(8,128)(2,1)S(1)}, bf16[64,2176]{1,0:T(8,128)(2,1)S(1)}, u32[]{:S(2)}, u32[]{:S(2)}) collective-permute-start(bf16[64,2176]{1,0:T(8,128)(2,1)S(1)} %get-tuple-element.12), channel_id=1, source_target_pairs={{0,4},{2,6},{4,0},{6,2},{8,12},{10,14},{12,8},{14,10},{1,5},{3,7},... | collective-permute-start | bytes 835592 | tf_op jit(solution)/shard_map/ppermute | solution.py:259
  4.9 1.4 %collective-permute-start.1 = (bf16[64,2176]{1,0:T(8,128)(2,1)S(1)}, bf16[64,2176]{1,0:T(8,128)(2,1)S(1)}, u32[]{:S(2)}, u32[]{:S(2)}) collective-permute-start(bf16[64,2176]{1,0:T(8,128)(2,1)S(1)} %get-tuple-element.13), channel_id=1, source_target_pairs={{0,6},{2,4},{4,2},{6,0},{8,14},{10,12},{12,10},{14,8},{1,7},{3,5},... | collective-permute-start | bytes 835592 | tf_op jit(solution)/shard_map/ppermute | solution.py:259
  6.3 0.2 collective-permute-start.2
  6.4 3.9 %training_gradients.1 = (bf16[64,1024]{1,0:T(8,128)(2,1)S(1)}, bf16[64,1024]{1,0:T(8,128)(2,1)S(1)}) custom-call(s32[2]{0:T(128)} %length_source.1, bf16[2,128,4096]{2,1,0:T(8,128)(2,1)} %inputs.3, bf16[2,128,4096]{2,1,0:T(8,128)(2,1)} %gradient.3, bf16[16,4096]{1,0:T(8,128)(2,1)} %bitcast.12, bf16[16,4096]{1,0:T(8,128)(2,1)} %bitcast.14), custom_call_target="tpu_custom_call" | custom-call | flops 201326592 | bytes 12582912 | tf_op jit(solution)/shard_map/training_gradients/pallas_call | solution.py:261
  10.3 3.0 %collective-permute-start.5 = (bf16[64,1024]{1,0:T(8,128)(2,1)S(1)}, bf16[64,1024]{1,0:T(8,128)(2,1)S(1)}, u32[]{:S(2)}, u32[]{:S(2)}) collective-permute-start(bf16[64,1024]{1,0:T(8,128)(2,1)S(1)} %get-tuple-element.15.refs_0_), channel_id=1, source_target_pairs={{0,8},{4,12},{8,0},{12,4},{1,9},{5,13},{9,1},{13,5},{2,10},{6,14},... | collective-permute-start | bytes 393224 | tf_op jit(solution)/shard_map/ppermute | solution.py:32
  13.3 1.3 %collective-permute-start.6 = (bf16[64,1024]{1,0:T(8,128)(2,1)S(1)}, bf16[64,1024]{1,0:T(8,128)(2,1)S(1)}, u32[]{:S(2)}, u32[]{:S(2)}) collective-permute-start(bf16[64,1024]{1,0:T(8,128)(2,1)S(1)} %get-tuple-element.16.source), channel_id=1, source_target_pairs={{0,12},{4,8},{8,4},{12,0},{1,13},{5,9},{9,5},{13,1},{2,14},{6,10},... | collective-permute-start | bytes 393224 | tf_op jit(solution)/shard_map/ppermute | solution.py:32
  14.7 0.0 collective-permute-done.refs_1_
  14.7 6.7 %collective-permute-done.1.refs_2_ = bf16[64,2176]{1,0:T(8,128)(2,1)S(1)} collective-permute-done((bf16[64,2176]{1,0:T(8,128)(2,1)S(1)}, bf16[64,2176]{1,0:T(8,128)(2,1)S(1)}, u32[]{:S(2)}, u32[]{:S(2)}) %collective-permute-start.1) | collective-permute-done | bytes 278560 | tf_op jit(solution)/shard_map/ppermute | solution.py:259
  21.4 0.0 collective-permute-done.2.refs_3_
  21.4 0.2 token_stack.1._.refs_0_
  21.7 0.1 collective-permute-start.3
  21.8 0.3 collective-permute-start.4
  22.0 0.0 collective-permute-done.5.refs_0_
  22.0 3.4 %collective-permute-done.6.refs_1_ = bf16[64,1024]{1,0:T(8,128)(2,1)S(1)} collective-permute-done((bf16[64,1024]{1,0:T(8,128)(2,1)S(1)}, bf16[64,1024]{1,0:T(8,128)(2,1)S(1)}, u32[]{:S(2)}, u32[]{:S(2)}) %collective-permute-start.6) | collective-permute-done | bytes 131104 | tf_op jit(solution)/shard_map/ppermute | solution.py:32
  25.5 0.0 collective-permute-done.3.refs_1_
  25.5 0.9 %far_scores.1 = f32[2,4,8]{2,1,0:T(4,128)S(1)} custom-call(bf16[560,1024]{1,0:T(8,128)(2,1)S(1)} %token_stack.1._.refs_0_, bf16[560,1024]{1,0:T(8,128)(2,1)S(1)} %collective-permute-done.3.refs_1_, bf16[128,1024]{1,0:T(8,128)(2,1)S(1)} %far_gradients.1.refs_2_), custom_call_target="tpu_custom_call" | custom-call | bytes 573440 | tf_op jit(solution)/shard_map/far_scores/pallas_call | solution.py:287
  26.4 1.8 %collective-permute-start.7 = (f32[2,4,8]{2,1,0:T(4,128)S(1)}, f32[2,4,8]{2,1,0:T(4,128)S(1)}, u32[]{:S(2)}, u32[]{:S(2)}) collective-permute-start(f32[2,4,8]{2,1,0:T(4,128)S(1)} %far_scores.1), channel_id=1, source_target_pairs={{0,8},{4,12},{8,0},{12,4},{1,9},{5,13},{9,1},{13,5},{2,10},{6,14},... | collective-permute-start | bytes 776 | tf_op jit(solution)/shard_map/ppermute | solution.py:32
  28.2 0.0 collective-permute-done.4.refs_1_
  28.2 0.9 %near_scores.1 = f32[2,4,8]{2,1,0:T(4,128)S(1)} custom-call(bf16[560,1024]{1,0:T(8,128)(2,1)S(1)} %token_stack.1._.refs_0_, bf16[560,1024]{1,0:T(8,128)(2,1)S(1)} %collective-permute-done.3.refs_1_, bf16[128,1024]{1,0:T(8,128)(2,1)S(1)} %near_gradients.1.refs_2_), custom_call_target="tpu_custom_call" | custom-call | bytes 573440 | tf_op jit(solution)/shard_map/near_scores/pallas_call | solution.py:287
  29.2 1.8 %collective-permute-done.7 = f32[2,4,8]{2,1,0:T(4,128)S(1)} collective-permute-done((f32[2,4,8]{2,1,0:T(4,128)S(1)}, f32[2,4,8]{2,1,0:T(4,128)S(1)}, u32[]{:S(2)}, u32[]{:S(2)}) %collective-permute-start.7) | collective-permute-done | bytes 288 | tf_op jit(solution)/shard_map/ppermute | solution.py:32
  30.9 1.5 %collective-permute-start.8 = (f32[1,4,8]{2,1,0:T(4,128)S(1)}, f32[1,4,8]{2,1,0:T(4,128)S(1)}, u32[]{:S(2)}, u32[]{:S(2)}) collective-permute-start(f32[1,4,8]{2,1,0:T(4,128)S(1)} %slice.25), channel_id=1, source_target_pairs={{0,2},{2,0},{1,3},{3,1},{4,6},{6,4},{5,7},{7,5},{8,10},{10,8},{9,1... | collective-permute-start | bytes 392 | tf_op jit(solution)/shard_map/ppermute | solution.py:32
  32.5 2.0 %collective-permute-done.8 = f32[1,4,8]{2,1,0:T(4,128)S(1)} collective-permute-done((f32[1,4,8]{2,1,0:T(4,128)S(1)}, f32[1,4,8]{2,1,0:T(4,128)S(1)}, u32[]{:S(2)}, u32[]{:S(2)}) %collective-permute-start.8) | collective-permute-done | bytes 160 | tf_op jit(solution)/shard_map/ppermute | solution.py:32
  34.5 1.5 %collective-permute-start.9 = (f32[2,8]{1,0:T(2,128)S(1)}, f32[2,8]{1,0:T(2,128)S(1)}, u32[]{:S(2)}, u32[]{:S(2)}) collective-permute-start(f32[2,8]{1,0:T(2,128)S(1)} %slice_bitcast_fusion), channel_id=1, source_target_pairs={{0,4},{4,0},{8,12},{12,8},{1,5},{5,1},{9,13},{13,9},{2,6},{6,2},{1... | collective-permute-start | bytes 200 | tf_op jit(solution)/shard_map/ppermute | solution.py:32
  36.0 2.1 %collective-permute-done.9 = f32[2,8]{1,0:T(2,128)S(1)} collective-permute-done((f32[2,8]{1,0:T(2,128)S(1)}, f32[2,8]{1,0:T(2,128)S(1)}, u32[]{:S(2)}, u32[]{:S(2)}) %collective-permute-start.9) | collective-permute-done | bytes 96 | tf_op jit(solution)/shard_map/ppermute | solution.py:32
  38.1 0.6 %fusion = f32[8,2]{0,1:T(2,128)} fusion(f32[2,8]{1,0:T(2,128)S(1)} %collective-permute-done.9, f32[1,4,8]{2,1,0:T(4,128)S(1)} %slice_add_fusion), kind=kLoop, calls=%fused_computation.2 | loop fusion | flops 16 | bytes 192 | tf_op jit(solution)/shard_map/transpose | solution.py:345
  (7 shorter events, 0.1 us)
Async XLA Ops:
  1.8 12.9 %collective-permute-start = (bf16[64,2176]{1,0:T(8,128)(2,1)S(1)}, bf16[64,2176]{1,0:T(8,128)(2,1)S(1)}, u32[]{:S(2)}, u32[]{:S(2)}) collective-permute-start(bf16[64,2176]{1,0:T(8,128)(2,1)S(1)} %get-tuple-element.12), channel_id=1, source_target_pairs={{0,4},{2,6},{4,0},{6,2},{8,12},{10,14},{12,8},{14,10},{1,5},{3,7},... | collective-permute-start | bytes 835592 | tf_op jit(solution)/shard_map/ppermute | solution.py:259
  4.9 16.5 %collective-permute-start.1 = (bf16[64,2176]{1,0:T(8,128)(2,1)S(1)}, bf16[64,2176]{1,0:T(8,128)(2,1)S(1)}, u32[]{:S(2)}, u32[]{:S(2)}) collective-permute-start(bf16[64,2176]{1,0:T(8,128)(2,1)S(1)} %get-tuple-element.13), channel_id=1, source_target_pairs={{0,6},{2,4},{4,2},{6,0},{8,14},{10,12},{12,10},{14,8},{1,7},{3,5},... | collective-permute-start | bytes 835592 | tf_op jit(solution)/shard_map/ppermute | solution.py:259
  6.3 15.2 %collective-permute-start.2 = (bf16[64,2176]{1,0:T(8,128)(2,1)S(1)}, bf16[64,2176]{1,0:T(8,128)(2,1)S(1)}, u32[]{:S(2)}, u32[]{:S(2)}) collective-permute-start(bf16[64,2176]{1,0:T(8,128)(2,1)S(1)} %get-tuple-element.14), channel_id=1, source_target_pairs={{0,2},{2,0},{4,6},{6,4},{8,10},{10,8},{12,14},{14,12},{1,3},{3,1},... | collective-permute-start | bytes 835592 | tf_op jit(solution)/shard_map/ppermute | solution.py:259
  10.3 11.7 %collective-permute-start.5 = (bf16[64,1024]{1,0:T(8,128)(2,1)S(1)}, bf16[64,1024]{1,0:T(8,128)(2,1)S(1)}, u32[]{:S(2)}, u32[]{:S(2)}) collective-permute-start(bf16[64,1024]{1,0:T(8,128)(2,1)S(1)} %get-tuple-element.15.refs_0_), channel_id=1, source_target_pairs={{0,8},{4,12},{8,0},{12,4},{1,9},{5,13},{9,1},{13,5},{2,10},{6,14},... | collective-permute-start | bytes 393224 | tf_op jit(solution)/shard_map/ppermute | solution.py:32
  13.3 12.1 %collective-permute-start.6 = (bf16[64,1024]{1,0:T(8,128)(2,1)S(1)}, bf16[64,1024]{1,0:T(8,128)(2,1)S(1)}, u32[]{:S(2)}, u32[]{:S(2)}) collective-permute-start(bf16[64,1024]{1,0:T(8,128)(2,1)S(1)} %get-tuple-element.16.source), channel_id=1, source_target_pairs={{0,12},{4,8},{8,4},{12,0},{1,13},{5,9},{9,5},{13,1},{2,14},{6,10},... | collective-permute-start | bytes 393224 | tf_op jit(solution)/shard_map/ppermute | solution.py:32
  21.7 3.8 %collective-permute-start.3 = (bf16[560,1024]{1,0:T(8,128)(2,1)S(1)}, bf16[560,1024]{1,0:T(8,128)(2,1)S(1)}, u32[]{:S(2)}, u32[]{:S(2)}) collective-permute-start(bf16[560,1024]{1,0:T(8,128)(2,1)S(1)} %token_stack.1._.refs_0_), channel_id=1, source_target_pairs={{0,1},{1,0},{2,3},{3,2},{4,5},{5,4},{6,7},{7,6},{8,9},{9,8},{10,11... | collective-permute-start | bytes 3440648 | tf_op jit(solution)/shard_map/ppermute | solution.py:32
  21.8 6.5 %collective-permute-start.4 = (bf16[64,1024]{1,0:T(8,128)(2,1)S(1)}, bf16[64,1024]{1,0:T(8,128)(2,1)S(1)}, u32[]{:S(2)}, u32[]{:S(2)}) collective-permute-start(bf16[64,1024]{1,0:T(8,128)(2,1)S(1)} %near_gradient.1), channel_id=1, source_target_pairs={{0,4},{4,0},{8,12},{12,8},{1,5},{5,1},{9,13},{13,9},{2,6},{6,2},{1... | collective-permute-start | bytes 393224 | tf_op jit(solution)/shard_map/ppermute | solution.py:32
  26.4 4.5 %collective-permute-start.7 = (f32[2,4,8]{2,1,0:T(4,128)S(1)}, f32[2,4,8]{2,1,0:T(4,128)S(1)}, u32[]{:S(2)}, u32[]{:S(2)}) collective-permute-start(f32[2,4,8]{2,1,0:T(4,128)S(1)} %far_scores.1), channel_id=1, source_target_pairs={{0,8},{4,12},{8,0},{12,4},{1,9},{5,13},{9,1},{13,5},{2,10},{6,14},... | collective-permute-start | bytes 776 | tf_op jit(solution)/shard_map/ppermute | solution.py:32
  30.9 3.6 %collective-permute-start.8 = (f32[1,4,8]{2,1,0:T(4,128)S(1)}, f32[1,4,8]{2,1,0:T(4,128)S(1)}, u32[]{:S(2)}, u32[]{:S(2)}) collective-permute-start(f32[1,4,8]{2,1,0:T(4,128)S(1)} %slice.25), channel_id=1, source_target_pairs={{0,2},{2,0},{1,3},{3,1},{4,6},{6,4},{5,7},{7,5},{8,10},{10,8},{9,1... | collective-permute-start | bytes 392 | tf_op jit(solution)/shard_map/ppermute | solution.py:32
  34.5 3.6 %collective-permute-start.9 = (f32[2,8]{1,0:T(2,128)S(1)}, f32[2,8]{1,0:T(2,128)S(1)}, u32[]{:S(2)}, u32[]{:S(2)}) collective-permute-start(f32[2,8]{1,0:T(2,128)S(1)} %slice_bitcast_fusion), channel_id=1, source_target_pairs={{0,4},{4,0},{8,12},{12,8},{1,5},{5,1},{9,13},{13,9},{2,6},{6,2},{1... | collective-permute-start | bytes 200 | tf_op jit(solution)/shard_map/ppermute | solution.py:32

commit v5 on v4

--- a/solution.py
+++ b/solution.py
@@ -177,6 +177,10 @@
         out[start : start + half, :] = block[half:, :]
 
 
+def move_kernel(source, target):
+    target[...] = source[...]
+
+
 def copy_kernel(source, _, target):
     target[...] = source[...]
 
@@ -330,19 +334,42 @@
 
     far_scores = partial(far, "far_scores")
     near_scores = partial(near, "near_scores")
+    def crossing(value, distance):
+        pairs = [
+            (i * npair + k, (i ^ distance) * npair + (k ^ 1))
+            for i in range(ndp)
+            for k in range(npair)
+        ]
+        return lax.ppermute(value, ("dp", "pair"), pairs)
+
+    near_count = 2 * sequences
     distance = ndp // 2
+    kept = (distance - 2) * sequences
+    received = crossing(far_scores[:, kept:], distance)
+    received = call(
+        move_kernel,
+        (received.shape, received.dtype),
+        received,
+        name="received_scores",
+        flops=FAR_COST * stack.size,
+    )
+    near_scores = swap(near_scores, "pair", 1) + received[:, :near_count]
+    if kept:
+        far_scores = swap(far_scores[:, :kept], "pair", 1) + received[:, near_count:]
+    distance //= 2
     while distance > 1:
         kept = (distance - 2) * sequences
         received = swap(far_scores[:, kept:], "dp", distance)
-        near_scores += received[:, : 2 * sequences]
-        far_scores = far_scores[:, :kept] + received[:, 2 * sequences :]
+        near_scores += received[:, :near_count]
+        far_scores = far_scores[:, :kept] + received[:, near_count:]
         distance //= 2
     distance = nsub // 2
     while distance:
         near_scores = near_scores[:distance] + swap(near_scores[distance:], "sub", distance)
         distance //= 2
     scores = near_scores[0]
-    return (scores[:sequences] + swap(scores[sequences:], "dp", 1)).T
+    other = crossing(scores[sequences:], 1)
+    return (swap(scores[:sequences], "pair", 1) + other).T
 
 
 def solution(mesh):

time: 38.8 us -> 38 us (0.979)
  waiting for transfers between devices: 16 us -> 14.3 us
  starting transfers between devices: 14.2 us -> 15 us
    ppermute x7, waiting for transfers between devices: 9.3 us -> 5.97 us  [swap(): lax.ppermute(value, axis, [(source, source ^ distance) for source in rang...]
    ppermute x0 -> x2, starting transfers between devices: none -> 2.59 us  [crossing(): return lax.ppermute(value, ('dp', 'pair'), pairs)]
    ppermute x7, starting transfers between devices: 9.56 us -> 7.81 us  [swap(): lax.ppermute(value, axis, [(source, source ^ distance) for source in rang...]
    ppermute x0 -> x2, waiting for transfers between devices: none -> 1.64 us  [crossing(): return lax.ppermute(value, ('dp', 'pair'), pairs)]
    pallas_call x6 -> x7, Pallas kernels: 2.11 us -> 2.11 us  [call(): pl.pallas_call(kernel, out_shape=jax.ShapeDtypeStruct(*shape), in_specs=[...]
  transfers between devices with their start and end apart: 10 -> 12, of which waited for: 5 -> 7; matrix products, arithmetic and copies ran while one was open for 0% -> 0% of each run, Pallas kernels for 15% -> 16%
where the time goes in v5:
time: 38 us; the launch traced here: 37.8 us
  starting transfers between devices  15 us (39%)
  waiting for transfers between devices  14.3 us (38%)
  Pallas kernels  7.79 us (20%)
  other arithmetic  0.57 us (1%)
    ppermute x7, starting transfers between devices, swap(): lax.ppermute(value, axis, [(source, source ^ distance) for source in rang...  7.81 us
    ppermute x3, waiting for transfers between devices, per_device(): blocks.append(lax.ppermute(shares[place], ('dp', 'sub'), pairs))  6.74 us
    ppermute x7, waiting for transfers between devices, swap(): lax.ppermute(value, axis, [(source, source ^ distance) for source in rang...  5.97 us
    ppermute x3, starting transfers between devices, per_device(): blocks.append(lax.ppermute(shares[place], ('dp', 'sub'), pairs))  4.63 us
    pallas_call x1, Pallas kernels, per_device(): pl.pallas_call(functools.partial(training_kernel, nlo, nsub), out_shape=[...  3.87 us
    ppermute x2, starting transfers between devices, crossing(): return lax.ppermute(value, ('dp', 'pair'), pairs)  2.59 us
    pallas_call x7, Pallas kernels, call(): pl.pallas_call(kernel, out_shape=jax.ShapeDtypeStruct(*shape), in_specs=[...  2.11 us
    pallas_call x1, Pallas kernels, per_device(): pl.pallas_call(functools.partial(query_kernel, nlo, nsub), out_shape=[jax...  1.8 us
  transfers between devices with their start and end apart: 12, of which 7 were waited for; matrix products, arithmetic and copies ran while one was open for 0% of the time, Pallas kernels for 16%

profile of v5, /device:TPU:0, one launch (start us, length us, event | category | flops | bytes accessed | tf_op | source)
XLA Modules:
  0.0 37.8 jit_solution(13006001121579468768)
XLA Ops:
  0.0 1.8 %query_shares.1 = (bf16[64,2176]{1,0:T(8,128)(2,1)S(1)}, bf16[64,2176]{1,0:T(8,128)(2,1)S(1)}, bf16[64,2176]{1,0:T(8,128)(2,1)S(1)}, bf16[64,2176]{1,0:T(8,128)(2,1)S(1)}) custom-call(bf16[64,4096]{1,0:T(8,128)(2,1)} %inputs.2, bf16[64,4096]{1,0:T(8,128)(2,1)} %gradient.2, s32[1,64]{1,0:T(1,128)} %bitcast.13, bf16[16,4096]{1,0:T(8,128)(2,1)} %bitcast.9, ...), custom_call_target="tpu_custom_call" | custom-call | tf_op jit(solution)/shard_map/query_shares/pallas_call | solution.py:241
  1.8 3.1 %collective-permute-start = (bf16[64,2176]{1,0:T(8,128)(2,1)S(1)}, bf16[64,2176]{1,0:T(8,128)(2,1)S(1)}, u32[]{:S(2)}, u32[]{:S(2)}) collective-permute-start(bf16[64,2176]{1,0:T(8,128)(2,1)S(1)} %get-tuple-element.12), channel_id=1, source_target_pairs={{0,4},{2,6},{4,0},{6,2},{8,12},{10,14},{12,8},{14,10},{1,5},{3,7},... | collective-permute-start | bytes 835592 | tf_op jit(solution)/shard_map/ppermute | solution.py:263
  4.9 1.4 %collective-permute-start.1 = (bf16[64,2176]{1,0:T(8,128)(2,1)S(1)}, bf16[64,2176]{1,0:T(8,128)(2,1)S(1)}, u32[]{:S(2)}, u32[]{:S(2)}) collective-permute-start(bf16[64,2176]{1,0:T(8,128)(2,1)S(1)} %get-tuple-element.13), channel_id=1, source_target_pairs={{0,6},{2,4},{4,2},{6,0},{8,14},{10,12},{12,10},{14,8},{1,7},{3,5},... | collective-permute-start | bytes 835592 | tf_op jit(solution)/shard_map/ppermute | solution.py:263
  6.3 0.2 collective-permute-start.2
  6.4 3.9 %training_gradients.1 = (bf16[64,1024]{1,0:T(8,128)(2,1)S(1)}, bf16[64,1024]{1,0:T(8,128)(2,1)S(1)}) custom-call(s32[2]{0:T(128)} %length_source.1, bf16[2,128,4096]{2,1,0:T(8,128)(2,1)} %inputs.3, bf16[2,128,4096]{2,1,0:T(8,128)(2,1)} %gradient.3, bf16[16,4096]{1,0:T(8,128)(2,1)} %bitcast.10, bf16[16,4096]{1,0:T(8,128)(2,1)} %bitcast.12), custom_call_target="tpu_custom_call" | custom-call | flops 201326592 | bytes 12582912 | tf_op jit(solution)/shard_map/training_gradients/pallas_call | solution.py:265
  10.3 3.0 %collective-permute-start.6 = (bf16[64,1024]{1,0:T(8,128)(2,1)S(1)}, bf16[64,1024]{1,0:T(8,128)(2,1)S(1)}, u32[]{:S(2)}, u32[]{:S(2)}) collective-permute-start(bf16[64,1024]{1,0:T(8,128)(2,1)S(1)} %get-tuple-element.15.refs_0_), channel_id=1, source_target_pairs={{0,8},{4,12},{8,0},{12,4},{1,9},{5,13},{9,1},{13,5},{2,10},{6,14},... | collective-permute-start | bytes 393224 | tf_op jit(solution)/shard_map/ppermute | solution.py:32
  13.3 1.3 %collective-permute-start.7 = (bf16[64,1024]{1,0:T(8,128)(2,1)S(1)}, bf16[64,1024]{1,0:T(8,128)(2,1)S(1)}, u32[]{:S(2)}, u32[]{:S(2)}) collective-permute-start(bf16[64,1024]{1,0:T(8,128)(2,1)S(1)} %get-tuple-element.16.source), channel_id=1, source_target_pairs={{0,12},{4,8},{8,4},{12,0},{1,13},{5,9},{9,5},{13,1},{2,14},{6,10},... | collective-permute-start | bytes 393224 | tf_op jit(solution)/shard_map/ppermute | solution.py:32
  14.7 0.0 collective-permute-done.refs_1_
  14.7 6.7 %collective-permute-done.1.refs_2_ = bf16[64,2176]{1,0:T(8,128)(2,1)S(1)} collective-permute-done((bf16[64,2176]{1,0:T(8,128)(2,1)S(1)}, bf16[64,2176]{1,0:T(8,128)(2,1)S(1)}, u32[]{:S(2)}, u32[]{:S(2)}) %collective-permute-start.1) | collective-permute-done | bytes 278560 | tf_op jit(solution)/shard_map/ppermute | solution.py:263
  21.4 0.0 collective-permute-done.2.refs_3_
  21.4 0.2 token_stack.1._.refs_0_
  21.7 0.1 collective-permute-start.3
  21.8 0.3 collective-permute-start.4
  22.0 0.0 collective-permute-done.6.refs_0_
  22.0 3.4 %collective-permute-done.7.refs_1_ = bf16[64,1024]{1,0:T(8,128)(2,1)S(1)} collective-permute-done((bf16[64,1024]{1,0:T(8,128)(2,1)S(1)}, bf16[64,1024]{1,0:T(8,128)(2,1)S(1)}, u32[]{:S(2)}, u32[]{:S(2)}) %collective-permute-start.7) | collective-permute-done | bytes 131104 | tf_op jit(solution)/shard_map/ppermute | solution.py:32
  25.5 0.0 collective-permute-done.3.refs_1_
  25.5 0.9 %far_scores.1 = f32[2,4,8]{2,1,0:T(4,128)S(1)} custom-call(bf16[560,1024]{1,0:T(8,128)(2,1)S(1)} %token_stack.1._.refs_0_, bf16[560,1024]{1,0:T(8,128)(2,1)S(1)} %collective-permute-done.3.refs_1_, bf16[128,1024]{1,0:T(8,128)(2,1)S(1)} %far_gradients.1.refs_2_), custom_call_target="tpu_custom_call" | custom-call | bytes 573440 | tf_op jit(solution)/shard_map/far_scores/pallas_call | solution.py:291
  26.4 1.5 %collective-permute-start.8 = (f32[2,4,8]{2,1,0:T(4,128)S(1)}, f32[2,4,8]{2,1,0:T(4,128)S(1)}, u32[]{:S(2)}, u32[]{:S(2)}) collective-permute-start(f32[2,4,8]{2,1,0:T(4,128)S(1)} %far_scores.1), channel_id=1, source_target_pairs={{0,9},{1,8},{4,13},{5,12},{8,1},{9,0},{12,5},{13,4},{2,11},{3,10},... | collective-permute-start | bytes 776 | tf_op jit(solution)/shard_map/ppermute | solution.py:343
  27.9 0.3 collective-permute-done.4.refs_1_
  28.2 0.9 %near_scores.1 = f32[2,4,8]{2,1,0:T(4,128)S(1)} custom-call(bf16[560,1024]{1,0:T(8,128)(2,1)S(1)} %token_stack.1._.refs_0_, bf16[560,1024]{1,0:T(8,128)(2,1)S(1)} %collective-permute-done.3.refs_1_, bf16[128,1024]{1,0:T(8,128)(2,1)S(1)} %near_gradients.1.refs_2_), custom_call_target="tpu_custom_call" | custom-call | bytes 573440 | tf_op jit(solution)/shard_map/near_scores/pallas_call | solution.py:291
  29.1 0.2 collective-permute-start.5
  29.3 1.1 %collective-permute-done.8.source = f32[2,4,8]{2,1,0:T(4,128)S(1)} collective-permute-done((f32[2,4,8]{2,1,0:T(4,128)S(1)}, f32[2,4,8]{2,1,0:T(4,128)S(1)}, u32[]{:S(2)}, u32[]{:S(2)}) %collective-permute-start.8) | collective-permute-done | bytes 288 | tf_op jit(solution)/shard_map/ppermute | solution.py:343
  30.3 0.0 collective-permute-done.5
  30.4 1.6 %collective-permute-start.9 = (f32[1,4,8]{2,1,0:T(4,128)S(1)}, f32[1,4,8]{2,1,0:T(4,128)S(1)}, u32[]{:S(2)}, u32[]{:S(2)}) collective-permute-start(f32[1,4,8]{2,1,0:T(4,128)S(1)} %slice.25), channel_id=1, source_target_pairs={{0,2},{2,0},{1,3},{3,1},{4,6},{6,4},{5,7},{7,5},{8,10},{10,8},{9,1... | collective-permute-start | bytes 392 | tf_op jit(solution)/shard_map/ppermute | solution.py:32
  32.0 2.0 %collective-permute-done.9 = f32[1,4,8]{2,1,0:T(4,128)S(1)} collective-permute-done((f32[1,4,8]{2,1,0:T(4,128)S(1)}, f32[1,4,8]{2,1,0:T(4,128)S(1)}, u32[]{:S(2)}, u32[]{:S(2)}) %collective-permute-start.9) | collective-permute-done | bytes 160 | tf_op jit(solution)/shard_map/ppermute | solution.py:32
  34.0 1.1 %collective-permute-start.11 = (f32[2,8]{1,0:T(2,128)S(1)}, f32[2,8]{1,0:T(2,128)S(1)}, u32[]{:S(2)}, u32[]{:S(2)}) collective-permute-start(f32[2,8]{1,0:T(2,128)S(1)} %get-tuple-element.17), channel_id=1, source_target_pairs={{0,5},{1,4},{4,1},{5,0},{8,13},{9,12},{12,9},{13,8},{2,7},{3,6},{6... | collective-permute-start | bytes 200 | tf_op jit(solution)/shard_map/ppermute | solution.py:343
  35.1 1.3 %collective-permute-start.10 = (f32[2,8]{1,0:T(2,128)S(1)}, f32[2,8]{1,0:T(2,128)S(1)}, u32[]{:S(2)}, u32[]{:S(2)}) collective-permute-start(f32[2,8]{1,0:T(2,128)S(1)} %get-tuple-element.18), channel_id=1, source_target_pairs={{0,1},{1,0},{2,3},{3,2},{4,5},{5,4},{6,7},{7,6},{8,9},{9,8},{10,11... | collective-permute-start | bytes 200 | tf_op jit(solution)/shard_map/ppermute | solution.py:32
  36.4 0.6 %collective-permute-done.11 = f32[2,8]{1,0:T(2,128)S(1)} collective-permute-done((f32[2,8]{1,0:T(2,128)S(1)}, f32[2,8]{1,0:T(2,128)S(1)}, u32[]{:S(2)}, u32[]{:S(2)}) %collective-permute-start.11) | collective-permute-done | bytes 96 | tf_op jit(solution)/shard_map/ppermute | solution.py:343
  37.0 0.2 collective-permute-done.10
  37.3 0.6 %add_bitcast_fusion = f32[8,2]{0,1:T(2,128)} fusion(f32[2,8]{1,0:T(2,128)S(1)} %collective-permute-done.10, f32[2,8]{1,0:T(2,128)S(1)} %collective-permute-done.11), kind=kLoop, calls=%fused_computation.1 | loop fusion | flops 16 | bytes 192 | tf_op jit(solution)/shard_map/transpose | solution.py:372
  (8 shorter events, 0.1 us)
Async XLA Ops:
  1.8 12.9 %collective-permute-start = (bf16[64,2176]{1,0:T(8,128)(2,1)S(1)}, bf16[64,2176]{1,0:T(8,128)(2,1)S(1)}, u32[]{:S(2)}, u32[]{:S(2)}) collective-permute-start(bf16[64,2176]{1,0:T(8,128)(2,1)S(1)} %get-tuple-element.12), channel_id=1, source_target_pairs={{0,4},{2,6},{4,0},{6,2},{8,12},{10,14},{12,8},{14,10},{1,5},{3,7},... | collective-permute-start | bytes 835592 | tf_op jit(solution)/shard_map/ppermute | solution.py:263
  4.9 16.5 %collective-permute-start.1 = (bf16[64,2176]{1,0:T(8,128)(2,1)S(1)}, bf16[64,2176]{1,0:T(8,128)(2,1)S(1)}, u32[]{:S(2)}, u32[]{:S(2)}) collective-permute-start(bf16[64,2176]{1,0:T(8,128)(2,1)S(1)} %get-tuple-element.13), channel_id=1, source_target_pairs={{0,6},{2,4},{4,2},{6,0},{8,14},{10,12},{12,10},{14,8},{1,7},{3,5},... | collective-permute-start | bytes 835592 | tf_op jit(solution)/shard_map/ppermute | solution.py:263
  6.3 15.2 %collective-permute-start.2 = (bf16[64,2176]{1,0:T(8,128)(2,1)S(1)}, bf16[64,2176]{1,0:T(8,128)(2,1)S(1)}, u32[]{:S(2)}, u32[]{:S(2)}) collective-permute-start(bf16[64,2176]{1,0:T(8,128)(2,1)S(1)} %get-tuple-element.14), channel_id=1, source_target_pairs={{0,2},{2,0},{4,6},{6,4},{8,10},{10,8},{12,14},{14,12},{1,3},{3,1},... | collective-permute-start | bytes 835592 | tf_op jit(solution)/shard_map/ppermute | solution.py:263
  10.3 11.7 %collective-permute-start.6 = (bf16[64,1024]{1,0:T(8,128)(2,1)S(1)}, bf16[64,1024]{1,0:T(8,128)(2,1)S(1)}, u32[]{:S(2)}, u32[]{:S(2)}) collective-permute-start(bf16[64,1024]{1,0:T(8,128)(2,1)S(1)} %get-tuple-element.15.refs_0_), channel_id=1, source_target_pairs={{0,8},{4,12},{8,0},{12,4},{1,9},{5,13},{9,1},{13,5},{2,10},{6,14},... | collective-permute-start | bytes 393224 | tf_op jit(solution)/shard_map/ppermute | solution.py:32
  13.3 12.1 %collective-permute-start.7 = (bf16[64,1024]{1,0:T(8,128)(2,1)S(1)}, bf16[64,1024]{1,0:T(8,128)(2,1)S(1)}, u32[]{:S(2)}, u32[]{:S(2)}) collective-permute-start(bf16[64,1024]{1,0:T(8,128)(2,1)S(1)} %get-tuple-element.16.source), channel_id=1, source_target_pairs={{0,12},{4,8},{8,4},{12,0},{1,13},{5,9},{9,5},{13,1},{2,14},{6,10},... | collective-permute-start | bytes 393224 | tf_op jit(solution)/shard_map/ppermute | solution.py:32
  21.7 3.8 %collective-permute-start.3 = (bf16[560,1024]{1,0:T(8,128)(2,1)S(1)}, bf16[560,1024]{1,0:T(8,128)(2,1)S(1)}, u32[]{:S(2)}, u32[]{:S(2)}) collective-permute-start(bf16[560,1024]{1,0:T(8,128)(2,1)S(1)} %token_stack.1._.refs_0_), channel_id=1, source_target_pairs={{0,1},{1,0},{2,3},{3,2},{4,5},{5,4},{6,7},{7,6},{8,9},{9,8},{10,11... | collective-permute-start | bytes 3440648 | tf_op jit(solution)/shard_map/ppermute | solution.py:32
  21.8 6.4 %collective-permute-start.4 = (bf16[64,1024]{1,0:T(8,128)(2,1)S(1)}, bf16[64,1024]{1,0:T(8,128)(2,1)S(1)}, u32[]{:S(2)}, u32[]{:S(2)}) collective-permute-start(bf16[64,1024]{1,0:T(8,128)(2,1)S(1)} %near_gradient.1), channel_id=1, source_target_pairs={{0,4},{4,0},{8,12},{12,8},{1,5},{5,1},{9,13},{13,9},{2,6},{6,2},{1... | collective-permute-start | bytes 393224 | tf_op jit(solution)/shard_map/ppermute | solution.py:32
  26.4 3.9 %collective-permute-start.8 = (f32[2,4,8]{2,1,0:T(4,128)S(1)}, f32[2,4,8]{2,1,0:T(4,128)S(1)}, u32[]{:S(2)}, u32[]{:S(2)}) collective-permute-start(f32[2,4,8]{2,1,0:T(4,128)S(1)} %far_scores.1), channel_id=1, source_target_pairs={{0,9},{1,8},{4,13},{5,12},{8,1},{9,0},{12,5},{13,4},{2,11},{3,10},... | collective-permute-start | bytes 776 | tf_op jit(solution)/shard_map/ppermute | solution.py:343
  29.1 1.2 %collective-permute-start.5 = (f32[2,4,8]{2,1,0:T(4,128)S(1)}, f32[2,4,8]{2,1,0:T(4,128)S(1)}, u32[]{:S(2)}, u32[]{:S(2)}) collective-permute-start(f32[2,4,8]{2,1,0:T(4,128)S(1)} %near_scores.1), channel_id=1, source_target_pairs={{0,1},{1,0},{2,3},{3,2},{4,5},{5,4},{6,7},{7,6},{8,9},{9,8},{10,11... | collective-permute-start | bytes 776 | tf_op jit(solution)/shard_map/ppermute | solution.py:32
  30.4 3.7 %collective-permute-start.9 = (f32[1,4,8]{2,1,0:T(4,128)S(1)}, f32[1,4,8]{2,1,0:T(4,128)S(1)}, u32[]{:S(2)}, u32[]{:S(2)}) collective-permute-start(f32[1,4,8]{2,1,0:T(4,128)S(1)} %slice.25), channel_id=1, source_target_pairs={{0,2},{2,0},{1,3},{3,1},{4,6},{6,4},{5,7},{7,5},{8,10},{10,8},{9,1... | collective-permute-start | bytes 392 | tf_op jit(solution)/shard_map/ppermute | solution.py:32
  34.0 3.0 %collective-permute-start.11 = (f32[2,8]{1,0:T(2,128)S(1)}, f32[2,8]{1,0:T(2,128)S(1)}, u32[]{:S(2)}, u32[]{:S(2)}) collective-permute-start(f32[2,8]{1,0:T(2,128)S(1)} %get-tuple-element.17), channel_id=1, source_target_pairs={{0,5},{1,4},{4,1},{5,0},{8,13},{9,12},{12,9},{13,8},{2,7},{3,6},{6... | collective-permute-start | bytes 200 | tf_op jit(solution)/shard_map/ppermute | solution.py:343
  35.1 2.1 %collective-permute-start.10 = (f32[2,8]{1,0:T(2,128)S(1)}, f32[2,8]{1,0:T(2,128)S(1)}, u32[]{:S(2)}, u32[]{:S(2)}) collective-permute-start(f32[2,8]{1,0:T(2,128)S(1)} %get-tuple-element.18), channel_id=1, source_target_pairs={{0,1},{1,0},{2,3},{3,2},{4,5},{5,4},{6,7},{7,6},{8,9},{9,8},{10,11... | collective-permute-start | bytes 200 | tf_op jit(solution)/shard_map/ppermute | solution.py:32

commit v6 on v4

--- a/solution.py
+++ b/solution.py
@@ -234,6 +234,14 @@
     down, up = adapter_down_map.T, adapter_up_map.T
     params = pltpu.CompilerParams(vmem_limit_bytes=LIMIT)
 
+    def crossing(value, axis, distance):
+        pairs = [
+            (i * npair + k, (i ^ distance) * npair + (k ^ 1))
+            for i in range(lax.axis_size(axis))
+            for k in range(npair)
+        ]
+        return lax.ppermute(value, (axis, "pair"), pairs)
+
     shares = pl.pallas_call(
         functools.partial(query_kernel, nlo, nsub),
         out_shape=[jax.ShapeDtypeStruct((tokens, 2 * width + EXTRA), jnp.bfloat16)] * (nlo * nsub),
@@ -253,10 +261,14 @@
     blocks = [shares[0]]
     for place in sorted(range(1, nlo * nsub), key=lambda place: place < nsub):
         dlo, dsub = place // nsub, place % nsub
-        pairs = [
-            (i * nsub + j, (i ^ dlo) * nsub + (j ^ dsub)) for i in range(ndp) for j in range(nsub)
-        ]
-        blocks.append(lax.ppermute(shares[place], ("dp", "sub"), pairs))
+        flip = dlo & (dsub > 0)
+        pairs = []
+        for i in range(ndp):
+            for j in range(nsub):
+                for k in range(npair):
+                    target = ((i ^ dlo) * nsub + (j ^ dsub)) * npair + (k ^ flip)
+                    pairs.append(((i * nsub + j) * npair + k, target))
+        blocks.append(lax.ppermute(shares[place], ("dp", "sub", "pair"), pairs))
 
     grads = pl.pallas_call(
         functools.partial(training_kernel, nlo, nsub),
@@ -297,7 +309,7 @@
         )(*operands)
 
     stack = call(stack_kernel, ((rows, width), jnp.bfloat16), *blocks, name="token_stack")
-    far = [swap(grads[distance % nlo], "dp", distance) for distance in range(2, ndp)]
+    far = [crossing(grads[distance % nlo], "dp", distance) for distance in range(2, ndp)]
     owned = count // nsub
     per = grads[0].shape[0]
 
@@ -330,19 +342,28 @@
 
     far_scores = partial(far, "far_scores")
     near_scores = partial(near, "near_scores")
+    near_count = 2 * sequences
     distance = ndp // 2
+    kept = (distance - 2) * sequences
+    received = crossing(far_scores[:, kept:], "dp", distance)
+    near_scores += received[:, :near_count]
+    if kept:
+        far_scores = swap(far_scores[:, :kept], "pair", 1) + received[:, near_count:]
+    distance //= 2
     while distance > 1:
         kept = (distance - 2) * sequences
         received = swap(far_scores[:, kept:], "dp", distance)
-        near_scores += received[:, : 2 * sequences]
-        far_scores = far_scores[:, :kept] + received[:, 2 * sequences :]
+        near_scores += received[:, :near_count]
+        far_scores = far_scores[:, :kept] + received[:, near_count:]
         distance //= 2
     distance = nsub // 2
-    while distance:
+    while distance > 1:
         near_scores = near_scores[:distance] + swap(near_scores[distance:], "sub", distance)
         distance //= 2
+    near_scores = swap(near_scores[:1], "pair", 1) + crossing(near_scores[1:], "sub", 1)
     scores = near_scores[0]
-    return (scores[:sequences] + swap(scores[sequences:], "dp", 1)).T
+    other = crossing(scores[sequences:], "dp", 1)
+    return (swap(scores[:sequences], "pair", 1) + other).T
 
 
 def solution(mesh):

time: 38.8 us -> 36.7 us (0.946)
  waiting for transfers between devices: 16 us -> 10.4 us
  starting transfers between devices: 14.2 us -> 17.4 us
    ppermute x3 -> x8, starting transfers between devices: 4.63 us -> 14.6 us  [the longest x5 10 us: crossing(): return lax.ppermute(value, (axis, 'pair'), pairs)]
    ppermute x7 -> x4, waiting for transfers between devices: 9.3 us -> 0.11 us  [swap(): lax.ppermute(value, axis, [(source, source ^ distance) for source in rang...]
    ppermute x7 -> x4, starting transfers between devices: 9.56 us -> 2.82 us  [swap(): lax.ppermute(value, axis, [(source, source ^ distance) for source in rang...]
    ppermute x3 -> x8, waiting for transfers between devices: 6.74 us -> 10.3 us  [the longest x3 6.45 us: per_device(): blocks.append(lax.ppermute(shares[place], ('dp', 'sub', 'pair'), pairs))]
  transfers between devices with their start and end apart: 10 -> 12, of which waited for: 5 -> 6; matrix products, arithmetic and copies ran while one was open for 0% -> 0% of each run, Pallas kernels for 15% -> 16%
where the time goes in v6:
time: 36.7 us; the launch traced here: 36.3 us
  starting transfers between devices  17.4 us (47%)
  waiting for transfers between devices  10.4 us (28%)
  Pallas kernels  7.78 us (21%)
  other arithmetic  0.57 us (2%)
    ppermute x5, starting transfers between devices, crossing(): return lax.ppermute(value, (axis, 'pair'), pairs)  10 us
    ppermute x3, waiting for transfers between devices, per_device(): blocks.append(lax.ppermute(shares[place], ('dp', 'sub', 'pair'), pairs))  6.45 us
    ppermute x3, starting transfers between devices, per_device(): blocks.append(lax.ppermute(shares[place], ('dp', 'sub', 'pair'), pairs))  4.58 us
    ppermute x5, waiting for transfers between devices, crossing(): return lax.ppermute(value, (axis, 'pair'), pairs)  3.88 us
    pallas_call x1, Pallas kernels, per_device(): pl.pallas_call(functools.partial(training_kernel, nlo, nsub), out_shape=[...  3.87 us
    ppermute x4, starting transfers between devices, swap(): lax.ppermute(value, axis, [(source, source ^ distance) for source in rang...  2.82 us
    pallas_call x6, Pallas kernels, call(): pl.pallas_call(kernel, out_shape=jax.ShapeDtypeStruct(*shape), in_specs=[...  2.11 us
    pallas_call x1, Pallas kernels, per_device(): pl.pallas_call(functools.partial(query_kernel, nlo, nsub), out_shape=[jax...  1.8 us
  transfers between devices with their start and end apart: 12, of which 6 were waited for; matrix products, arithmetic and copies ran while one was open for 0% of the time, Pallas kernels for 16%

profile of v6, /device:TPU:0, one launch (start us, length us, event | category | flops | bytes accessed | tf_op | source)
XLA Modules:
  0.0 36.3 jit_solution(15218194223019995166)
XLA Ops:
  0.0 1.8 %query_shares.1 = (bf16[64,2176]{1,0:T(8,128)(2,1)S(1)}, bf16[64,2176]{1,0:T(8,128)(2,1)S(1)}, bf16[64,2176]{1,0:T(8,128)(2,1)S(1)}, bf16[64,2176]{1,0:T(8,128)(2,1)S(1)}) custom-call(bf16[64,4096]{1,0:T(8,128)(2,1)} %inputs.2, bf16[64,4096]{1,0:T(8,128)(2,1)} %gradient.2, s32[1,64]{1,0:T(1,128)} %bitcast.13, bf16[16,4096]{1,0:T(8,128)(2,1)} %bitcast.9, ...), custom_call_target="tpu_custom_call" | custom-call | tf_op jit(solution)/shard_map/query_shares/pallas_call | solution.py:245
  1.8 3.1 %collective-permute-start = (bf16[64,2176]{1,0:T(8,128)(2,1)S(1)}, bf16[64,2176]{1,0:T(8,128)(2,1)S(1)}, u32[]{:S(2)}, u32[]{:S(2)}) collective-permute-start(bf16[64,2176]{1,0:T(8,128)(2,1)S(1)} %get-tuple-element.12), channel_id=1, source_target_pairs={{0,4},{1,5},{2,6},{3,7},{4,0},{5,1},{6,2},{7,3},{8,12},{9,13},{10,... | collective-permute-start | bytes 835592 | tf_op jit(solution)/shard_map/ppermute | solution.py:271
  4.9 0.5 %collective-permute-start.1 = (bf16[64,2176]{1,0:T(8,128)(2,1)S(1)}, bf16[64,2176]{1,0:T(8,128)(2,1)S(1)}, u32[]{:S(2)}, u32[]{:S(2)}) collective-permute-start(bf16[64,2176]{1,0:T(8,128)(2,1)S(1)} %get-tuple-element.13), channel_id=1, source_target_pairs={{0,7},{1,6},{2,5},{3,4},{4,3},{5,2},{6,1},{7,0},{8,15},{9,14},{10,... | collective-permute-start | bytes 835592 | tf_op jit(solution)/shard_map/ppermute | solution.py:271
  5.4 1.0 %collective-permute-start.2 = (bf16[64,2176]{1,0:T(8,128)(2,1)S(1)}, bf16[64,2176]{1,0:T(8,128)(2,1)S(1)}, u32[]{:S(2)}, u32[]{:S(2)}) collective-permute-start(bf16[64,2176]{1,0:T(8,128)(2,1)S(1)} %get-tuple-element.14), channel_id=1, source_target_pairs={{0,2},{1,3},{2,0},{3,1},{4,6},{5,7},{6,4},{7,5},{8,10},{9,11},{10,... | collective-permute-start | bytes 835592 | tf_op jit(solution)/shard_map/ppermute | solution.py:271
  6.4 3.9 %training_gradients.1 = (bf16[64,1024]{1,0:T(8,128)(2,1)S(1)}, bf16[64,1024]{1,0:T(8,128)(2,1)S(1)}) custom-call(s32[2]{0:T(128)} %length_source.1, bf16[2,128,4096]{2,1,0:T(8,128)(2,1)} %inputs.3, bf16[2,128,4096]{2,1,0:T(8,128)(2,1)} %gradient.3, bf16[16,4096]{1,0:T(8,128)(2,1)} %bitcast.10, bf16[16,4096]{1,0:T(8,128)(2,1)} %bitcast.12), custom_call_target="tpu_custom_call" | custom-call | flops 201326592 | bytes 12582912 | tf_op jit(solution)/shard_map/training_gradients/pallas_call | solution.py:273
  10.3 2.5 %collective-permute-start.5 = (bf16[64,1024]{1,0:T(8,128)(2,1)S(1)}, bf16[64,1024]{1,0:T(8,128)(2,1)S(1)}, u32[]{:S(2)}, u32[]{:S(2)}) collective-permute-start(bf16[64,1024]{1,0:T(8,128)(2,1)S(1)} %get-tuple-element.15.refs_0_), channel_id=1, source_target_pairs={{0,9},{1,8},{4,13},{5,12},{8,1},{9,0},{12,5},{13,4},{2,11},{3,10},... | collective-permute-start | bytes 393224 | tf_op jit(solution)/shard_map/ppermute | solution.py:243
  12.8 1.1 %collective-permute-start.6 = (bf16[64,1024]{1,0:T(8,128)(2,1)S(1)}, bf16[64,1024]{1,0:T(8,128)(2,1)S(1)}, u32[]{:S(2)}, u32[]{:S(2)}) collective-permute-start(bf16[64,1024]{1,0:T(8,128)(2,1)S(1)} %get-tuple-element.16.source), channel_id=1, source_target_pairs={{0,13},{1,12},{4,9},{5,8},{8,5},{9,4},{12,1},{13,0},{2,15},{3,14},... | collective-permute-start | bytes 393224 | tf_op jit(solution)/shard_map/ppermute | solution.py:243
  13.9 0.0 collective-permute-done.refs_1_
  13.9 6.4 %collective-permute-done.1.refs_2_ = bf16[64,2176]{1,0:T(8,128)(2,1)S(1)} collective-permute-done((bf16[64,2176]{1,0:T(8,128)(2,1)S(1)}, bf16[64,2176]{1,0:T(8,128)(2,1)S(1)}, u32[]{:S(2)}, u32[]{:S(2)}) %collective-permute-start.1) | collective-permute-done | bytes 278560 | tf_op jit(solution)/shard_map/ppermute | solution.py:271
  20.3 0.0 collective-permute-done.2.refs_3_
  20.3 0.2 token_stack.1._.refs_0_
  20.6 1.3 %collective-permute-start.3 = (bf16[560,1024]{1,0:T(8,128)(2,1)S(1)}, bf16[560,1024]{1,0:T(8,128)(2,1)S(1)}, u32[]{:S(2)}, u32[]{:S(2)}) collective-permute-start(bf16[560,1024]{1,0:T(8,128)(2,1)S(1)} %token_stack.1._.refs_0_), channel_id=1, source_target_pairs={{0,1},{1,0},{2,3},{3,2},{4,5},{5,4},{6,7},{7,6},{8,9},{9,8},{10,11... | collective-permute-start | bytes 3440648 | tf_op jit(solution)/shard_map/ppermute | solution.py:32
  21.9 1.0 %collective-permute-start.4 = (bf16[64,1024]{1,0:T(8,128)(2,1)S(1)}, bf16[64,1024]{1,0:T(8,128)(2,1)S(1)}, u32[]{:S(2)}, u32[]{:S(2)}) collective-permute-start(bf16[64,1024]{1,0:T(8,128)(2,1)S(1)} %near_gradient.1), channel_id=1, source_target_pairs={{0,4},{4,0},{8,12},{12,8},{1,5},{5,1},{9,13},{13,9},{2,6},{6,2},{1... | collective-permute-start | bytes 393224 | tf_op jit(solution)/shard_map/ppermute | solution.py:32
  22.9 0.0 collective-permute-done.5.refs_0_
  22.9 1.4 %collective-permute-done.6.refs_1_ = bf16[64,1024]{1,0:T(8,128)(2,1)S(1)} collective-permute-done((bf16[64,1024]{1,0:T(8,128)(2,1)S(1)}, bf16[64,1024]{1,0:T(8,128)(2,1)S(1)}, u32[]{:S(2)}, u32[]{:S(2)}) %collective-permute-start.6) | collective-permute-done | bytes 131104 | tf_op jit(solution)/shard_map/ppermute | solution.py:243
  24.4 0.0 collective-permute-done.3.refs_1_
  24.4 0.9 %far_scores.1 = f32[2,4,8]{2,1,0:T(4,128)S(1)} custom-call(bf16[560,1024]{1,0:T(8,128)(2,1)S(1)} %token_stack.1._.refs_0_, bf16[560,1024]{1,0:T(8,128)(2,1)S(1)} %collective-permute-done.3.refs_1_, bf16[128,1024]{1,0:T(8,128)(2,1)S(1)} %far_gradients.1.refs_2_), custom_call_target="tpu_custom_call" | custom-call | bytes 573440 | tf_op jit(solution)/shard_map/far_scores/pallas_call | solution.py:299
  25.3 2.9 %collective-permute-start.7 = (f32[2,4,8]{2,1,0:T(4,128)S(1)}, f32[2,4,8]{2,1,0:T(4,128)S(1)}, u32[]{:S(2)}, u32[]{:S(2)}) collective-permute-start(f32[2,4,8]{2,1,0:T(4,128)S(1)} %far_scores.1), channel_id=1, source_target_pairs={{0,9},{1,8},{4,13},{5,12},{8,1},{9,0},{12,5},{13,4},{2,11},{3,10},... | collective-permute-start | bytes 776 | tf_op jit(solution)/shard_map/ppermute | solution.py:243
  28.2 0.1 collective-permute-done.4.refs_1_
  28.3 0.9 %near_scores.1 = f32[2,4,8]{2,1,0:T(4,128)S(1)} custom-call(bf16[560,1024]{1,0:T(8,128)(2,1)S(1)} %token_stack.1._.refs_0_, bf16[560,1024]{1,0:T(8,128)(2,1)S(1)} %collective-permute-done.3.refs_1_, bf16[128,1024]{1,0:T(8,128)(2,1)S(1)} %near_gradients.1.refs_2_), custom_call_target="tpu_custom_call" | custom-call | bytes 573440 | tf_op jit(solution)/shard_map/near_scores/pallas_call | solution.py:299
  29.2 0.3 collective-permute-done.7
  29.5 1.8 %collective-permute-start.9 = (f32[1,4,8]{2,1,0:T(4,128)S(1)}, f32[1,4,8]{2,1,0:T(4,128)S(1)}, u32[]{:S(2)}, u32[]{:S(2)}) collective-permute-start(f32[1,4,8]{2,1,0:T(4,128)S(1)} %get-tuple-element.17), channel_id=1, source_target_pairs={{0,3},{1,2},{2,1},{3,0},{4,7},{5,6},{6,5},{7,4},{8,11},{9,10},{10,... | collective-permute-start | bytes 392 | tf_op jit(solution)/shard_map/ppermute | solution.py:243
  31.3 0.1 collective-permute-start.8
  31.4 1.2 %collective-permute-done.9 = f32[1,4,8]{2,1,0:T(4,128)S(1)} collective-permute-done((f32[1,4,8]{2,1,0:T(4,128)S(1)}, f32[1,4,8]{2,1,0:T(4,128)S(1)}, u32[]{:S(2)}, u32[]{:S(2)}) %collective-permute-start.9) | collective-permute-done | bytes 160 | tf_op jit(solution)/shard_map/ppermute | solution.py:243
  32.7 0.0 collective-permute-done.8
  32.7 1.7 %collective-permute-start.11 = (f32[2,8]{1,0:T(2,128)S(1)}, f32[2,8]{1,0:T(2,128)S(1)}, u32[]{:S(2)}, u32[]{:S(2)}) collective-permute-start(f32[2,8]{1,0:T(2,128)S(1)} %get-tuple-element.19), channel_id=1, source_target_pairs={{0,5},{1,4},{4,1},{5,0},{8,13},{9,12},{12,9},{13,8},{2,7},{3,6},{6... | collective-permute-start | bytes 200 | tf_op jit(solution)/shard_map/ppermute | solution.py:243
  34.4 0.4 %collective-permute-start.10 = (f32[2,8]{1,0:T(2,128)S(1)}, f32[2,8]{1,0:T(2,128)S(1)}, u32[]{:S(2)}, u32[]{:S(2)}) collective-permute-start(f32[2,8]{1,0:T(2,128)S(1)} %get-tuple-element.20), channel_id=1, source_target_pairs={{0,1},{1,0},{2,3},{3,2},{4,5},{5,4},{6,7},{7,6},{8,9},{9,8},{10,11... | collective-permute-start | bytes 200 | tf_op jit(solution)/shard_map/ppermute | solution.py:32
  34.8 1.0 %collective-permute-done.11 = f32[2,8]{1,0:T(2,128)S(1)} collective-permute-done((f32[2,8]{1,0:T(2,128)S(1)}, f32[2,8]{1,0:T(2,128)S(1)}, u32[]{:S(2)}, u32[]{:S(2)}) %collective-permute-start.11) | collective-permute-done | bytes 96 | tf_op jit(solution)/shard_map/ppermute | solution.py:243
  35.7 0.0 collective-permute-done.10
  35.7 0.6 %add_bitcast_fusion = f32[8,2]{0,1:T(2,128)} fusion(f32[2,8]{1,0:T(2,128)S(1)} %collective-permute-done.10, f32[2,8]{1,0:T(2,128)S(1)} %collective-permute-done.11), kind=kLoop, calls=%fused_computation | loop fusion | flops 16 | bytes 192 | tf_op jit(solution)/shard_map/transpose | solution.py:366
  (7 shorter events, 0.1 us)
Async XLA Ops:
  1.8 12.1 %collective-permute-start = (bf16[64,2176]{1,0:T(8,128)(2,1)S(1)}, bf16[64,2176]{1,0:T(8,128)(2,1)S(1)}, u32[]{:S(2)}, u32[]{:S(2)}) collective-permute-start(bf16[64,2176]{1,0:T(8,128)(2,1)S(1)} %get-tuple-element.12), channel_id=1, source_target_pairs={{0,4},{1,5},{2,6},{3,7},{4,0},{5,1},{6,2},{7,3},{8,12},{9,13},{10,... | collective-permute-start | bytes 835592 | tf_op jit(solution)/shard_map/ppermute | solution.py:271
  4.9 15.4 %collective-permute-start.1 = (bf16[64,2176]{1,0:T(8,128)(2,1)S(1)}, bf16[64,2176]{1,0:T(8,128)(2,1)S(1)}, u32[]{:S(2)}, u32[]{:S(2)}) collective-permute-start(bf16[64,2176]{1,0:T(8,128)(2,1)S(1)} %get-tuple-element.13), channel_id=1, source_target_pairs={{0,7},{1,6},{2,5},{3,4},{4,3},{5,2},{6,1},{7,0},{8,15},{9,14},{10,... | collective-permute-start | bytes 835592 | tf_op jit(solution)/shard_map/ppermute | solution.py:271
  5.4 14.9 %collective-permute-start.2 = (bf16[64,2176]{1,0:T(8,128)(2,1)S(1)}, bf16[64,2176]{1,0:T(8,128)(2,1)S(1)}, u32[]{:S(2)}, u32[]{:S(2)}) collective-permute-start(bf16[64,2176]{1,0:T(8,128)(2,1)S(1)} %get-tuple-element.14), channel_id=1, source_target_pairs={{0,2},{1,3},{2,0},{3,1},{4,6},{5,7},{6,4},{7,5},{8,10},{9,11},{10,... | collective-permute-start | bytes 835592 | tf_op jit(solution)/shard_map/ppermute | solution.py:271
  10.3 12.6 %collective-permute-start.5 = (bf16[64,1024]{1,0:T(8,128)(2,1)S(1)}, bf16[64,1024]{1,0:T(8,128)(2,1)S(1)}, u32[]{:S(2)}, u32[]{:S(2)}) collective-permute-start(bf16[64,1024]{1,0:T(8,128)(2,1)S(1)} %get-tuple-element.15.refs_0_), channel_id=1, source_target_pairs={{0,9},{1,8},{4,13},{5,12},{8,1},{9,0},{12,5},{13,4},{2,11},{3,10},... | collective-permute-start | bytes 393224 | tf_op jit(solution)/shard_map/ppermute | solution.py:243
  12.8 11.5 %collective-permute-start.6 = (bf16[64,1024]{1,0:T(8,128)(2,1)S(1)}, bf16[64,1024]{1,0:T(8,128)(2,1)S(1)}, u32[]{:S(2)}, u32[]{:S(2)}) collective-permute-start(bf16[64,1024]{1,0:T(8,128)(2,1)S(1)} %get-tuple-element.16.source), channel_id=1, source_target_pairs={{0,13},{1,12},{4,9},{5,8},{8,5},{9,4},{12,1},{13,0},{2,15},{3,14},... | collective-permute-start | bytes 393224 | tf_op jit(solution)/shard_map/ppermute | solution.py:243
  20.6 3.8 %collective-permute-start.3 = (bf16[560,1024]{1,0:T(8,128)(2,1)S(1)}, bf16[560,1024]{1,0:T(8,128)(2,1)S(1)}, u32[]{:S(2)}, u32[]{:S(2)}) collective-permute-start(bf16[560,1024]{1,0:T(8,128)(2,1)S(1)} %token_stack.1._.refs_0_), channel_id=1, source_target_pairs={{0,1},{1,0},{2,3},{3,2},{4,5},{5,4},{6,7},{7,6},{8,9},{9,8},{10,11... | collective-permute-start | bytes 3440648 | tf_op jit(solution)/shard_map/ppermute | solution.py:32
  21.9 6.4 %collective-permute-start.4 = (bf16[64,1024]{1,0:T(8,128)(2,1)S(1)}, bf16[64,1024]{1,0:T(8,128)(2,1)S(1)}, u32[]{:S(2)}, u32[]{:S(2)}) collective-permute-start(bf16[64,1024]{1,0:T(8,128)(2,1)S(1)} %near_gradient.1), channel_id=1, source_target_pairs={{0,4},{4,0},{8,12},{12,8},{1,5},{5,1},{9,13},{13,9},{2,6},{6,2},{1... | collective-permute-start | bytes 393224 | tf_op jit(solution)/shard_map/ppermute | solution.py:32
  25.3 4.2 %collective-permute-start.7 = (f32[2,4,8]{2,1,0:T(4,128)S(1)}, f32[2,4,8]{2,1,0:T(4,128)S(1)}, u32[]{:S(2)}, u32[]{:S(2)}) collective-permute-start(f32[2,4,8]{2,1,0:T(4,128)S(1)} %far_scores.1), channel_id=1, source_target_pairs={{0,9},{1,8},{4,13},{5,12},{8,1},{9,0},{12,5},{13,4},{2,11},{3,10},... | collective-permute-start | bytes 776 | tf_op jit(solution)/shard_map/ppermute | solution.py:243
  29.5 3.1 %collective-permute-start.9 = (f32[1,4,8]{2,1,0:T(4,128)S(1)}, f32[1,4,8]{2,1,0:T(4,128)S(1)}, u32[]{:S(2)}, u32[]{:S(2)}) collective-permute-start(f32[1,4,8]{2,1,0:T(4,128)S(1)} %get-tuple-element.17), channel_id=1, source_target_pairs={{0,3},{1,2},{2,1},{3,0},{4,7},{5,6},{6,5},{7,4},{8,11},{9,10},{10,... | collective-permute-start | bytes 392 | tf_op jit(solution)/shard_map/ppermute | solution.py:243
  31.3 1.3 %collective-permute-start.8 = (f32[1,4,8]{2,1,0:T(4,128)S(1)}, f32[1,4,8]{2,1,0:T(4,128)S(1)}, u32[]{:S(2)}, u32[]{:S(2)}) collective-permute-start(f32[1,4,8]{2,1,0:T(4,128)S(1)} %get-tuple-element.18), channel_id=1, source_target_pairs={{0,1},{1,0},{2,3},{3,2},{4,5},{5,4},{6,7},{7,6},{8,9},{9,8},{10,11... | collective-permute-start | bytes 392 | tf_op jit(solution)/shard_map/ppermute | solution.py:32
  32.7 3.1 %collective-permute-start.11 = (f32[2,8]{1,0:T(2,128)S(1)}, f32[2,8]{1,0:T(2,128)S(1)}, u32[]{:S(2)}, u32[]{:S(2)}) collective-permute-start(f32[2,8]{1,0:T(2,128)S(1)} %get-tuple-element.19), channel_id=1, source_target_pairs={{0,5},{1,4},{4,1},{5,0},{8,13},{9,12},{12,9},{13,8},{2,7},{3,6},{6... | collective-permute-start | bytes 200 | tf_op jit(solution)/shard_map/ppermute | solution.py:243
  34.4 1.4 %collective-permute-start.10 = (f32[2,8]{1,0:T(2,128)S(1)}, f32[2,8]{1,0:T(2,128)S(1)}, u32[]{:S(2)}, u32[]{:S(2)}) collective-permute-start(f32[2,8]{1,0:T(2,128)S(1)} %get-tuple-element.20), channel_id=1, source_target_pairs={{0,1},{1,0},{2,3},{3,2},{4,5},{5,4},{6,7},{7,6},{8,9},{9,8},{10,11... | collective-permute-start | bytes 200 | tf_op jit(solution)/shard_map/ppermute | solution.py:32

commit v7 on v6

--- a/solution.py
+++ b/solution.py
@@ -259,7 +259,7 @@
         name="query_shares",
     )(*in_hbm(query_inputs, query_gradient, query_sequence_index.reshape(1, tokens), down, up))
     blocks = [shares[0]]
-    for place in sorted(range(1, nlo * nsub), key=lambda place: place < nsub):
+    for place in sorted(range(1, nlo * nsub), key=lambda place: (place != nsub, place > nsub)):
         dlo, dsub = place // nsub, place % nsub
         flip = dlo & (dsub > 0)
         pairs = []

time: 36.7 us -> 36.7 us (level)
  waiting for transfers between devices: 10.4 us -> 11.5 us
  starting transfers between devices: 17.4 us -> 16.5 us
    ppermute x4, starting transfers between devices: 2.82 us -> 1.73 us  [swap(): lax.ppermute(value, axis, [(source, source ^ distance) for source in rang...]
    ppermute x5, waiting for transfers between devices: 3.88 us -> 4.91 us  [crossing(): return lax.ppermute(value, (axis, 'pair'), pairs)]
where the time goes in v7:
time: 36.7 us; the launch traced here: 36.4 us
  starting transfers between devices  16.5 us (45%)
  waiting for transfers between devices  11.5 us (31%)
  Pallas kernels  7.78 us (21%)
  other arithmetic  0.57 us (2%)
    ppermute x5, starting transfers between devices, crossing(): return lax.ppermute(value, (axis, 'pair'), pairs)  10.2 us
    ppermute x3, waiting for transfers between devices, per_device(): blocks.append(lax.ppermute(shares[place], ('dp', 'sub', 'pair'), pairs))  6.16 us
    ppermute x5, waiting for transfers between devices, crossing(): return lax.ppermute(value, (axis, 'pair'), pairs)  4.91 us
    ppermute x3, starting transfers between devices, per_device(): blocks.append(lax.ppermute(shares[place], ('dp', 'sub', 'pair'), pairs))  4.58 us
    pallas_call x1, Pallas kernels, per_device(): pl.pallas_call(functools.partial(training_kernel, nlo, nsub), out_shape=[...  3.87 us
    pallas_call x6, Pallas kernels, call(): pl.pallas_call(kernel, out_shape=jax.ShapeDtypeStruct(*shape), in_specs=[...  2.11 us
    pallas_call x1, Pallas kernels, per_device(): pl.pallas_call(functools.partial(query_kernel, nlo, nsub), out_shape=[jax...  1.8 us
    ppermute x4, starting transfers between devices, swap(): lax.ppermute(value, axis, [(source, source ^ distance) for source in rang...  1.73 us
  transfers between devices with their start and end apart: 12, of which 6 were waited for; matrix products, arithmetic and copies ran while one was open for 0% of the time, Pallas kernels for 16%

profile of v7, /device:TPU:0, one launch (start us, length us, event | category | flops | bytes accessed | tf_op | source)
XLA Modules:
  0.0 36.4 jit_solution(9901807488433960449)
XLA Ops:
  0.0 1.8 %query_shares.1 = (bf16[64,2176]{1,0:T(8,128)(2,1)S(1)}, bf16[64,2176]{1,0:T(8,128)(2,1)S(1)}, bf16[64,2176]{1,0:T(8,128)(2,1)S(1)}, bf16[64,2176]{1,0:T(8,128)(2,1)S(1)}) custom-call(bf16[64,4096]{1,0:T(8,128)(2,1)} %inputs.2, bf16[64,4096]{1,0:T(8,128)(2,1)} %gradient.2, s32[1,64]{1,0:T(1,128)} %bitcast.13, bf16[16,4096]{1,0:T(8,128)(2,1)} %bitcast.9, ...), custom_call_target="tpu_custom_call" | custom-call | tf_op jit(solution)/shard_map/query_shares/pallas_call | solution.py:245
  1.8 3.1 %collective-permute-start = (bf16[64,2176]{1,0:T(8,128)(2,1)S(1)}, bf16[64,2176]{1,0:T(8,128)(2,1)S(1)}, u32[]{:S(2)}, u32[]{:S(2)}) collective-permute-start(bf16[64,2176]{1,0:T(8,128)(2,1)S(1)} %get-tuple-element.12), channel_id=1, source_target_pairs={{0,4},{1,5},{2,6},{3,7},{4,0},{5,1},{6,2},{7,3},{8,12},{9,13},{10,... | collective-permute-start | bytes 835592 | tf_op jit(solution)/shard_map/ppermute | solution.py:271
  4.9 1.5 %collective-permute-start.1 = (bf16[64,2176]{1,0:T(8,128)(2,1)S(1)}, bf16[64,2176]{1,0:T(8,128)(2,1)S(1)}, u32[]{:S(2)}, u32[]{:S(2)}) collective-permute-start(bf16[64,2176]{1,0:T(8,128)(2,1)S(1)} %get-tuple-element.13), channel_id=1, source_target_pairs={{0,2},{1,3},{2,0},{3,1},{4,6},{5,7},{6,4},{7,5},{8,10},{9,11},{10,... | collective-permute-start | bytes 835592 | tf_op jit(solution)/shard_map/ppermute | solution.py:271
  6.4 0.0 collective-permute-start.2
  6.4 3.9 %training_gradients.1 = (bf16[64,1024]{1,0:T(8,128)(2,1)S(1)}, bf16[64,1024]{1,0:T(8,128)(2,1)S(1)}) custom-call(s32[2]{0:T(128)} %length_source.1, bf16[2,128,4096]{2,1,0:T(8,128)(2,1)} %inputs.3, bf16[2,128,4096]{2,1,0:T(8,128)(2,1)} %gradient.3, bf16[16,4096]{1,0:T(8,128)(2,1)} %bitcast.10, bf16[16,4096]{1,0:T(8,128)(2,1)} %bitcast.12), custom_call_target="tpu_custom_call" | custom-call | flops 201326592 | bytes 12582912 | tf_op jit(solution)/shard_map/training_gradients/pallas_call | solution.py:273
  10.3 2.8 %collective-permute-start.5 = (bf16[64,1024]{1,0:T(8,128)(2,1)S(1)}, bf16[64,1024]{1,0:T(8,128)(2,1)S(1)}, u32[]{:S(2)}, u32[]{:S(2)}) collective-permute-start(bf16[64,1024]{1,0:T(8,128)(2,1)S(1)} %get-tuple-element.15.refs_0_), channel_id=1, source_target_pairs={{0,9},{1,8},{4,13},{5,12},{8,1},{9,0},{12,5},{13,4},{2,11},{3,10},... | collective-permute-start | bytes 393224 | tf_op jit(solution)/shard_map/ppermute | solution.py:243
  13.1 1.1 %collective-permute-start.6 = (bf16[64,1024]{1,0:T(8,128)(2,1)S(1)}, bf16[64,1024]{1,0:T(8,128)(2,1)S(1)}, u32[]{:S(2)}, u32[]{:S(2)}) collective-permute-start(bf16[64,1024]{1,0:T(8,128)(2,1)S(1)} %get-tuple-element.16.source), channel_id=1, source_target_pairs={{0,13},{1,12},{4,9},{5,8},{8,5},{9,4},{12,1},{13,0},{2,15},{3,14},... | collective-permute-start | bytes 393224 | tf_op jit(solution)/shard_map/ppermute | solution.py:243
  14.2 0.0 collective-permute-done.refs_1_
  14.2 1.5 %collective-permute-done.1.refs_2_ = bf16[64,2176]{1,0:T(8,128)(2,1)S(1)} collective-permute-done((bf16[64,2176]{1,0:T(8,128)(2,1)S(1)}, bf16[64,2176]{1,0:T(8,128)(2,1)S(1)}, u32[]{:S(2)}, u32[]{:S(2)}) %collective-permute-start.1) | collective-permute-done | bytes 278560 | tf_op jit(solution)/shard_map/ppermute | solution.py:271
  15.7 4.7 %collective-permute-done.2.refs_3_ = bf16[64,2176]{1,0:T(8,128)(2,1)S(1)} collective-permute-done((bf16[64,2176]{1,0:T(8,128)(2,1)S(1)}, bf16[64,2176]{1,0:T(8,128)(2,1)S(1)}, u32[]{:S(2)}, u32[]{:S(2)}) %collective-permute-start.2) | collective-permute-done | bytes 278560 | tf_op jit(solution)/shard_map/ppermute | solution.py:271
  20.3 0.2 token_stack.1._.refs_0_
  20.6 1.3 %collective-permute-start.3 = (bf16[560,1024]{1,0:T(8,128)(2,1)S(1)}, bf16[560,1024]{1,0:T(8,128)(2,1)S(1)}, u32[]{:S(2)}, u32[]{:S(2)}) collective-permute-start(bf16[560,1024]{1,0:T(8,128)(2,1)S(1)} %token_stack.1._.refs_0_), channel_id=1, source_target_pairs={{0,1},{1,0},{2,3},{3,2},{4,5},{5,4},{6,7},{7,6},{8,9},{9,8},{10,11... | collective-permute-start | bytes 3440648 | tf_op jit(solution)/shard_map/ppermute | solution.py:32
  21.9 0.0 collective-permute-start.4
  21.9 0.0 collective-permute-done.5.refs_0_
  21.9 2.4 %collective-permute-done.6.refs_1_ = bf16[64,1024]{1,0:T(8,128)(2,1)S(1)} collective-permute-done((bf16[64,1024]{1,0:T(8,128)(2,1)S(1)}, bf16[64,1024]{1,0:T(8,128)(2,1)S(1)}, u32[]{:S(2)}, u32[]{:S(2)}) %collective-permute-start.6) | collective-permute-done | bytes 131104 | tf_op jit(solution)/shard_map/ppermute | solution.py:243
  24.4 0.0 collective-permute-done.3.refs_1_
  24.4 0.9 %far_scores.1 = f32[2,4,8]{2,1,0:T(4,128)S(1)} custom-call(bf16[560,1024]{1,0:T(8,128)(2,1)S(1)} %token_stack.1._.refs_0_, bf16[560,1024]{1,0:T(8,128)(2,1)S(1)} %collective-permute-done.3.refs_1_, bf16[128,1024]{1,0:T(8,128)(2,1)S(1)} %far_gradients.1.refs_2_), custom_call_target="tpu_custom_call" | custom-call | bytes 573440 | tf_op jit(solution)/shard_map/far_scores/pallas_call | solution.py:299
  25.3 2.6 %collective-permute-start.7 = (f32[2,4,8]{2,1,0:T(4,128)S(1)}, f32[2,4,8]{2,1,0:T(4,128)S(1)}, u32[]{:S(2)}, u32[]{:S(2)}) collective-permute-start(f32[2,4,8]{2,1,0:T(4,128)S(1)} %far_scores.1), channel_id=1, source_target_pairs={{0,9},{1,8},{4,13},{5,12},{8,1},{9,0},{12,5},{13,4},{2,11},{3,10},... | collective-permute-start | bytes 776 | tf_op jit(solution)/shard_map/ppermute | solution.py:243
  27.9 0.4 %collective-permute-done.4.refs_1_ = bf16[64,1024]{1,0:T(8,128)(2,1)S(1)} collective-permute-done((bf16[64,1024]{1,0:T(8,128)(2,1)S(1)}, bf16[64,1024]{1,0:T(8,128)(2,1)S(1)}, u32[]{:S(2)}, u32[]{:S(2)}) %collective-permute-start.4) | collective-permute-done | bytes 131104 | tf_op jit(solution)/shard_map/ppermute | solution.py:32
  28.3 0.9 %near_scores.1 = f32[2,4,8]{2,1,0:T(4,128)S(1)} custom-call(bf16[560,1024]{1,0:T(8,128)(2,1)S(1)} %token_stack.1._.refs_0_, bf16[560,1024]{1,0:T(8,128)(2,1)S(1)} %collective-permute-done.3.refs_1_, bf16[128,1024]{1,0:T(8,128)(2,1)S(1)} %near_gradients.1.refs_2_), custom_call_target="tpu_custom_call" | custom-call | bytes 573440 | tf_op jit(solution)/shard_map/near_scores/pallas_call | solution.py:299
  29.2 0.0 collective-permute-done.7
  29.3 2.2 %collective-permute-start.9 = (f32[1,4,8]{2,1,0:T(4,128)S(1)}, f32[1,4,8]{2,1,0:T(4,128)S(1)}, u32[]{:S(2)}, u32[]{:S(2)}) collective-permute-start(f32[1,4,8]{2,1,0:T(4,128)S(1)} %get-tuple-element.17), channel_id=1, source_target_pairs={{0,3},{1,2},{2,1},{3,0},{4,7},{5,6},{6,5},{7,4},{8,11},{9,10},{10,... | collective-permute-start | bytes 392 | tf_op jit(solution)/shard_map/ppermute | solution.py:243
  31.4 0.0 collective-permute-start.8
  31.4 1.3 %collective-permute-done.9 = f32[1,4,8]{2,1,0:T(4,128)S(1)} collective-permute-done((f32[1,4,8]{2,1,0:T(4,128)S(1)}, f32[1,4,8]{2,1,0:T(4,128)S(1)}, u32[]{:S(2)}, u32[]{:S(2)}) %collective-permute-start.9) | collective-permute-done | bytes 160 | tf_op jit(solution)/shard_map/ppermute | solution.py:243
  32.7 0.0 collective-permute-done.8
  32.8 1.5 %collective-permute-start.11 = (f32[2,8]{1,0:T(2,128)S(1)}, f32[2,8]{1,0:T(2,128)S(1)}, u32[]{:S(2)}, u32[]{:S(2)}) collective-permute-start(f32[2,8]{1,0:T(2,128)S(1)} %get-tuple-element.19), channel_id=1, source_target_pairs={{0,5},{1,4},{4,1},{5,0},{8,13},{9,12},{12,9},{13,8},{2,7},{3,6},{6... | collective-permute-start | bytes 200 | tf_op jit(solution)/shard_map/ppermute | solution.py:243
  34.3 0.4 %collective-permute-start.10 = (f32[2,8]{1,0:T(2,128)S(1)}, f32[2,8]{1,0:T(2,128)S(1)}, u32[]{:S(2)}, u32[]{:S(2)}) collective-permute-start(f32[2,8]{1,0:T(2,128)S(1)} %get-tuple-element.20), channel_id=1, source_target_pairs={{0,1},{1,0},{2,3},{3,2},{4,5},{5,4},{6,7},{7,6},{8,9},{9,8},{10,11... | collective-permute-start | bytes 200 | tf_op jit(solution)/shard_map/ppermute | solution.py:32
  34.6 1.2 %collective-permute-done.11 = f32[2,8]{1,0:T(2,128)S(1)} collective-permute-done((f32[2,8]{1,0:T(2,128)S(1)}, f32[2,8]{1,0:T(2,128)S(1)}, u32[]{:S(2)}, u32[]{:S(2)}) %collective-permute-start.11) | collective-permute-done | bytes 96 | tf_op jit(solution)/shard_map/ppermute | solution.py:243
  35.8 0.0 collective-permute-done.10
  35.8 0.6 %add_bitcast_fusion = f32[8,2]{0,1:T(2,128)} fusion(f32[2,8]{1,0:T(2,128)S(1)} %collective-permute-done.10, f32[2,8]{1,0:T(2,128)S(1)} %collective-permute-done.11), kind=kLoop, calls=%fused_computation | loop fusion | flops 16 | bytes 192 | tf_op jit(solution)/shard_map/transpose | solution.py:366
  (7 shorter events, 0.1 us)
Async XLA Ops:
  1.8 12.3 %collective-permute-start = (bf16[64,2176]{1,0:T(8,128)(2,1)S(1)}, bf16[64,2176]{1,0:T(8,128)(2,1)S(1)}, u32[]{:S(2)}, u32[]{:S(2)}) collective-permute-start(bf16[64,2176]{1,0:T(8,128)(2,1)S(1)} %get-tuple-element.12), channel_id=1, source_target_pairs={{0,4},{1,5},{2,6},{3,7},{4,0},{5,1},{6,2},{7,3},{8,12},{9,13},{10,... | collective-permute-start | bytes 835592 | tf_op jit(solution)/shard_map/ppermute | solution.py:271
  4.9 10.8 %collective-permute-start.1 = (bf16[64,2176]{1,0:T(8,128)(2,1)S(1)}, bf16[64,2176]{1,0:T(8,128)(2,1)S(1)}, u32[]{:S(2)}, u32[]{:S(2)}) collective-permute-start(bf16[64,2176]{1,0:T(8,128)(2,1)S(1)} %get-tuple-element.13), channel_id=1, source_target_pairs={{0,2},{1,3},{2,0},{3,1},{4,6},{5,7},{6,4},{7,5},{8,10},{9,11},{10,... | collective-permute-start | bytes 835592 | tf_op jit(solution)/shard_map/ppermute | solution.py:271
  6.4 13.9 %collective-permute-start.2 = (bf16[64,2176]{1,0:T(8,128)(2,1)S(1)}, bf16[64,2176]{1,0:T(8,128)(2,1)S(1)}, u32[]{:S(2)}, u32[]{:S(2)}) collective-permute-start(bf16[64,2176]{1,0:T(8,128)(2,1)S(1)} %get-tuple-element.14), channel_id=1, source_target_pairs={{0,7},{1,6},{2,5},{3,4},{4,3},{5,2},{6,1},{7,0},{8,15},{9,14},{10,... | collective-permute-start | bytes 835592 | tf_op jit(solution)/shard_map/ppermute | solution.py:271
  10.3 11.6 %collective-permute-start.5 = (bf16[64,1024]{1,0:T(8,128)(2,1)S(1)}, bf16[64,1024]{1,0:T(8,128)(2,1)S(1)}, u32[]{:S(2)}, u32[]{:S(2)}) collective-permute-start(bf16[64,1024]{1,0:T(8,128)(2,1)S(1)} %get-tuple-element.15.refs_0_), channel_id=1, source_target_pairs={{0,9},{1,8},{4,13},{5,12},{8,1},{9,0},{12,5},{13,4},{2,11},{3,10},... | collective-permute-start | bytes 393224 | tf_op jit(solution)/shard_map/ppermute | solution.py:243
  13.1 11.3 %collective-permute-start.6 = (bf16[64,1024]{1,0:T(8,128)(2,1)S(1)}, bf16[64,1024]{1,0:T(8,128)(2,1)S(1)}, u32[]{:S(2)}, u32[]{:S(2)}) collective-permute-start(bf16[64,1024]{1,0:T(8,128)(2,1)S(1)} %get-tuple-element.16.source), channel_id=1, source_target_pairs={{0,13},{1,12},{4,9},{5,8},{8,5},{9,4},{12,1},{13,0},{2,15},{3,14},... | collective-permute-start | bytes 393224 | tf_op jit(solution)/shard_map/ppermute | solution.py:243
  20.6 3.8 %collective-permute-start.3 = (bf16[560,1024]{1,0:T(8,128)(2,1)S(1)}, bf16[560,1024]{1,0:T(8,128)(2,1)S(1)}, u32[]{:S(2)}, u32[]{:S(2)}) collective-permute-start(bf16[560,1024]{1,0:T(8,128)(2,1)S(1)} %token_stack.1._.refs_0_), channel_id=1, source_target_pairs={{0,1},{1,0},{2,3},{3,2},{4,5},{5,4},{6,7},{7,6},{8,9},{9,8},{10,11... | collective-permute-start | bytes 3440648 | tf_op jit(solution)/shard_map/ppermute | solution.py:32
  21.9 6.4 %collective-permute-start.4 = (bf16[64,1024]{1,0:T(8,128)(2,1)S(1)}, bf16[64,1024]{1,0:T(8,128)(2,1)S(1)}, u32[]{:S(2)}, u32[]{:S(2)}) collective-permute-start(bf16[64,1024]{1,0:T(8,128)(2,1)S(1)} %near_gradient.1), channel_id=1, source_target_pairs={{0,4},{4,0},{8,12},{12,8},{1,5},{5,1},{9,13},{13,9},{2,6},{6,2},{1... | collective-permute-start | bytes 393224 | tf_op jit(solution)/shard_map/ppermute | solution.py:32
  25.3 4.0 %collective-permute-start.7 = (f32[2,4,8]{2,1,0:T(4,128)S(1)}, f32[2,4,8]{2,1,0:T(4,128)S(1)}, u32[]{:S(2)}, u32[]{:S(2)}) collective-permute-start(f32[2,4,8]{2,1,0:T(4,128)S(1)} %far_scores.1), channel_id=1, source_target_pairs={{0,9},{1,8},{4,13},{5,12},{8,1},{9,0},{12,5},{13,4},{2,11},{3,10},... | collective-permute-start | bytes 776 | tf_op jit(solution)/shard_map/ppermute | solution.py:243
  29.3 3.5 %collective-permute-start.9 = (f32[1,4,8]{2,1,0:T(4,128)S(1)}, f32[1,4,8]{2,1,0:T(4,128)S(1)}, u32[]{:S(2)}, u32[]{:S(2)}) collective-permute-start(f32[1,4,8]{2,1,0:T(4,128)S(1)} %get-tuple-element.17), channel_id=1, source_target_pairs={{0,3},{1,2},{2,1},{3,0},{4,7},{5,6},{6,5},{7,4},{8,11},{9,10},{10,... | collective-permute-start | bytes 392 | tf_op jit(solution)/shard_map/ppermute | solution.py:243
  31.4 1.3 %collective-permute-start.8 = (f32[1,4,8]{2,1,0:T(4,128)S(1)}, f32[1,4,8]{2,1,0:T(4,128)S(1)}, u32[]{:S(2)}, u32[]{:S(2)}) collective-permute-start(f32[1,4,8]{2,1,0:T(4,128)S(1)} %get-tuple-element.18), channel_id=1, source_target_pairs={{0,1},{1,0},{2,3},{3,2},{4,5},{5,4},{6,7},{7,6},{8,9},{9,8},{10,11... | collective-permute-start | bytes 392 | tf_op jit(solution)/shard_map/ppermute | solution.py:32
  32.8 3.1 %collective-permute-start.11 = (f32[2,8]{1,0:T(2,128)S(1)}, f32[2,8]{1,0:T(2,128)S(1)}, u32[]{:S(2)}, u32[]{:S(2)}) collective-permute-start(f32[2,8]{1,0:T(2,128)S(1)} %get-tuple-element.19), channel_id=1, source_target_pairs={{0,5},{1,4},{4,1},{5,0},{8,13},{9,12},{12,9},{13,8},{2,7},{3,6},{6... | collective-permute-start | bytes 200 | tf_op jit(solution)/shard_map/ppermute | solution.py:243
  34.3 1.6 %collective-permute-start.10 = (f32[2,8]{1,0:T(2,128)S(1)}, f32[2,8]{1,0:T(2,128)S(1)}, u32[]{:S(2)}, u32[]{:S(2)}) collective-permute-start(f32[2,8]{1,0:T(2,128)S(1)} %get-tuple-element.20), channel_id=1, source_target_pairs={{0,1},{1,0},{2,3},{3,2},{4,5},{5,4},{6,7},{7,6},{8,9},{9,8},{10,11... | collective-permute-start | bytes 200 | tf_op jit(solution)/shard_map/ppermute | solution.py:32

commit v8 on v7

--- a/solution.py
+++ b/solution.py
@@ -72,10 +72,11 @@
     for start, share in zip(starts, shares):
         share[:, width : 2 * width] = held_gradient[:, pl.ds(start, width)]
     rank = low_down.shape[0]
-    id_rows = jnp.broadcast_to(held_ids[...].astype(jnp.float32), (EXTRA - 2 * rank, tokens))
-    extras = jnp.concatenate([low_down, low_up, id_rows], axis=0).T.astype(jnp.bfloat16)
+    id_rows = jnp.broadcast_to(held_ids[...].astype(jnp.float32), (KEPT - 2 * rank, tokens))
+    extras = jnp.concatenate([low_down, low_up, id_rows], axis=0).astype(jnp.bfloat16)
     for share in shares:
-        share[:, 2 * width :] = extras
+        share[:, 2 * width :] = jnp.zeros((tokens, EXTRA), jnp.bfloat16)
+        share[0:KEPT, 2 * width : 2 * width + tokens] = extras
 
 
 def training_kernel(nlo, nsub, length_source, inputs, gradient, down, up, *rest):
@@ -160,7 +161,7 @@
         out[place * tokens : (place + 1) * tokens, :] = block[:, 0:width]
         start = total + place * tokens
         out[start : start + tokens, :] = block[:, width : 2 * width]
-        extras.append(block[:, 2 * width :].astype(jnp.float32).T[:KEPT].astype(jnp.bfloat16))
+        extras.append(block[0:KEPT, 2 * width : 2 * width + tokens])
     chunk = min(width, total)
     for place in range(total // chunk):
         some = extras[place * chunk // tokens : (place + 1) * chunk // tokens]

time: 36.7 us -> 36.6 us (level)
  no operation moved by 1% of the time
where the time goes in v8:
time: 36.6 us; the launch traced here: 36.3 us
  starting transfers between devices  16.4 us (45%)
  waiting for transfers between devices  11.7 us (32%)
  Pallas kernels  7.6 us (21%)
  other arithmetic  0.57 us (2%)
    ppermute x5, starting transfers between devices, crossing(): return lax.ppermute(value, (axis, 'pair'), pairs)  10 us
    ppermute x3, waiting for transfers between devices, per_device(): blocks.append(lax.ppermute(shares[place], ('dp', 'sub', 'pair'), pairs))  6.16 us
    ppermute x5, waiting for transfers between devices, crossing(): return lax.ppermute(value, (axis, 'pair'), pairs)  5.15 us
    ppermute x3, starting transfers between devices, per_device(): blocks.append(lax.ppermute(shares[place], ('dp', 'sub', 'pair'), pairs))  4.58 us
    pallas_call x1, Pallas kernels, per_device(): pl.pallas_call(functools.partial(training_kernel, nlo, nsub), out_shape=[...  3.87 us
    pallas_call x6, Pallas kernels, call(): pl.pallas_call(kernel, out_shape=jax.ShapeDtypeStruct(*shape), in_specs=[...  2.01 us
    ppermute x4, starting transfers between devices, swap(): lax.ppermute(value, axis, [(source, source ^ distance) for source in rang...  1.73 us
    pallas_call x1, Pallas kernels, per_device(): pl.pallas_call(functools.partial(query_kernel, nlo, nsub), out_shape=[jax...  1.73 us
  transfers between devices with their start and end apart: 12, of which 6 were waited for; matrix products, arithmetic and copies ran while one was open for 0% of the time, Pallas kernels for 16%

profile of v8, /device:TPU:0, one launch (start us, length us, event | category | flops | bytes accessed | tf_op | source)
XLA Modules:
  0.0 36.3 jit_solution(6277367673043083162)
XLA Ops:
  0.0 1.7 %query_shares.1 = (bf16[64,2176]{1,0:T(8,128)(2,1)S(1)}, bf16[64,2176]{1,0:T(8,128)(2,1)S(1)}, bf16[64,2176]{1,0:T(8,128)(2,1)S(1)}, bf16[64,2176]{1,0:T(8,128)(2,1)S(1)}) custom-call(bf16[64,4096]{1,0:T(8,128)(2,1)} %inputs.2, bf16[64,4096]{1,0:T(8,128)(2,1)} %gradient.2, s32[1,64]{1,0:T(1,128)} %bitcast.13, bf16[16,4096]{1,0:T(8,128)(2,1)} %bitcast.9, ...), custom_call_target="tpu_custom_call" | custom-call | tf_op jit(solution)/shard_map/query_shares/pallas_call | solution.py:246
  1.7 3.1 %collective-permute-start = (bf16[64,2176]{1,0:T(8,128)(2,1)S(1)}, bf16[64,2176]{1,0:T(8,128)(2,1)S(1)}, u32[]{:S(2)}, u32[]{:S(2)}) collective-permute-start(bf16[64,2176]{1,0:T(8,128)(2,1)S(1)} %get-tuple-element.12), channel_id=1, source_target_pairs={{0,4},{1,5},{2,6},{3,7},{4,0},{5,1},{6,2},{7,3},{8,12},{9,13},{10,... | collective-permute-start | bytes 835592 | tf_op jit(solution)/shard_map/ppermute | solution.py:272
  4.8 1.5 %collective-permute-start.1 = (bf16[64,2176]{1,0:T(8,128)(2,1)S(1)}, bf16[64,2176]{1,0:T(8,128)(2,1)S(1)}, u32[]{:S(2)}, u32[]{:S(2)}) collective-permute-start(bf16[64,2176]{1,0:T(8,128)(2,1)S(1)} %get-tuple-element.13), channel_id=1, source_target_pairs={{0,2},{1,3},{2,0},{3,1},{4,6},{5,7},{6,4},{7,5},{8,10},{9,11},{10,... | collective-permute-start | bytes 835592 | tf_op jit(solution)/shard_map/ppermute | solution.py:272
  6.3 0.0 collective-permute-start.2
  6.3 3.9 %training_gradients.1 = (bf16[64,1024]{1,0:T(8,128)(2,1)S(1)}, bf16[64,1024]{1,0:T(8,128)(2,1)S(1)}) custom-call(s32[2]{0:T(128)} %length_source.1, bf16[2,128,4096]{2,1,0:T(8,128)(2,1)} %inputs.3, bf16[2,128,4096]{2,1,0:T(8,128)(2,1)} %gradient.3, bf16[16,4096]{1,0:T(8,128)(2,1)} %bitcast.10, bf16[16,4096]{1,0:T(8,128)(2,1)} %bitcast.12), custom_call_target="tpu_custom_call" | custom-call | flops 201326592 | bytes 12582912 | tf_op jit(solution)/shard_map/training_gradients/pallas_call | solution.py:274
  10.2 2.8 %collective-permute-start.5 = (bf16[64,1024]{1,0:T(8,128)(2,1)S(1)}, bf16[64,1024]{1,0:T(8,128)(2,1)S(1)}, u32[]{:S(2)}, u32[]{:S(2)}) collective-permute-start(bf16[64,1024]{1,0:T(8,128)(2,1)S(1)} %get-tuple-element.15.refs_0_), channel_id=1, source_target_pairs={{0,9},{1,8},{4,13},{5,12},{8,1},{9,0},{12,5},{13,4},{2,11},{3,10},... | collective-permute-start | bytes 393224 | tf_op jit(solution)/shard_map/ppermute | solution.py:244
  13.0 1.1 %collective-permute-start.6 = (bf16[64,1024]{1,0:T(8,128)(2,1)S(1)}, bf16[64,1024]{1,0:T(8,128)(2,1)S(1)}, u32[]{:S(2)}, u32[]{:S(2)}) collective-permute-start(bf16[64,1024]{1,0:T(8,128)(2,1)S(1)} %get-tuple-element.16.source), channel_id=1, source_target_pairs={{0,13},{1,12},{4,9},{5,8},{8,5},{9,4},{12,1},{13,0},{2,15},{3,14},... | collective-permute-start | bytes 393224 | tf_op jit(solution)/shard_map/ppermute | solution.py:244
  14.1 0.0 collective-permute-done.refs_1_
  14.1 1.5 %collective-permute-done.1.refs_2_ = bf16[64,2176]{1,0:T(8,128)(2,1)S(1)} collective-permute-done((bf16[64,2176]{1,0:T(8,128)(2,1)S(1)}, bf16[64,2176]{1,0:T(8,128)(2,1)S(1)}, u32[]{:S(2)}, u32[]{:S(2)}) %collective-permute-start.1) | collective-permute-done | bytes 278560 | tf_op jit(solution)/shard_map/ppermute | solution.py:272
  15.6 4.7 %collective-permute-done.2.refs_3_ = bf16[64,2176]{1,0:T(8,128)(2,1)S(1)} collective-permute-done((bf16[64,2176]{1,0:T(8,128)(2,1)S(1)}, bf16[64,2176]{1,0:T(8,128)(2,1)S(1)}, u32[]{:S(2)}, u32[]{:S(2)}) %collective-permute-start.2) | collective-permute-done | bytes 278560 | tf_op jit(solution)/shard_map/ppermute | solution.py:272
  20.2 0.1 token_stack.1._.refs_0_
  20.4 1.3 %collective-permute-start.3 = (bf16[560,1024]{1,0:T(8,128)(2,1)S(1)}, bf16[560,1024]{1,0:T(8,128)(2,1)S(1)}, u32[]{:S(2)}, u32[]{:S(2)}) collective-permute-start(bf16[560,1024]{1,0:T(8,128)(2,1)S(1)} %token_stack.1._.refs_0_), channel_id=1, source_target_pairs={{0,1},{1,0},{2,3},{3,2},{4,5},{5,4},{6,7},{7,6},{8,9},{9,8},{10,11... | collective-permute-start | bytes 3440648 | tf_op jit(solution)/shard_map/ppermute | solution.py:32
  21.7 0.0 collective-permute-start.4
  21.7 0.0 collective-permute-done.5.refs_0_
  21.7 2.5 %collective-permute-done.6.refs_1_ = bf16[64,1024]{1,0:T(8,128)(2,1)S(1)} collective-permute-done((bf16[64,1024]{1,0:T(8,128)(2,1)S(1)}, bf16[64,1024]{1,0:T(8,128)(2,1)S(1)}, u32[]{:S(2)}, u32[]{:S(2)}) %collective-permute-start.6) | collective-permute-done | bytes 131104 | tf_op jit(solution)/shard_map/ppermute | solution.py:244
  24.3 0.0 collective-permute-done.3.refs_1_
  24.3 0.9 %far_scores.1 = f32[2,4,8]{2,1,0:T(4,128)S(1)} custom-call(bf16[560,1024]{1,0:T(8,128)(2,1)S(1)} %token_stack.1._.refs_0_, bf16[560,1024]{1,0:T(8,128)(2,1)S(1)} %collective-permute-done.3.refs_1_, bf16[128,1024]{1,0:T(8,128)(2,1)S(1)} %far_gradients.1.refs_2_), custom_call_target="tpu_custom_call" | custom-call | bytes 573440 | tf_op jit(solution)/shard_map/far_scores/pallas_call | solution.py:300
  25.2 2.6 %collective-permute-start.7 = (f32[2,4,8]{2,1,0:T(4,128)S(1)}, f32[2,4,8]{2,1,0:T(4,128)S(1)}, u32[]{:S(2)}, u32[]{:S(2)}) collective-permute-start(f32[2,4,8]{2,1,0:T(4,128)S(1)} %far_scores.1), channel_id=1, source_target_pairs={{0,9},{1,8},{4,13},{5,12},{8,1},{9,0},{12,5},{13,4},{2,11},{3,10},... | collective-permute-start | bytes 776 | tf_op jit(solution)/shard_map/ppermute | solution.py:244
  27.8 0.4 %collective-permute-done.4.refs_1_ = bf16[64,1024]{1,0:T(8,128)(2,1)S(1)} collective-permute-done((bf16[64,1024]{1,0:T(8,128)(2,1)S(1)}, bf16[64,1024]{1,0:T(8,128)(2,1)S(1)}, u32[]{:S(2)}, u32[]{:S(2)}) %collective-permute-start.4) | collective-permute-done | bytes 131104 | tf_op jit(solution)/shard_map/ppermute | solution.py:32
  28.2 0.9 %near_scores.1 = f32[2,4,8]{2,1,0:T(4,128)S(1)} custom-call(bf16[560,1024]{1,0:T(8,128)(2,1)S(1)} %token_stack.1._.refs_0_, bf16[560,1024]{1,0:T(8,128)(2,1)S(1)} %collective-permute-done.3.refs_1_, bf16[128,1024]{1,0:T(8,128)(2,1)S(1)} %near_gradients.1.refs_2_), custom_call_target="tpu_custom_call" | custom-call | bytes 573440 | tf_op jit(solution)/shard_map/near_scores/pallas_call | solution.py:300
  29.2 0.0 collective-permute-done.7
  29.2 2.2 %collective-permute-start.9 = (f32[1,4,8]{2,1,0:T(4,128)S(1)}, f32[1,4,8]{2,1,0:T(4,128)S(1)}, u32[]{:S(2)}, u32[]{:S(2)}) collective-permute-start(f32[1,4,8]{2,1,0:T(4,128)S(1)} %get-tuple-element.17), channel_id=1, source_target_pairs={{0,3},{1,2},{2,1},{3,0},{4,7},{5,6},{6,5},{7,4},{8,11},{9,10},{10,... | collective-permute-start | bytes 392 | tf_op jit(solution)/shard_map/ppermute | solution.py:244
  31.4 0.0 collective-permute-start.8
  31.4 1.3 %collective-permute-done.9 = f32[1,4,8]{2,1,0:T(4,128)S(1)} collective-permute-done((f32[1,4,8]{2,1,0:T(4,128)S(1)}, f32[1,4,8]{2,1,0:T(4,128)S(1)}, u32[]{:S(2)}, u32[]{:S(2)}) %collective-permute-start.9) | collective-permute-done | bytes 160 | tf_op jit(solution)/shard_map/ppermute | solution.py:244
  32.7 0.0 collective-permute-done.8
  32.7 1.4 %collective-permute-start.11 = (f32[2,8]{1,0:T(2,128)S(1)}, f32[2,8]{1,0:T(2,128)S(1)}, u32[]{:S(2)}, u32[]{:S(2)}) collective-permute-start(f32[2,8]{1,0:T(2,128)S(1)} %get-tuple-element.19), channel_id=1, source_target_pairs={{0,5},{1,4},{4,1},{5,0},{8,13},{9,12},{12,9},{13,8},{2,7},{3,6},{6... | collective-permute-start | bytes 200 | tf_op jit(solution)/shard_map/ppermute | solution.py:244
  34.1 0.4 %collective-permute-start.10 = (f32[2,8]{1,0:T(2,128)S(1)}, f32[2,8]{1,0:T(2,128)S(1)}, u32[]{:S(2)}, u32[]{:S(2)}) collective-permute-start(f32[2,8]{1,0:T(2,128)S(1)} %get-tuple-element.20), channel_id=1, source_target_pairs={{0,1},{1,0},{2,3},{3,2},{4,5},{5,4},{6,7},{7,6},{8,9},{9,8},{10,11... | collective-permute-start | bytes 200 | tf_op jit(solution)/shard_map/ppermute | solution.py:32
  34.5 1.3 %collective-permute-done.11 = f32[2,8]{1,0:T(2,128)S(1)} collective-permute-done((f32[2,8]{1,0:T(2,128)S(1)}, f32[2,8]{1,0:T(2,128)S(1)}, u32[]{:S(2)}, u32[]{:S(2)}) %collective-permute-start.11) | collective-permute-done | bytes 96 | tf_op jit(solution)/shard_map/ppermute | solution.py:244
  35.7 0.0 collective-permute-done.10
  35.7 0.6 %add_bitcast_fusion = f32[8,2]{0,1:T(2,128)} fusion(f32[2,8]{1,0:T(2,128)S(1)} %collective-permute-done.10, f32[2,8]{1,0:T(2,128)S(1)} %collective-permute-done.11), kind=kLoop, calls=%fused_computation | loop fusion | flops 16 | bytes 192 | tf_op jit(solution)/shard_map/transpose | solution.py:367
  (7 shorter events, 0.1 us)
Async XLA Ops:
  1.7 12.3 %collective-permute-start = (bf16[64,2176]{1,0:T(8,128)(2,1)S(1)}, bf16[64,2176]{1,0:T(8,128)(2,1)S(1)}, u32[]{:S(2)}, u32[]{:S(2)}) collective-permute-start(bf16[64,2176]{1,0:T(8,128)(2,1)S(1)} %get-tuple-element.12), channel_id=1, source_target_pairs={{0,4},{1,5},{2,6},{3,7},{4,0},{5,1},{6,2},{7,3},{8,12},{9,13},{10,... | collective-permute-start | bytes 835592 | tf_op jit(solution)/shard_map/ppermute | solution.py:272
  4.8 10.8 %collective-permute-start.1 = (bf16[64,2176]{1,0:T(8,128)(2,1)S(1)}, bf16[64,2176]{1,0:T(8,128)(2,1)S(1)}, u32[]{:S(2)}, u32[]{:S(2)}) collective-permute-start(bf16[64,2176]{1,0:T(8,128)(2,1)S(1)} %get-tuple-element.13), channel_id=1, source_target_pairs={{0,2},{1,3},{2,0},{3,1},{4,6},{5,7},{6,4},{7,5},{8,10},{9,11},{10,... | collective-permute-start | bytes 835592 | tf_op jit(solution)/shard_map/ppermute | solution.py:272
  6.3 13.9 %collective-permute-start.2 = (bf16[64,2176]{1,0:T(8,128)(2,1)S(1)}, bf16[64,2176]{1,0:T(8,128)(2,1)S(1)}, u32[]{:S(2)}, u32[]{:S(2)}) collective-permute-start(bf16[64,2176]{1,0:T(8,128)(2,1)S(1)} %get-tuple-element.14), channel_id=1, source_target_pairs={{0,7},{1,6},{2,5},{3,4},{4,3},{5,2},{6,1},{7,0},{8,15},{9,14},{10,... | collective-permute-start | bytes 835592 | tf_op jit(solution)/shard_map/ppermute | solution.py:272
  10.2 11.5 %collective-permute-start.5 = (bf16[64,1024]{1,0:T(8,128)(2,1)S(1)}, bf16[64,1024]{1,0:T(8,128)(2,1)S(1)}, u32[]{:S(2)}, u32[]{:S(2)}) collective-permute-start(bf16[64,1024]{1,0:T(8,128)(2,1)S(1)} %get-tuple-element.15.refs_0_), channel_id=1, source_target_pairs={{0,9},{1,8},{4,13},{5,12},{8,1},{9,0},{12,5},{13,4},{2,11},{3,10},... | collective-permute-start | bytes 393224 | tf_op jit(solution)/shard_map/ppermute | solution.py:244
  13.0 11.3 %collective-permute-start.6 = (bf16[64,1024]{1,0:T(8,128)(2,1)S(1)}, bf16[64,1024]{1,0:T(8,128)(2,1)S(1)}, u32[]{:S(2)}, u32[]{:S(2)}) collective-permute-start(bf16[64,1024]{1,0:T(8,128)(2,1)S(1)} %get-tuple-element.16.source), channel_id=1, source_target_pairs={{0,13},{1,12},{4,9},{5,8},{8,5},{9,4},{12,1},{13,0},{2,15},{3,14},... | collective-permute-start | bytes 393224 | tf_op jit(solution)/shard_map/ppermute | solution.py:244
  20.4 3.9 %collective-permute-start.3 = (bf16[560,1024]{1,0:T(8,128)(2,1)S(1)}, bf16[560,1024]{1,0:T(8,128)(2,1)S(1)}, u32[]{:S(2)}, u32[]{:S(2)}) collective-permute-start(bf16[560,1024]{1,0:T(8,128)(2,1)S(1)} %token_stack.1._.refs_0_), channel_id=1, source_target_pairs={{0,1},{1,0},{2,3},{3,2},{4,5},{5,4},{6,7},{7,6},{8,9},{9,8},{10,11... | collective-permute-start | bytes 3440648 | tf_op jit(solution)/shard_map/ppermute | solution.py:32
  21.7 6.5 %collective-permute-start.4 = (bf16[64,1024]{1,0:T(8,128)(2,1)S(1)}, bf16[64,1024]{1,0:T(8,128)(2,1)S(1)}, u32[]{:S(2)}, u32[]{:S(2)}) collective-permute-start(bf16[64,1024]{1,0:T(8,128)(2,1)S(1)} %near_gradient.1), channel_id=1, source_target_pairs={{0,4},{4,0},{8,12},{12,8},{1,5},{5,1},{9,13},{13,9},{2,6},{6,2},{1... | collective-permute-start | bytes 393224 | tf_op jit(solution)/shard_map/ppermute | solution.py:32
  25.2 4.0 %collective-permute-start.7 = (f32[2,4,8]{2,1,0:T(4,128)S(1)}, f32[2,4,8]{2,1,0:T(4,128)S(1)}, u32[]{:S(2)}, u32[]{:S(2)}) collective-permute-start(f32[2,4,8]{2,1,0:T(4,128)S(1)} %far_scores.1), channel_id=1, source_target_pairs={{0,9},{1,8},{4,13},{5,12},{8,1},{9,0},{12,5},{13,4},{2,11},{3,10},... | collective-permute-start | bytes 776 | tf_op jit(solution)/shard_map/ppermute | solution.py:244
  29.2 3.5 %collective-permute-start.9 = (f32[1,4,8]{2,1,0:T(4,128)S(1)}, f32[1,4,8]{2,1,0:T(4,128)S(1)}, u32[]{:S(2)}, u32[]{:S(2)}) collective-permute-start(f32[1,4,8]{2,1,0:T(4,128)S(1)} %get-tuple-element.17), channel_id=1, source_target_pairs={{0,3},{1,2},{2,1},{3,0},{4,7},{5,6},{6,5},{7,4},{8,11},{9,10},{10,... | collective-permute-start | bytes 392 | tf_op jit(solution)/shard_map/ppermute | solution.py:244
  31.4 1.3 %collective-permute-start.8 = (f32[1,4,8]{2,1,0:T(4,128)S(1)}, f32[1,4,8]{2,1,0:T(4,128)S(1)}, u32[]{:S(2)}, u32[]{:S(2)}) collective-permute-start(f32[1,4,8]{2,1,0:T(4,128)S(1)} %get-tuple-element.18), channel_id=1, source_target_pairs={{0,1},{1,0},{2,3},{3,2},{4,5},{5,4},{6,7},{7,6},{8,9},{9,8},{10,11... | collective-permute-start | bytes 392 | tf_op jit(solution)/shard_map/ppermute | solution.py:32
  32.7 3.1 %collective-permute-start.11 = (f32[2,8]{1,0:T(2,128)S(1)}, f32[2,8]{1,0:T(2,128)S(1)}, u32[]{:S(2)}, u32[]{:S(2)}) collective-permute-start(f32[2,8]{1,0:T(2,128)S(1)} %get-tuple-element.19), channel_id=1, source_target_pairs={{0,5},{1,4},{4,1},{5,0},{8,13},{9,12},{12,9},{13,8},{2,7},{3,6},{6... | collective-permute-start | bytes 200 | tf_op jit(solution)/shard_map/ppermute | solution.py:244
  34.1 1.7 %collective-permute-start.10 = (f32[2,8]{1,0:T(2,128)S(1)}, f32[2,8]{1,0:T(2,128)S(1)}, u32[]{:S(2)}, u32[]{:S(2)}) collective-permute-start(f32[2,8]{1,0:T(2,128)S(1)} %get-tuple-element.20), channel_id=1, source_target_pairs={{0,1},{1,0},{2,3},{3,2},{4,5},{5,4},{6,7},{7,6},{8,9},{9,8},{10,11... | collective-permute-start | bytes 200 | tf_op jit(solution)/shard_map/ppermute | solution.py:32

commit v9 on v8

--- a/solution.py
+++ b/solution.py
@@ -59,6 +59,8 @@
     starts = [
         share_start(nlo, nsub, place // nsub, place % nsub, width) for place in range(len(shares))
     ]
+    for share in shares:
+        share[:, 2 * width :] = jnp.zeros((tokens, EXTRA), jnp.bfloat16)
     copies[0].wait()
     for start, share in zip(starts, shares):
         share[:, 0:width] = held_inputs[:, pl.ds(start, width)]
@@ -75,7 +77,6 @@
     id_rows = jnp.broadcast_to(held_ids[...].astype(jnp.float32), (KEPT - 2 * rank, tokens))
     extras = jnp.concatenate([low_down, low_up, id_rows], axis=0).astype(jnp.bfloat16)
     for share in shares:
-        share[:, 2 * width :] = jnp.zeros((tokens, EXTRA), jnp.bfloat16)
         share[0:KEPT, 2 * width : 2 * width + tokens] = extras
 
 

time: 36.6 us -> 36.6 us (level)
  no operation moved by 1% of the time
where the time goes in v9:
time: 36.6 us; the launch traced here: 36.3 us
  starting transfers between devices  16.4 us (45%)
  waiting for transfers between devices  11.7 us (32%)
  Pallas kernels  7.6 us (21%)
  other arithmetic  0.57 us (2%)
    ppermute x5, starting transfers between devices, crossing(): return lax.ppermute(value, (axis, 'pair'), pairs)  10.1 us
    ppermute x3, waiting for transfers between devices, per_device(): blocks.append(lax.ppermute(shares[place], ('dp', 'sub', 'pair'), pairs))  6.16 us
    ppermute x5, waiting for transfers between devices, crossing(): return lax.ppermute(value, (axis, 'pair'), pairs)  5.15 us
    ppermute x3, starting transfers between devices, per_device(): blocks.append(lax.ppermute(shares[place], ('dp', 'sub', 'pair'), pairs))  4.58 us
    pallas_call x1, Pallas kernels, per_device(): pl.pallas_call(functools.partial(training_kernel, nlo, nsub), out_shape=[...  3.87 us
    pallas_call x6, Pallas kernels, call(): pl.pallas_call(kernel, out_shape=jax.ShapeDtypeStruct(*shape), in_specs=[...  2.01 us
    ppermute x4, starting transfers between devices, swap(): lax.ppermute(value, axis, [(source, source ^ distance) for source in rang...  1.73 us
    pallas_call x1, Pallas kernels, per_device(): pl.pallas_call(functools.partial(query_kernel, nlo, nsub), out_shape=[jax...  1.73 us
  transfers between devices with their start and end apart: 12, of which 6 were waited for; matrix products, arithmetic and copies ran while one was open for 0% of the time, Pallas kernels for 16%

profile of v9, /device:TPU:0, one launch (start us, length us, event | category | flops | bytes accessed | tf_op | source)
XLA Modules:
  0.0 36.3 jit_solution(12707732141677898134)
XLA Ops:
  0.0 1.7 %query_shares.1 = (bf16[64,2176]{1,0:T(8,128)(2,1)S(1)}, bf16[64,2176]{1,0:T(8,128)(2,1)S(1)}, bf16[64,2176]{1,0:T(8,128)(2,1)S(1)}, bf16[64,2176]{1,0:T(8,128)(2,1)S(1)}) custom-call(bf16[64,4096]{1,0:T(8,128)(2,1)} %inputs.2, bf16[64,4096]{1,0:T(8,128)(2,1)} %gradient.2, s32[1,64]{1,0:T(1,128)} %bitcast.13, bf16[16,4096]{1,0:T(8,128)(2,1)} %bitcast.9, ...), custom_call_target="tpu_custom_call" | custom-call | tf_op jit(solution)/shard_map/query_shares/pallas_call | solution.py:247
  1.7 3.1 %collective-permute-start = (bf16[64,2176]{1,0:T(8,128)(2,1)S(1)}, bf16[64,2176]{1,0:T(8,128)(2,1)S(1)}, u32[]{:S(2)}, u32[]{:S(2)}) collective-permute-start(bf16[64,2176]{1,0:T(8,128)(2,1)S(1)} %get-tuple-element.12), channel_id=1, source_target_pairs={{0,4},{1,5},{2,6},{3,7},{4,0},{5,1},{6,2},{7,3},{8,12},{9,13},{10,... | collective-permute-start | bytes 835592 | tf_op jit(solution)/shard_map/ppermute | solution.py:273
  4.8 1.5 %collective-permute-start.1 = (bf16[64,2176]{1,0:T(8,128)(2,1)S(1)}, bf16[64,2176]{1,0:T(8,128)(2,1)S(1)}, u32[]{:S(2)}, u32[]{:S(2)}) collective-permute-start(bf16[64,2176]{1,0:T(8,128)(2,1)S(1)} %get-tuple-element.13), channel_id=1, source_target_pairs={{0,2},{1,3},{2,0},{3,1},{4,6},{5,7},{6,4},{7,5},{8,10},{9,11},{10,... | collective-permute-start | bytes 835592 | tf_op jit(solution)/shard_map/ppermute | solution.py:273
  6.3 0.0 collective-permute-start.2
  6.3 3.9 %training_gradients.1 = (bf16[64,1024]{1,0:T(8,128)(2,1)S(1)}, bf16[64,1024]{1,0:T(8,128)(2,1)S(1)}) custom-call(s32[2]{0:T(128)} %length_source.1, bf16[2,128,4096]{2,1,0:T(8,128)(2,1)} %inputs.3, bf16[2,128,4096]{2,1,0:T(8,128)(2,1)} %gradient.3, bf16[16,4096]{1,0:T(8,128)(2,1)} %bitcast.10, bf16[16,4096]{1,0:T(8,128)(2,1)} %bitcast.12), custom_call_target="tpu_custom_call" | custom-call | flops 201326592 | bytes 12582912 | tf_op jit(solution)/shard_map/training_gradients/pallas_call | solution.py:275
  10.2 2.8 %collective-permute-start.5 = (bf16[64,1024]{1,0:T(8,128)(2,1)S(1)}, bf16[64,1024]{1,0:T(8,128)(2,1)S(1)}, u32[]{:S(2)}, u32[]{:S(2)}) collective-permute-start(bf16[64,1024]{1,0:T(8,128)(2,1)S(1)} %get-tuple-element.15.refs_0_), channel_id=1, source_target_pairs={{0,9},{1,8},{4,13},{5,12},{8,1},{9,0},{12,5},{13,4},{2,11},{3,10},... | collective-permute-start | bytes 393224 | tf_op jit(solution)/shard_map/ppermute | solution.py:245
  13.0 1.1 %collective-permute-start.6 = (bf16[64,1024]{1,0:T(8,128)(2,1)S(1)}, bf16[64,1024]{1,0:T(8,128)(2,1)S(1)}, u32[]{:S(2)}, u32[]{:S(2)}) collective-permute-start(bf16[64,1024]{1,0:T(8,128)(2,1)S(1)} %get-tuple-element.16.source), channel_id=1, source_target_pairs={{0,13},{1,12},{4,9},{5,8},{8,5},{9,4},{12,1},{13,0},{2,15},{3,14},... | collective-permute-start | bytes 393224 | tf_op jit(solution)/shard_map/ppermute | solution.py:245
  14.1 0.0 collective-permute-done.refs_1_
  14.1 1.5 %collective-permute-done.1.refs_2_ = bf16[64,2176]{1,0:T(8,128)(2,1)S(1)} collective-permute-done((bf16[64,2176]{1,0:T(8,128)(2,1)S(1)}, bf16[64,2176]{1,0:T(8,128)(2,1)S(1)}, u32[]{:S(2)}, u32[]{:S(2)}) %collective-permute-start.1) | collective-permute-done | bytes 278560 | tf_op jit(solution)/shard_map/ppermute | solution.py:273
  15.6 4.7 %collective-permute-done.2.refs_3_ = bf16[64,2176]{1,0:T(8,128)(2,1)S(1)} collective-permute-done((bf16[64,2176]{1,0:T(8,128)(2,1)S(1)}, bf16[64,2176]{1,0:T(8,128)(2,1)S(1)}, u32[]{:S(2)}, u32[]{:S(2)}) %collective-permute-start.2) | collective-permute-done | bytes 278560 | tf_op jit(solution)/shard_map/ppermute | solution.py:273
  20.2 0.1 token_stack.1._.refs_0_
  20.4 1.3 %collective-permute-start.3 = (bf16[560,1024]{1,0:T(8,128)(2,1)S(1)}, bf16[560,1024]{1,0:T(8,128)(2,1)S(1)}, u32[]{:S(2)}, u32[]{:S(2)}) collective-permute-start(bf16[560,1024]{1,0:T(8,128)(2,1)S(1)} %token_stack.1._.refs_0_), channel_id=1, source_target_pairs={{0,1},{1,0},{2,3},{3,2},{4,5},{5,4},{6,7},{7,6},{8,9},{9,8},{10,11... | collective-permute-start | bytes 3440648 | tf_op jit(solution)/shard_map/ppermute | solution.py:32
  21.7 0.0 collective-permute-start.4
  21.7 0.0 collective-permute-done.5.refs_0_
  21.7 2.5 %collective-permute-done.6.refs_1_ = bf16[64,1024]{1,0:T(8,128)(2,1)S(1)} collective-permute-done((bf16[64,1024]{1,0:T(8,128)(2,1)S(1)}, bf16[64,1024]{1,0:T(8,128)(2,1)S(1)}, u32[]{:S(2)}, u32[]{:S(2)}) %collective-permute-start.6) | collective-permute-done | bytes 131104 | tf_op jit(solution)/shard_map/ppermute | solution.py:245
  24.3 0.0 collective-permute-done.3.refs_1_
  24.3 0.9 %far_scores.1 = f32[2,4,8]{2,1,0:T(4,128)S(1)} custom-call(bf16[560,1024]{1,0:T(8,128)(2,1)S(1)} %token_stack.1._.refs_0_, bf16[560,1024]{1,0:T(8,128)(2,1)S(1)} %collective-permute-done.3.refs_1_, bf16[128,1024]{1,0:T(8,128)(2,1)S(1)} %far_gradients.1.refs_2_), custom_call_target="tpu_custom_call" | custom-call | bytes 573440 | tf_op jit(solution)/shard_map/far_scores/pallas_call | solution.py:301
  25.2 2.6 %collective-permute-start.7 = (f32[2,4,8]{2,1,0:T(4,128)S(1)}, f32[2,4,8]{2,1,0:T(4,128)S(1)}, u32[]{:S(2)}, u32[]{:S(2)}) collective-permute-start(f32[2,4,8]{2,1,0:T(4,128)S(1)} %far_scores.1), channel_id=1, source_target_pairs={{0,9},{1,8},{4,13},{5,12},{8,1},{9,0},{12,5},{13,4},{2,11},{3,10},... | collective-permute-start | bytes 776 | tf_op jit(solution)/shard_map/ppermute | solution.py:245
  27.8 0.4 %collective-permute-done.4.refs_1_ = bf16[64,1024]{1,0:T(8,128)(2,1)S(1)} collective-permute-done((bf16[64,1024]{1,0:T(8,128)(2,1)S(1)}, bf16[64,1024]{1,0:T(8,128)(2,1)S(1)}, u32[]{:S(2)}, u32[]{:S(2)}) %collective-permute-start.4) | collective-permute-done | bytes 131104 | tf_op jit(solution)/shard_map/ppermute | solution.py:32
  28.2 0.9 %near_scores.1 = f32[2,4,8]{2,1,0:T(4,128)S(1)} custom-call(bf16[560,1024]{1,0:T(8,128)(2,1)S(1)} %token_stack.1._.refs_0_, bf16[560,1024]{1,0:T(8,128)(2,1)S(1)} %collective-permute-done.3.refs_1_, bf16[128,1024]{1,0:T(8,128)(2,1)S(1)} %near_gradients.1.refs_2_), custom_call_target="tpu_custom_call" | custom-call | bytes 573440 | tf_op jit(solution)/shard_map/near_scores/pallas_call | solution.py:301
  29.2 0.0 collective-permute-done.7
  29.2 2.2 %collective-permute-start.9 = (f32[1,4,8]{2,1,0:T(4,128)S(1)}, f32[1,4,8]{2,1,0:T(4,128)S(1)}, u32[]{:S(2)}, u32[]{:S(2)}) collective-permute-start(f32[1,4,8]{2,1,0:T(4,128)S(1)} %get-tuple-element.17), channel_id=1, source_target_pairs={{0,3},{1,2},{2,1},{3,0},{4,7},{5,6},{6,5},{7,4},{8,11},{9,10},{10,... | collective-permute-start | bytes 392 | tf_op jit(solution)/shard_map/ppermute | solution.py:245
  31.4 0.0 collective-permute-start.8
  31.4 1.3 %collective-permute-done.9 = f32[1,4,8]{2,1,0:T(4,128)S(1)} collective-permute-done((f32[1,4,8]{2,1,0:T(4,128)S(1)}, f32[1,4,8]{2,1,0:T(4,128)S(1)}, u32[]{:S(2)}, u32[]{:S(2)}) %collective-permute-start.9) | collective-permute-done | bytes 160 | tf_op jit(solution)/shard_map/ppermute | solution.py:245
  32.7 0.0 collective-permute-done.8
  32.7 1.4 %collective-permute-start.11 = (f32[2,8]{1,0:T(2,128)S(1)}, f32[2,8]{1,0:T(2,128)S(1)}, u32[]{:S(2)}, u32[]{:S(2)}) collective-permute-start(f32[2,8]{1,0:T(2,128)S(1)} %get-tuple-element.19), channel_id=1, source_target_pairs={{0,5},{1,4},{4,1},{5,0},{8,13},{9,12},{12,9},{13,8},{2,7},{3,6},{6... | collective-permute-start | bytes 200 | tf_op jit(solution)/shard_map/ppermute | solution.py:245
  34.1 0.4 %collective-permute-start.10 = (f32[2,8]{1,0:T(2,128)S(1)}, f32[2,8]{1,0:T(2,128)S(1)}, u32[]{:S(2)}, u32[]{:S(2)}) collective-permute-start(f32[2,8]{1,0:T(2,128)S(1)} %get-tuple-element.20), channel_id=1, source_target_pairs={{0,1},{1,0},{2,3},{3,2},{4,5},{5,4},{6,7},{7,6},{8,9},{9,8},{10,11... | collective-permute-start | bytes 200 | tf_op jit(solution)/shard_map/ppermute | solution.py:32
  34.5 1.3 %collective-permute-done.11 = f32[2,8]{1,0:T(2,128)S(1)} collective-permute-done((f32[2,8]{1,0:T(2,128)S(1)}, f32[2,8]{1,0:T(2,128)S(1)}, u32[]{:S(2)}, u32[]{:S(2)}) %collective-permute-start.11) | collective-permute-done | bytes 96 | tf_op jit(solution)/shard_map/ppermute | solution.py:245
  35.7 0.0 collective-permute-done.10
  35.7 0.6 %add_bitcast_fusion = f32[8,2]{0,1:T(2,128)} fusion(f32[2,8]{1,0:T(2,128)S(1)} %collective-permute-done.10, f32[2,8]{1,0:T(2,128)S(1)} %collective-permute-done.11), kind=kLoop, calls=%fused_computation | loop fusion | flops 16 | bytes 192 | tf_op jit(solution)/shard_map/transpose | solution.py:368
  (7 shorter events, 0.1 us)
Async XLA Ops:
  1.7 12.3 %collective-permute-start = (bf16[64,2176]{1,0:T(8,128)(2,1)S(1)}, bf16[64,2176]{1,0:T(8,128)(2,1)S(1)}, u32[]{:S(2)}, u32[]{:S(2)}) collective-permute-start(bf16[64,2176]{1,0:T(8,128)(2,1)S(1)} %get-tuple-element.12), channel_id=1, source_target_pairs={{0,4},{1,5},{2,6},{3,7},{4,0},{5,1},{6,2},{7,3},{8,12},{9,13},{10,... | collective-permute-start | bytes 835592 | tf_op jit(solution)/shard_map/ppermute | solution.py:273
  4.8 10.8 %collective-permute-start.1 = (bf16[64,2176]{1,0:T(8,128)(2,1)S(1)}, bf16[64,2176]{1,0:T(8,128)(2,1)S(1)}, u32[]{:S(2)}, u32[]{:S(2)}) collective-permute-start(bf16[64,2176]{1,0:T(8,128)(2,1)S(1)} %get-tuple-element.13), channel_id=1, source_target_pairs={{0,2},{1,3},{2,0},{3,1},{4,6},{5,7},{6,4},{7,5},{8,10},{9,11},{10,... | collective-permute-start | bytes 835592 | tf_op jit(solution)/shard_map/ppermute | solution.py:273
  6.3 13.9 %collective-permute-start.2 = (bf16[64,2176]{1,0:T(8,128)(2,1)S(1)}, bf16[64,2176]{1,0:T(8,128)(2,1)S(1)}, u32[]{:S(2)}, u32[]{:S(2)}) collective-permute-start(bf16[64,2176]{1,0:T(8,128)(2,1)S(1)} %get-tuple-element.14), channel_id=1, source_target_pairs={{0,7},{1,6},{2,5},{3,4},{4,3},{5,2},{6,1},{7,0},{8,15},{9,14},{10,... | collective-permute-start | bytes 835592 | tf_op jit(solution)/shard_map/ppermute | solution.py:273
  10.2 11.5 %collective-permute-start.5 = (bf16[64,1024]{1,0:T(8,128)(2,1)S(1)}, bf16[64,1024]{1,0:T(8,128)(2,1)S(1)}, u32[]{:S(2)}, u32[]{:S(2)}) collective-permute-start(bf16[64,1024]{1,0:T(8,128)(2,1)S(1)} %get-tuple-element.15.refs_0_), channel_id=1, source_target_pairs={{0,9},{1,8},{4,13},{5,12},{8,1},{9,0},{12,5},{13,4},{2,11},{3,10},... | collective-permute-start | bytes 393224 | tf_op jit(solution)/shard_map/ppermute | solution.py:245
  13.0 11.3 %collective-permute-start.6 = (bf16[64,1024]{1,0:T(8,128)(2,1)S(1)}, bf16[64,1024]{1,0:T(8,128)(2,1)S(1)}, u32[]{:S(2)}, u32[]{:S(2)}) collective-permute-start(bf16[64,1024]{1,0:T(8,128)(2,1)S(1)} %get-tuple-element.16.source), channel_id=1, source_target_pairs={{0,13},{1,12},{4,9},{5,8},{8,5},{9,4},{12,1},{13,0},{2,15},{3,14},... | collective-permute-start | bytes 393224 | tf_op jit(solution)/shard_map/ppermute | solution.py:245
  20.4 3.9 %collective-permute-start.3 = (bf16[560,1024]{1,0:T(8,128)(2,1)S(1)}, bf16[560,1024]{1,0:T(8,128)(2,1)S(1)}, u32[]{:S(2)}, u32[]{:S(2)}) collective-permute-start(bf16[560,1024]{1,0:T(8,128)(2,1)S(1)} %token_stack.1._.refs_0_), channel_id=1, source_target_pairs={{0,1},{1,0},{2,3},{3,2},{4,5},{5,4},{6,7},{7,6},{8,9},{9,8},{10,11... | collective-permute-start | bytes 3440648 | tf_op jit(solution)/shard_map/ppermute | solution.py:32
  21.7 6.5 %collective-permute-start.4 = (bf16[64,1024]{1,0:T(8,128)(2,1)S(1)}, bf16[64,1024]{1,0:T(8,128)(2,1)S(1)}, u32[]{:S(2)}, u32[]{:S(2)}) collective-permute-start(bf16[64,1024]{1,0:T(8,128)(2,1)S(1)} %near_gradient.1), channel_id=1, source_target_pairs={{0,4},{4,0},{8,12},{12,8},{1,5},{5,1},{9,13},{13,9},{2,6},{6,2},{1... | collective-permute-start | bytes 393224 | tf_op jit(solution)/shard_map/ppermute | solution.py:32
  25.2 4.0 %collective-permute-start.7 = (f32[2,4,8]{2,1,0:T(4,128)S(1)}, f32[2,4,8]{2,1,0:T(4,128)S(1)}, u32[]{:S(2)}, u32[]{:S(2)}) collective-permute-start(f32[2,4,8]{2,1,0:T(4,128)S(1)} %far_scores.1), channel_id=1, source_target_pairs={{0,9},{1,8},{4,13},{5,12},{8,1},{9,0},{12,5},{13,4},{2,11},{3,10},... | collective-permute-start | bytes 776 | tf_op jit(solution)/shard_map/ppermute | solution.py:245
  29.2 3.5 %collective-permute-start.9 = (f32[1,4,8]{2,1,0:T(4,128)S(1)}, f32[1,4,8]{2,1,0:T(4,128)S(1)}, u32[]{:S(2)}, u32[]{:S(2)}) collective-permute-start(f32[1,4,8]{2,1,0:T(4,128)S(1)} %get-tuple-element.17), channel_id=1, source_target_pairs={{0,3},{1,2},{2,1},{3,0},{4,7},{5,6},{6,5},{7,4},{8,11},{9,10},{10,... | collective-permute-start | bytes 392 | tf_op jit(solution)/shard_map/ppermute | solution.py:245
  31.4 1.3 %collective-permute-start.8 = (f32[1,4,8]{2,1,0:T(4,128)S(1)}, f32[1,4,8]{2,1,0:T(4,128)S(1)}, u32[]{:S(2)}, u32[]{:S(2)}) collective-permute-start(f32[1,4,8]{2,1,0:T(4,128)S(1)} %get-tuple-element.18), channel_id=1, source_target_pairs={{0,1},{1,0},{2,3},{3,2},{4,5},{5,4},{6,7},{7,6},{8,9},{9,8},{10,11... | collective-permute-start | bytes 392 | tf_op jit(solution)/shard_map/ppermute | solution.py:32
  32.7 3.1 %collective-permute-start.11 = (f32[2,8]{1,0:T(2,128)S(1)}, f32[2,8]{1,0:T(2,128)S(1)}, u32[]{:S(2)}, u32[]{:S(2)}) collective-permute-start(f32[2,8]{1,0:T(2,128)S(1)} %get-tuple-element.19), channel_id=1, source_target_pairs={{0,5},{1,4},{4,1},{5,0},{8,13},{9,12},{12,9},{13,8},{2,7},{3,6},{6... | collective-permute-start | bytes 200 | tf_op jit(solution)/shard_map/ppermute | solution.py:245
  34.1 1.7 %collective-permute-start.10 = (f32[2,8]{1,0:T(2,128)S(1)}, f32[2,8]{1,0:T(2,128)S(1)}, u32[]{:S(2)}, u32[]{:S(2)}) collective-permute-start(f32[2,8]{1,0:T(2,128)S(1)} %get-tuple-element.20), channel_id=1, source_target_pairs={{0,1},{1,0},{2,3},{3,2},{4,5},{5,4},{6,7},{7,6},{8,9},{9,8},{10,11... | collective-permute-start | bytes 200 | tf_op jit(solution)/shard_map/ppermute | solution.py:32
